TPU v7x, 32 devices: a whole 2x2x4 slice. The times are simulated.
32 devices in a mesh: parts: 2 (over x), col: 16 (over z, y, core).
Axes of the slice: x: 2, y: 2, z: 4, core: 2. Of those that a mesh axis runs over, the one named last changes fastest.
Arguments:
- view_factors: bfloat16 [8192, 4096], P(('parts', 'col')), parts along dimension 0, may hold values from -0.09375 to 0.09375
- direct_coeff: bfloat16 [8192, 2304], P(('parts', 'col')), parts along dimension 0, may hold values from -6 to 6
- material: int32 [8192], P(('parts', 'col')), parts along dimension 0, may hold values from 0 to 15
- albedo: float32 [32], P('parts'), parts along dimension 0, may hold values from 0.1 to 0.9
- sky_matrix: bfloat16 [2304, 128], P('col'), may hold values from -0.125 to 0.125
- sky_order: int32 [2304], replicated, may hold values from 0 to 2303, each once
Outputs:
- irradiance: bfloat16 [8192, 128], P(('parts', 'col')), parts along dimension 0
There are 2 independent parts, one for each index of `parts`. A program takes and returns all parts, laid end to end along the dimension named above; an argument that names none is the same for every part. Nothing has to cross between parts.
Inputs may be any that keep to these rules, and one draw needn't show every extreme that they name: sky_order names each of 0 to 2303 once.
All inputs are finite; a program needn't handle non-finite values.
Results may differ from a plain program's by a relative error of at most 0.0055.
Values may be sent and summed in bfloat16 or wider, within the bound.
No kernel may reach another device: no remote copies, remote signals or barrier semaphores. Data moves between devices by JAX's collectives and lax.ppermute only.
A program may use at most 128 MiB of HBM per device.

v0:
```python
import jax
import jax.numpy as jnp
from jax import lax
from jax.sharding import PartitionSpec as P


def split_parts(values):
    upper = values.astype(jnp.bfloat16)
    lower = (values - upper.astype(jnp.float32)).astype(jnp.bfloat16)
    return (upper, lower)


def shards(view_factors, direct_coeff, material, albedo, sky_matrix, sky_order):
    inverse = jnp.argsort(sky_order)
    direct_sorted = jnp.take(direct_coeff, inverse, axis=1)
    matches = material[:, None] == jnp.arange(albedo.shape[0], dtype=jnp.int32)[None, :]
    reflectance = jnp.sum(jnp.where(matches, albedo[None, :], 0.0), axis=1)
    reflected = (reflectance[:, None] * direct_sorted.astype(jnp.float32)).astype(jnp.bfloat16)
    piece = lax.all_gather(sky_matrix, "col", axis=0, tiled=True)
    direct_hours = jnp.dot(direct_sorted, piece, preferred_element_type=jnp.float32)
    own_reflected = jnp.dot(reflected, piece, preferred_element_type=jnp.float32)
    upper, lower = split_parts(lax.all_gather(own_reflected, "col", axis=0, tiled=True))
    running = jnp.dot(view_factors, upper, preferred_element_type=jnp.float32)
    bounce_hours = running + jnp.dot(view_factors, lower, preferred_element_type=jnp.float32)
    irradiance = direct_hours + bounce_hours
    return irradiance.astype(jnp.bfloat16)


def solution(mesh):
    return jax.shard_map(
        shards,
        mesh=mesh,
        in_specs=(
            P(("parts", "col"), None),
            P(("parts", "col"), None),
            P(("parts", "col")),
            P("parts"),
            P("col", None),
            P(),
        ),
        out_specs=P(("parts", "col"), None),
        check_vma=False,
    )
```

profile of v0, /device:TPU:0, one launch (start us, length us, event | category | flops | bytes accessed | tf_op | source)
XLA Modules:
  0.0 101.4 jit_solution(16061025368571012396)
XLA Ops:
  6.5 0.0 copy-start
  6.5 0.0 all-gather.2.cloned.1.call-start
  6.5 6.6 %sort.17 = (s32[2304]{0:T(1024)}, s32[2304]{0:T(1024)S(1)}) sort(s32[2304]{0:T(1024)} %param.11, s32[2304]{0:T(1024)S(1)} %iota.8), dimensions={0}, to_apply=%region_0.0 | sort | flops 27648 | bytes 36864 | tf_op jit(solution)/shard_map/jit(argsort)/sort | solution.py:14
  13.2 26.5 %all_gather.6 = bf16[2304,128]{1,0:T(8,128)(2,1)} all-gather(bf16[144,128]{1,0:T(8,128)(2,1)} %param.10), channel_id=1, replica_groups=mesh['parts'=2,'col'=16] {'col'}, dimensions={0}, use_global_device_ids=true | all-gather | bytes 626688 | tf_op jit(solution)/shard_map/all_gather | solution.py:19
  39.7 0.0 copy-start.3
  39.7 0.0 copy-start.4
  39.7 1.6 %copy.10 = bf16[256,2304]{0,1:T(8,128)(2,1)S(1)} copy(bf16[256,2304]{1,0:T(8,128)(2,1)} %param.7) | data formatting | bytes 2359296 | tf_op args[1]
  41.3 0.0 copy-done.3
  41.3 0.0 copy-done.4
  41.3 0.1 select_reduce_fusion
  41.4 7.4 %gather_fusion = bf16[2304,256]{1,0:T(8,128)(2,1)} fusion(bf16[256,2304]{0,1:T(8,128)(2,1)S(1)} %copy.10, s32[3072]{0:T(1024)S(1)} %pad_clamp_fusion), kind=kCustom, calls=%fused_computation | custom fusion | bytes 2368512 | tf_op jit(solution)/shard_map/jit(_take)/gather | solution.py:15
  48.8 0.0 copy-start.2
  48.8 3.1 %fusion = f32[256,128]{1,0:T(8,128)} fusion(bf16[2304,128]{1,0:T(8,128)(2,1)} %all_gather.6, f32[256]{0:T(256)S(1)} %select_reduce_fusion, bf16[2304,256]{1,0:T(8,128)(2,1)} %gather_fusion, pred[2304]{0:T(1024)(128)(4,1)S(1)} %compare_and_fusion), kind=kOutput, calls=%fused_computation.3 | convolution fusion | flops 153354240 | bytes 1903872 | tf_op jit(solution)/shard_map/dot_general | solution.py:21
  51.9 0.0 all-gather.2.cloned.1.call-update
  51.9 0.0 copy-done.2
  51.9 1.9 %fusion.8 = f32[256,128]{1,0:T(8,128)S(1)} fusion(bf16[2304,128]{1,0:T(8,128)(2,1)} %all_gather.6, bf16[2304,256]{1,0:T(8,128)(2,1)S(1)} %copy-done.2, pred[2304]{0:T(1024)(128)(4,1)S(1)} %compare_and_fusion), kind=kOutput, calls=%fused_computation.13 | convolution fusion | flops 151584768 | bytes 1902848 | tf_op jit(solution)/shard_map/dot_general | solution.py:20
  53.9 36.9 %all-gather.2.cloned.1.call-done = f32[4096,128]{1,0:T(8,128)} async-done(((f32[256,128]{1,0:T(8,128)}), f32[4096,128]{1,0:T(8,128)}) %all-gather.2.cloned.1.call-update) | async-done | bytes 2097168 | tf_op jit(solution)/shard_map/all_gather | solution.py:22
  90.8 0.0 copy-done
  90.8 0.0 copy-start.1
  90.8 2.4 %fusion.6 = f32[128,256]{0,1:T(8,128)S(1)} fusion(bf16[256,4096]{1,0:T(8,128)(2,1)S(1)} %copy-done, f32[4096,128]{1,0:T(8,128)} %all-gather.2.cloned.1.call-done), kind=kOutput, calls=%fused_computation.11 | convolution fusion | flops 268959744 | bytes 4325376 | tf_op jit(solution)/shard_map/dot_general | solution.py:23
  93.2 0.0 copy-done.1
  93.2 1.3 %fusion.4 = bf16[256,128]{1,0:T(8,128)(2,1)} fusion(f32[256,128]{1,0:T(8,128)S(1)} %fusion.8, f32[128,256]{0,1:T(8,128)S(1)} %fusion.6, bf16[256,4096]{1,0:T(8,128)(2,1)S(1)} %copy-done, f32[4096,128]{1,0:T(8,128)S(1)} %copy-done.1), kind=kOutput, calls=%fused_computation.9 | convolution fusion | flops 270630912 | bytes 4521984 | tf_op jit(solution)/shard_map/dot_general | solution.py:24
  (4 shorter events, 0.0 us)
Async XLA Ops:
  6.5 84.2 %copy-start = (bf16[256,4096]{1,0:T(8,128)(2,1)S(1)}, bf16[256,4096]{1,0:T(8,128)(2,1)}, u32[]{:S(2)}) copy-start(bf16[256,4096]{1,0:T(8,128)(2,1)} %param.6) | copy-start | bytes 6291460
  6.5 84.2 %all-gather.2.cloned.1.call-start = ((), (), s32[]{:S(2)}) async-start(), calls=%async_computation | async-start | bytes 2228224 | tf_op jit(solution)/shard_map/all_gather | solution.py:22
  39.7 1.6 %copy-start.3 = (s32[256]{0:T(256)S(1)}, s32[256]{0:T(256)}, u32[]{:S(2)}) copy-start(s32[256]{0:T(256)} %param.8) | copy-start | bytes 3076
  39.7 1.6 %copy-start.4 = (f32[16]{0:T(128)S(1)}, f32[16]{0:T(128)}, u32[]{:S(2)}) copy-start(f32[16]{0:T(128)} %param.9) | copy-start | bytes 196
  48.8 3.1 %copy-start.2 = (bf16[2304,256]{1,0:T(8,128)(2,1)S(1)}, bf16[2304,256]{1,0:T(8,128)(2,1)}, u32[]{:S(2)}) copy-start(bf16[2304,256]{1,0:T(8,128)(2,1)} %gather_fusion) | copy-start | bytes 3538948
  90.8 2.4 %copy-start.1 = (f32[4096,128]{1,0:T(8,128)S(1)}, f32[4096,128]{1,0:T(8,128)}, u32[]{:S(2)}) copy-start(f32[4096,128]{1,0:T(8,128)} %all-gather.2.cloned.1.call-done) | copy-start | bytes 6291460
Sparse Core Ops, SparseCore 0:
  52.0 38.6 all-gather.1
where the time goes:
time: 102 us; the launch traced here: 101 us
  waiting for transfers between devices  36.9 us (36%)
  blocking collectives  26.5 us (26%)
  between operations  13.5 us (13%)
  local copies, waits for them, and re-layouts  9.05 us (9%)
  matrix products  8.78 us (9%)
  other arithmetic  6.73 us (7%)
    all_gather x1, waiting for transfers between devices, shards(): lax.all_gather(own_reflected, 'col', axis=0, tiled=True)  36.9 us
    all_gather x1, blocking collectives, shards(): piece = lax.all_gather(sky_matrix, 'col', axis=0, tiled=True)  26.5 us
    gather x1, local copies, waits for them, and re-layouts, shards(): direct_sorted = jnp.take(direct_coeff, inverse, axis=1)  7.43 us
    sort x1, other arithmetic, shards(): inverse = jnp.argsort(sky_order)  6.62 us
    dot_general x1, matrix products, shards(): jnp.dot(reflected, piece, preferred_element_type=jnp.float32)  3.05 us
    dot_general x1, matrix products, shards(): running = jnp.dot(view_factors, upper, preferred_element_type=jnp.float32)  2.44 us
  transfers between devices with their start and end apart: 1, of which 1 were waited for; matrix products, arithmetic and copies ran while one was open for 2% of the time, Pallas kernels for 0%

commit v1 on v0

v1 whole, which is shorter than its diff:
```python
import jax
import jax.numpy as jnp
from jax import lax
from jax.sharding import PartitionSpec as P


def exchange_plan(size):
    bits = [1 << b for b in range(1, size.bit_length() - 1)][::-1]
    return bits, bits[-1:] + bits[:-1]


def arrival(order):
    masks = [0]
    for bit in order:
        masks = masks + [m ^ bit for m in masks]
    return masks


def owners(size):
    even, odd = (arrival(order) for order in exchange_plan(size))
    return even + [m ^ 1 for m in odd], odd + [m ^ 1 for m in even]


def gather(block, size):
    for even, odd in zip(*exchange_plan(size)):
        pairs = [(i, i ^ (odd if i & 1 else even)) for i in range(size)]
        block = jnp.concatenate([block, lax.ppermute(block, "col", pairs)], axis=0)
    other = lax.ppermute(block, "col", [(i, i ^ 1) for i in range(size)])
    return jnp.concatenate([block, other], axis=0)


def shards(size, view_factors, direct_coeff, material, albedo, sky_matrix, sky_order):
    me = lax.axis_index("col")
    even, odd = owners(size)
    masks = jnp.where(me & 1 == 0, jnp.array(even, jnp.int32), jnp.array(odd, jnp.int32))
    owner = me ^ masks
    rows = sky_matrix.shape[0]
    patches = direct_coeff.shape[0]
    held = (owner[:, None] * rows + jnp.arange(rows, dtype=jnp.int32)[None, :]).reshape(-1)
    matches = material[:, None] == jnp.arange(albedo.shape[0], dtype=jnp.int32)[None, :]
    reflectance = jnp.sum(jnp.where(matches, albedo[None, :], 0.0), axis=1)
    place = (sky_order[:, None] == held[None, :]).astype(jnp.bfloat16)
    direct = jnp.dot(direct_coeff, place, preferred_element_type=jnp.float32).astype(jnp.bfloat16)
    reflected = (reflectance[:, None] * direct.astype(jnp.float32)).astype(jnp.bfloat16)
    sky = gather(sky_matrix, size)
    hours = jnp.dot(reflected, sky, preferred_element_type=jnp.float32).astype(jnp.bfloat16)
    direct_hours = jnp.dot(direct, sky, preferred_element_type=jnp.float32)
    all_hours = gather(hours, size)
    total = direct_hours
    for slot in range(size):
        columns = lax.dynamic_slice_in_dim(view_factors, owner[slot] * patches, patches, axis=1)
        total += jnp.dot(columns, all_hours[slot * patches : (slot + 1) * patches], preferred_element_type=jnp.float32)
    return total.astype(jnp.bfloat16)


def solution(mesh):
    size = mesh.shape["col"]

    def body(*args):
        return shards(size, *args)

    return jax.shard_map(
        body,
        mesh=mesh,
        in_specs=(
            P(("parts", "col"), None),
            P(("parts", "col"), None),
            P(("parts", "col")),
            P("parts"),
            P("col", None),
            P(),
        ),
        out_specs=P(("parts", "col"), None),
        check_vma=False,
    )
```

time: 102 us -> 55.6 us (0.55)
  blocking collectives: 26.5 us -> 0 us
  waiting for transfers between devices: 36.9 us -> 16.1 us
  starting transfers between devices: 0.01 us -> 10.9 us
  other arithmetic: 6.73 us -> 2.5 us
  local copies, waits for them, and re-layouts: 9.05 us -> 4.99 us
  between operations: 13.5 us -> 10.5 us
  matrix products: 8.78 us -> 10.3 us
    all_gather x1 -> x0, waiting for transfers between devices: 36.9 us -> none  [shards(): lax.all_gather(own_reflected, 'col', axis=0, tiled=True)]
    all_gather x1 -> x0, blocking collectives: 26.5 us -> none  [shards(): piece = lax.all_gather(sky_matrix, 'col', axis=0, tiled=True)]
    ppermute x0 -> x8, waiting for transfers between devices: none -> 16.1 us  [the longest x6 14.9 us: gather(): block = jnp.concatenate([block, lax.ppermute(block, 'col', pairs)], axis=0)]
    ppermute x0 -> x8, starting transfers between devices: none -> 10.9 us  [the longest x6 10.7 us: gather(): block = jnp.concatenate([block, lax.ppermute(block, 'col', pairs)], axis=0)]
    gather x1 -> x0, local copies, waits for them, and re-layouts: 7.43 us -> none  [shards(): direct_sorted = jnp.take(direct_coeff, inverse, axis=1)]
    sort x1 -> x0, other arithmetic: 6.62 us -> none  [shards(): inverse = jnp.argsort(sky_order)]
    unnamed x11 -> x14, local copies, waits for them, and re-layouts: 1.61 us -> 3.47 us
    concatenate x0 -> x6, other arithmetic: none -> 1.67 us  [gather(): block = jnp.concatenate([block, lax.ppermute(block, 'col', pairs)], axis=0)]
  transfers between devices with their start and end apart: 1 -> 8, of which waited for: 1 -> 5; matrix products, arithmetic and copies ran while one was open for 2% -> 20% of each run, Pallas kernels for 0% -> 0%
where the time goes in v1:
time: 55.6 us; the launch traced here: 55.3 us
  waiting for transfers between devices  16.1 us (29%)
  starting transfers between devices  10.9 us (20%)
  between operations  10.5 us (19%)
  matrix products  10.3 us (19%)
  local copies, waits for them, and re-layouts  4.99 us (9%)
  other arithmetic  2.5 us (4%)
    ppermute x6, waiting for transfers between devices, gather(): block = jnp.concatenate([block, lax.ppermute(block, 'col', pairs)], axis=0)  14.9 us
    ppermute x6, starting transfers between devices, gather(): block = jnp.concatenate([block, lax.ppermute(block, 'col', pairs)], axis=0)  10.7 us
    dot_general x1, matrix products, shards(): jnp.dot(direct_coeff, place, preferred_element_type=jnp.float32)  4.84 us
    unnamed x14, local copies, waits for them, and re-layouts  3.47 us
    dot_general x16, matrix products, shards(): jnp.dot(columns, all_hours[slot * patches:(slot + 1) * patches], preferre...  2.69 us
    concatenate x6, other arithmetic, gather(): block = jnp.concatenate([block, lax.ppermute(block, 'col', pairs)], axis=0)  1.67 us
    dot_general x1, matrix products, shards(): jnp.dot(reflected, sky, preferred_element_type=jnp.float32)  1.59 us
    ppermute x2, waiting for transfers between devices, gather(): other = lax.ppermute(block, 'col', [(i, i ^ 1) for i in range(size)])  1.19 us
  transfers between devices with their start and end apart: 8, of which 5 were waited for; matrix products, arithmetic and copies ran while one was open for 20% of the time, Pallas kernels for 0%

profile of v1, /device:TPU:0, one launch (start us, length us, event | category | flops | bytes accessed | tf_op | source)
XLA Modules:
  0.0 55.3 jit_solution(12882002028943594080)
XLA Ops:
  0.0 4.0 %collective-permute-start = (bf16[144,128]{1,0:T(8,128)(2,1)}, bf16[144,128]{1,0:T(8,128)(2,1)S(1)}, u32[]{:S(2)}, u32[]{:S(2)}) collective-permute-start(bf16[144,128]{1,0:T(8,128)(2,1)} %param.12), channel_id=1, source_target_pairs={{0,8},{1,3},{2,10},{3,1},{4,12},{5,7},{6,14},{7,5},{8,0},{9,11},{1... | collective-permute-start | bytes 110600 | tf_op jit(solution)/shard_map/ppermute | solution.py:27
  4.0 0.7 %broadcast_multiply_fusion = (s32[16]{0:T(128)S(1)}, s32[16]{0:T(128)S(1)}) fusion(s32[16]{0:T(128)} %constant.36.clone, s32[16]{0:T(128)} %constant.37.clone, pred[]{:T(512)S(6)} %eq.30, s32[]{:T(128)S(6)} %axis_index.12), kind=kLoop, calls=%fused_computation.104 | loop fusion | flops 48 | bytes 261 | tf_op jit(solution)/shard_map/mul | solution.py:39
  4.9 4.8 %fusion.3 = bf16[2304,256]{1,0:T(8,128)(2,1)S(1)} fusion(bf16[256,2304]{1,0:T(8,128)(2,1)} %param.9, s32[2304]{0:T(1024)S(1)} %add.119, s32[2304]{0:T(1024)} %param.13), kind=kOutput, calls=%fused_computation.4 | convolution fusion | flops 2729115648 | bytes 2377728 | tf_op jit(solution)/shard_map/dot_general | solution.py:43
  9.8 1.6 %collective-permute-start.1 = (bf16[288,128]{1,0:T(8,128)(2,1)S(1)}, bf16[288,128]{1,0:T(8,128)(2,1)S(1)}, u32[]{:S(2)}, u32[]{:S(2)}) collective-permute-start(bf16[288,128]{1,0:T(8,128)(2,1)S(1)} %pad_maximum_fusion.5), channel_id=1, source_target_pairs={{0,4},{1,9},{2,6},{3,11},{4,0},{5,13},{6,2},{7,15},{8,12},{9,1},{1... | collective-permute-start | bytes 221192 | tf_op jit(solution)/shard_map/ppermute | solution.py:27
  11.4 0.6 %constant_dynamic-update-slice_fusion.4 = bf16[2304,128]{1,0:T(8,128)(2,1)} fusion(bf16[144,128]{1,0:T(8,128)(2,1)S(1)} %copy-done.2), kind=kLoop, calls=%fused_computation.85 | loop fusion | bytes 73728
  12.0 2.2 %collective-permute-done.1 = bf16[288,128]{1,0:T(8,128)(2,1)S(1)} collective-permute-done((bf16[288,128]{1,0:T(8,128)(2,1)S(1)}, bf16[288,128]{1,0:T(8,128)(2,1)S(1)}, u32[]{:S(2)}, u32[]{:S(2)}) %collective-permute-start.1) | collective-permute-done | bytes 73760 | tf_op jit(solution)/shard_map/ppermute | solution.py:27
  14.2 0.7 %pad_maximum_fusion.3 = bf16[576,128]{1,0:T(8,128)(2,1)} fusion(bf16[288,128]{1,0:T(8,128)(2,1)S(1)} %collective-permute-done.1, bf16[144,128]{1,0:T(8,128)(2,1)S(1)} %collective-permute-done, bf16[144,128]{1,0:T(8,128)(2,1)S(1)} %copy-done.2), kind=kLoop, calls=%fused_computation.29 | loop fusion | flops 442368 | bytes 294912 | tf_op jit(solution)/shard_map/concatenate | solution.py:27
  14.9 1.5 %collective-permute-start.2 = (bf16[576,128]{1,0:T(8,128)(2,1)}, bf16[576,128]{1,0:T(8,128)(2,1)}, u32[]{:S(2)}, u32[]{:S(2)}) collective-permute-start(bf16[576,128]{1,0:T(8,128)(2,1)} %pad_maximum_fusion.3), channel_id=1, source_target_pairs={{0,2},{1,5},{2,0},{3,7},{4,6},{5,1},{6,4},{7,3},{8,10},{9,13},{10,... | collective-permute-start | bytes 442376 | tf_op jit(solution)/shard_map/ppermute | solution.py:27
  16.4 0.7 %fusion.87 = (s32[1]{0:T(128)}, s32[1]{0:T(128)}, s32[1]{0:T(128)}, s32[1]{0:T(128)}, s32[1]{0:T(128)}, /*index=5*/s32[1]{0:T(128)}, s32[1]{0:T(128)}, s32[1]{0:...) fusion(s32[16]{0:T(128)S(1)} %get-tuple-element.6), kind=kLoop, calls=%fused_computation.105 | loop fusion | bytes 128 | tf_op jit(solution)/shard_map/slice | solution.py:51
  27.4 0.9 %pad_maximum_fusion.1 = bf16[1152,128]{1,0:T(8,128)(2,1)S(1)} fusion(bf16[576,128]{1,0:T(8,128)(2,1)} %collective-permute-done.2, bf16[288,128]{1,0:T(8,128)(2,1)S(1)} %collective-permute-done.1, bf16[144,128]{1,0:T(8,128)(2,1)S(1)} %collective-permute-done, bf16[144,128]{1,0:T(8,128)(2,1)S(1)} %copy-done.2), kind=kLoop, calls=%fused_computation.27 | loop fusion | flops 1179648 | bytes 589824 | tf_op jit(solution)/shard_map/concatenate | solution.py:27
  28.5 0.6 %constant_dynamic-update-slice_fusion.3 = bf16[2304,128]{1,0:T(8,128)(2,1)} fusion(bf16[2304,128]{1,0:T(8,128)(2,1)} %constant_dynamic-update-slice_fusion.4, bf16[144,128]{1,0:T(8,128)(2,1)S(1)} %collective-permute-done), kind=kLoop, calls=%fused_computation.84 | loop fusion | bytes 73728
  29.1 0.6 %constant_dynamic-update-slice_fusion.2 = bf16[2304,128]{1,0:T(8,128)(2,1)} fusion(bf16[2304,128]{1,0:T(8,128)(2,1)} %constant_dynamic-update-slice_fusion.3, bf16[288,128]{1,0:T(8,128)(2,1)S(1)} %collective-permute-done.1), kind=kLoop, calls=%fused_computation.83 | loop fusion | bytes 147456
  29.7 1.6 %constant_dynamic-update-slice_fusion.1 = bf16[2304,128]{1,0:T(8,128)(2,1)} fusion(bf16[2304,128]{1,0:T(8,128)(2,1)} %constant_dynamic-update-slice_fusion.2, bf16[576,128]{1,0:T(8,128)(2,1)} %collective-permute-done.2), kind=kLoop, calls=%fused_computation.82 | loop fusion | bytes 294912
  31.3 0.7 %constant_dynamic-update-slice_fusion = bf16[2304,128]{1,0:T(8,128)(2,1)} fusion(bf16[2304,128]{1,0:T(8,128)(2,1)} %constant_dynamic-update-slice_fusion.1, bf16[1152,128]{1,0:T(8,128)(2,1)S(1)} %collective-permute-done.3), kind=kLoop, calls=%fused_computation.81 | loop fusion | bytes 589824 | tf_op jit(solution)/shard_map/concatenate | solution.py:29
  32.0 1.6 %fusion.21 = bf16[256,128]{1,0:T(8,128)(2,1)S(1)} fusion(bf16[2304,128]{1,0:T(8,128)(2,1)} %constant_dynamic-update-slice_fusion, bf16[2304,256]{1,0:T(8,128)(2,1)S(1)} %fusion.3, f32[256]{0:T(256)S(1)} %select_reduce_fusion), kind=kOutput, calls=%fused_computation.24 | convolution fusion | flops 152797184 | bytes 1836032 | tf_op jit(solution)/shard_map/dot_general | solution.py:46
  33.6 1.3 %collective-permute-start.4 = (bf16[256,128]{1,0:T(8,128)(2,1)S(1)}, bf16[256,128]{1,0:T(8,128)(2,1)S(1)}, u32[]{:S(2)}, u32[]{:S(2)}) collective-permute-start(bf16[256,128]{1,0:T(8,128)(2,1)S(1)} %fusion.21), channel_id=1, source_target_pairs={{0,8},{1,3},{2,10},{3,1},{4,12},{5,7},{6,14},{7,5},{8,0},{9,11},{1... | collective-permute-start | bytes 196616 | tf_op jit(solution)/shard_map/ppermute | solution.py:27
  35.1 3.7 %collective-permute-done.4 = bf16[256,128]{1,0:T(8,128)(2,1)S(1)} collective-permute-done((bf16[256,128]{1,0:T(8,128)(2,1)S(1)}, bf16[256,128]{1,0:T(8,128)(2,1)S(1)}, u32[]{:S(2)}, u32[]{:S(2)}) %collective-permute-start.4) | collective-permute-done | bytes 65568 | tf_op jit(solution)/shard_map/ppermute | solution.py:27
  38.8 1.6 %collective-permute-start.5 = (bf16[512,128]{1,0:T(8,128)(2,1)S(1)}, bf16[512,128]{1,0:T(8,128)(2,1)S(1)}, u32[]{:S(2)}, u32[]{:S(2)}) collective-permute-start(bf16[512,128]{1,0:T(8,128)(2,1)S(1)} %pad_maximum_fusion.4), channel_id=1, source_target_pairs={{0,4},{1,9},{2,6},{3,11},{4,0},{5,13},{6,2},{7,15},{8,12},{9,1},{1... | collective-permute-start | bytes 393224 | tf_op jit(solution)/shard_map/ppermute | solution.py:27
  40.7 3.5 %collective-permute-done.5 = bf16[512,128]{1,0:T(8,128)(2,1)S(1)} collective-permute-done((bf16[512,128]{1,0:T(8,128)(2,1)S(1)}, bf16[512,128]{1,0:T(8,128)(2,1)S(1)}, u32[]{:S(2)}, u32[]{:S(2)}) %collective-permute-start.5) | collective-permute-done | bytes 131104 | tf_op jit(solution)/shard_map/ppermute | solution.py:27
  44.2 0.6 %collective-permute-start.6 = (bf16[1024,128]{1,0:T(8,128)(2,1)S(1)}, bf16[1024,128]{1,0:T(8,128)(2,1)S(1)}, u32[]{:S(2)}, u32[]{:S(2)}) collective-permute-start(bf16[1024,128]{1,0:T(8,128)(2,1)S(1)} %pad_maximum_fusion.2), channel_id=1, source_target_pairs={{0,2},{1,5},{2,0},{3,7},{4,6},{5,1},{6,4},{7,3},{8,10},{9,13},{10,... | collective-permute-start | bytes 786440 | tf_op jit(solution)/shard_map/ppermute | solution.py:27
  45.1 5.5 %collective-permute-done.6 = bf16[1024,128]{1,0:T(8,128)(2,1)S(1)} collective-permute-done((bf16[1024,128]{1,0:T(8,128)(2,1)S(1)}, bf16[1024,128]{1,0:T(8,128)(2,1)S(1)}, u32[]{:S(2)}, u32[]{:S(2)}) %collective-permute-start.6) | collective-permute-done | bytes 262176 | tf_op jit(solution)/shard_map/ppermute | solution.py:27
  51.3 0.2 fusion.45
  51.5 1.2 %collective-permute-done.7 = bf16[2048,128]{1,0:T(8,128)(2,1)S(1)} collective-permute-done((bf16[2048,128]{1,0:T(8,128)(2,1)S(1)}, bf16[2048,128]{1,0:T(8,128)(2,1)S(1)}, u32[]{:S(2)}, u32[]{:S(2)}) %collective-permute-start.7) | collective-permute-done | bytes 524320 | tf_op jit(solution)/shard_map/ppermute | solution.py:28
  54.1 1.2 %fusion.22 = bf16[256,128]{1,0:T(8,128)(2,1)} fusion(f32[256,128]{1,0:T(8,128)S(1)} %fusion.23, f32[256,128]{1,0:T(8,128)S(1)} %fusion.25, f32[256,128]{1,0:T(8,128)S(1)} %fusion.27, f32[256,128]{1,0:T(8,128)S(1)} %fusion.29, f32[256,128]{1,0:T(8,128)S(1)} %fusion.31, f32[256,128]{1,0:T(8,128)S(1)} %fusion.33, f32[256,128]{1,0:T(8,128)S(1)} %fusion.35, ...), kind=kOutput, calls=%fused_computation.25 | convolution fusion | flops 151552000 | bytes 3932160 | tf_op jit(solution)/shard_map/dot_general | solution.py:47
  (37 shorter events, 3.0 us)
Async XLA Ops:
  0.0 34.9 %copy-start = (bf16[256,4096]{1,0:T(8,128)(2,1)S(1)}, bf16[256,4096]{1,0:T(8,128)(2,1)}, u32[]{:S(2)}) copy-start(bf16[256,4096]{1,0:T(8,128)(2,1)} %param.8) | copy-start | bytes 6291460
  0.0 9.7 %collective-permute-start = (bf16[144,128]{1,0:T(8,128)(2,1)}, bf16[144,128]{1,0:T(8,128)(2,1)S(1)}, u32[]{:S(2)}, u32[]{:S(2)}) collective-permute-start(bf16[144,128]{1,0:T(8,128)(2,1)} %param.12), channel_id=1, source_target_pairs={{0,8},{1,3},{2,10},{3,1},{4,12},{5,7},{6,14},{7,5},{8,0},{9,11},{1... | collective-permute-start | bytes 110600 | tf_op jit(solution)/shard_map/ppermute | solution.py:27
  4.9 4.9 %copy-start.2 = (bf16[144,128]{1,0:T(8,128)(2,1)S(1)}, bf16[144,128]{1,0:T(8,128)(2,1)}, u32[]{:S(2)}) copy-start(bf16[144,128]{1,0:T(8,128)(2,1)} %param.12) | copy-start | bytes 110596
  4.9 22.4 %copy-start.3 = (s32[256]{0:T(256)S(1)}, s32[256]{0:T(256)}, u32[]{:S(2)}) copy-start(s32[256]{0:T(256)} %param.10) | copy-start | bytes 3076
  4.9 22.4 %copy-start.4 = (f32[16]{0:T(128)S(1)}, f32[16]{0:T(128)}, u32[]{:S(2)}) copy-start(f32[16]{0:T(128)} %param.11) | copy-start | bytes 196
  9.8 4.4 %collective-permute-start.1 = (bf16[288,128]{1,0:T(8,128)(2,1)S(1)}, bf16[288,128]{1,0:T(8,128)(2,1)S(1)}, u32[]{:S(2)}, u32[]{:S(2)}) collective-permute-start(bf16[288,128]{1,0:T(8,128)(2,1)S(1)} %pad_maximum_fusion.5), channel_id=1, source_target_pairs={{0,4},{1,9},{2,6},{3,11},{4,0},{5,13},{6,2},{7,15},{8,12},{9,1},{1... | collective-permute-start | bytes 221192 | tf_op jit(solution)/shard_map/ppermute | solution.py:27
  14.9 12.6 %collective-permute-start.2 = (bf16[576,128]{1,0:T(8,128)(2,1)}, bf16[576,128]{1,0:T(8,128)(2,1)}, u32[]{:S(2)}, u32[]{:S(2)}) collective-permute-start(bf16[576,128]{1,0:T(8,128)(2,1)} %pad_maximum_fusion.3), channel_id=1, source_target_pairs={{0,2},{1,5},{2,0},{3,7},{4,6},{5,1},{6,4},{7,3},{8,10},{9,13},{10,... | collective-permute-start | bytes 442376 | tf_op jit(solution)/shard_map/ppermute | solution.py:27
  28.4 2.9 %collective-permute-start.3 = (bf16[1152,128]{1,0:T(8,128)(2,1)S(1)}, bf16[1152,128]{1,0:T(8,128)(2,1)S(1)}, u32[]{:S(2)}, u32[]{:S(2)}) collective-permute-start(bf16[1152,128]{1,0:T(8,128)(2,1)S(1)} %pad_maximum_fusion.1), channel_id=1, source_target_pairs={{0,1},{1,0},{2,3},{3,2},{4,5},{5,4},{6,7},{7,6},{8,9},{9,8},{10,11... | collective-permute-start | bytes 884744 | tf_op jit(solution)/shard_map/ppermute | solution.py:28
  33.6 5.2 %collective-permute-start.4 = (bf16[256,128]{1,0:T(8,128)(2,1)S(1)}, bf16[256,128]{1,0:T(8,128)(2,1)S(1)}, u32[]{:S(2)}, u32[]{:S(2)}) collective-permute-start(bf16[256,128]{1,0:T(8,128)(2,1)S(1)} %fusion.21), channel_id=1, source_target_pairs={{0,8},{1,3},{2,10},{3,1},{4,12},{5,7},{6,14},{7,5},{8,0},{9,11},{1... | collective-permute-start | bytes 196616 | tf_op jit(solution)/shard_map/ppermute | solution.py:27
  38.8 5.3 %collective-permute-start.5 = (bf16[512,128]{1,0:T(8,128)(2,1)S(1)}, bf16[512,128]{1,0:T(8,128)(2,1)S(1)}, u32[]{:S(2)}, u32[]{:S(2)}) collective-permute-start(bf16[512,128]{1,0:T(8,128)(2,1)S(1)} %pad_maximum_fusion.4), channel_id=1, source_target_pairs={{0,4},{1,9},{2,6},{3,11},{4,0},{5,13},{6,2},{7,15},{8,12},{9,1},{1... | collective-permute-start | bytes 393224 | tf_op jit(solution)/shard_map/ppermute | solution.py:27
  44.2 6.4 %collective-permute-start.6 = (bf16[1024,128]{1,0:T(8,128)(2,1)S(1)}, bf16[1024,128]{1,0:T(8,128)(2,1)S(1)}, u32[]{:S(2)}, u32[]{:S(2)}) collective-permute-start(bf16[1024,128]{1,0:T(8,128)(2,1)S(1)} %pad_maximum_fusion.2), channel_id=1, source_target_pairs={{0,2},{1,5},{2,0},{3,7},{4,6},{5,1},{6,4},{7,3},{8,10},{9,13},{10,... | collective-permute-start | bytes 786440 | tf_op jit(solution)/shard_map/ppermute | solution.py:27
  50.7 3.4 %copy-start.1 = (bf16[2304,128]{1,0:T(8,128)(2,1)S(1)}, bf16[2304,128]{1,0:T(8,128)(2,1)}, u32[]{:S(2)}) copy-start(bf16[2304,128]{1,0:T(8,128)(2,1)} %constant_dynamic-update-slice_fusion) | copy-start | bytes 1769476
  50.7 2.0 %collective-permute-start.7 = (bf16[2048,128]{1,0:T(8,128)(2,1)S(1)}, bf16[2048,128]{1,0:T(8,128)(2,1)S(1)}, u32[]{:S(2)}, u32[]{:S(2)}) collective-permute-start(bf16[2048,128]{1,0:T(8,128)(2,1)S(1)} %pad_maximum_fusion), channel_id=1, source_target_pairs={{0,1},{1,0},{2,3},{3,2},{4,5},{5,4},{6,7},{7,6},{8,9},{9,8},{10,11... | collective-permute-start | bytes 1572872 | tf_op jit(solution)/shard_map/ppermute | solution.py:28

commit v2 on v0

v2 whole, which is shorter than its diff:
```python
import functools

import jax
import jax.numpy as jnp
from jax import lax
from jax.experimental import pallas as pl
from jax.experimental.pallas import tpu as pltpu
from jax.sharding import PartitionSpec as P

WHOLE = pl.BlockSpec(memory_space=pltpu.VMEM)
ANYWHERE = pl.BlockSpec(memory_space=pltpu.HBM)
SCALARS = pl.BlockSpec(memory_space=pltpu.SMEM)


def exchange_plan(size):
    bits = [1 << b for b in range(1, size.bit_length() - 1)][::-1]
    return bits[:-2] + bits[-2:][::-1], bits


def arrival(order):
    masks = [0]
    for bit in order:
        masks = masks + [m ^ bit for m in masks]
    return masks


def owner_of(me, even, odd):
    return me ^ jnp.where(me & 1 == 0, even, odd)


def call(kernel, name, outs, specs, flops, *args, scratch=(), vmem=24):
    return pl.pallas_call(
        kernel,
        scratch_shapes=scratch,
        out_shape=outs,
        in_specs=specs,
        out_specs=jax.tree.map(lambda _: WHOLE, outs),
        compiler_params=pltpu.CompilerParams(vmem_limit_bytes=vmem * 2**20),
        cost_estimate=pl.CostEstimate(flops=flops, bytes_accessed=0, transcendentals=0),
        name=name,
    )(*args)


def prepare_kernel(size, albedo_in, material_in, order_in, sky_in, direct_in, me_ref, *refs):
    sky_out, direct_out, reflectance_out, place_out, albedo_ref, material_ref, order_ref, sems = refs
    moves = ((albedo_in, albedo_ref), (material_in, material_ref), (order_in, order_ref))
    moves += ((sky_in, sky_out), (direct_in, direct_out))
    copies = [pltpu.make_async_copy(source, target, sems.at[i]) for i, (source, target) in enumerate(moves)]
    for copy in copies:
        copy.start()
    for copy in copies[:3]:
        copy.wait()
    material = material_ref[...].reshape(1, -1)
    reflectance = jnp.zeros(material.shape, jnp.float32)
    for m in range(albedo_ref.shape[0]):
        reflectance = jnp.where(material == m, albedo_ref[m], reflectance)
    reflectance_out[...] = jnp.broadcast_to(reflectance, (128, reflectance.shape[1])).T
    me = me_ref[0]
    rows = sky_in.shape[0]
    order = order_ref[...].reshape(1, -1)
    owner = (order * -(-(1 << 20) // rows)) >> 20
    row = order - owner * rows
    apart = owner ^ me
    slot = jnp.where(apart & 1 != 0, size // 2, 0)
    for k, (even, odd) in enumerate(zip(*exchange_plan(size))):
        slot += jnp.where(apart & jnp.where(owner & 1 == 0, even, odd) != 0, 1 << k, 0)
    place_out[...] = slot * rows + row
    for copy in copies[3:]:
        copy.wait()


def permute_kernel(start, place_ref, reflectance_ref, direct_ref, sorted_ref, reflected_ref):
    count = sorted_ref.shape[1]
    place = place_ref[...]
    reflectance = reflectance_ref[:, :1]
    step = 384
    for j in range(0, count, step):
        width = min(step, count - j)
        position = lax.broadcasted_iota(jnp.int32, (width, place.shape[1]), 0) + (start + j)
        pick = jnp.where(position == place, 1.0, 0.0).astype(jnp.bfloat16)
        part = lax.dot_general(direct_ref[...], pick, (((1,), (1,)), ((), ())), preferred_element_type=jnp.float32)
        sorted_ref[:, j : j + width] = part.astype(jnp.bfloat16)
        reflected_ref[:, j : j + width] = (reflectance * part).astype(jnp.bfloat16)


def dot_kernel(a_ref, b_ref, out_ref):
    out_ref[...] = jnp.dot(a_ref[...], b_ref[...], preferred_element_type=jnp.float32)


def direct_kernel(own_ref, other_ref, sky_own_ref, sky_other_ref, factors_ref, out_ref, factors_out, sem):
    copy = pltpu.make_async_copy(factors_ref, factors_out, sem)
    copy.start()
    out = jnp.dot(own_ref[...], sky_own_ref[...], preferred_element_type=jnp.float32)
    out_ref[...] = out + jnp.dot(other_ref[...], sky_other_ref[...], preferred_element_type=jnp.float32)
    copy.wait()


def add_dot_kernel(base_ref, a_ref, b_ref, out_ref):
    part = jnp.dot(a_ref[...], b_ref[...], preferred_element_type=jnp.float32)
    out_ref[...] = (base_ref[...] + part).astype(out_ref.dtype)


def bounce_kernel(masks, me_ref, base_ref, factors_ref, hours_ref, out_ref):
    me = me_ref[0]
    total = base_ref[...]
    patches = out_ref.shape[0]
    for slot, (even, odd) in enumerate(masks):
        first = pl.multiple_of(owner_of(me, even, odd) * patches, patches)
        total += jnp.dot(
            factors_ref[:, pl.ds(first, patches)],
            hours_ref[slot * patches : (slot + 1) * patches, :],
            preferred_element_type=jnp.float32,
        )
    out_ref[...] = total.astype(out_ref.dtype)


def shards(size, view_factors, direct_coeff, material, albedo, sky_matrix, sky_order):
    me = lax.axis_index("col")
    even, odd = exchange_plan(size)
    rows, hours = sky_matrix.shape
    patches, skies = direct_coeff.shape
    half = size // 2
    pairs = [[(i, i ^ (b if i & 1 else a)) for i in range(size)] for a, b in zip(even, odd)]
    cores = [(i, i ^ 1) for i in range(size)]

    def exchange(block, step):
        return jnp.concatenate([block, lax.ppermute(block, "col", pairs[step])], axis=0)

    span = half * rows
    index = me.reshape(1)
    sky_own, direct_coeff, reflectance, place = call(
        functools.partial(prepare_kernel, size),
        "prepare",
        (
            pltpu.VMEM(sky_matrix.shape, sky_matrix.dtype),
            pltpu.VMEM(direct_coeff.shape, direct_coeff.dtype),
            pltpu.VMEM((patches, 128), jnp.float32),
            pltpu.VMEM((1, skies), jnp.int32),
        ),
        [ANYWHERE] * 5 + [SCALARS],
        10**9,
        *(pltpu.with_memory_space_constraint(x, pltpu.HBM) for x in (albedo, material, sky_order, sky_matrix, direct_coeff)),
        index,
        scratch=[
            pltpu.SMEM(albedo.shape, albedo.dtype),
            pltpu.VMEM(material.shape, material.dtype),
            pltpu.VMEM(sky_order.shape, sky_order.dtype),
            pltpu.SemaphoreType.DMA((5,)),
        ],
    )

    def permute(h, after):
        where, _ = lax.optimization_barrier((place, after))
        return call(
            functools.partial(permute_kernel, h * span),
            f"permute{h}",
            (jax.ShapeDtypeStruct((patches, span), jnp.bfloat16),) * 2,
            [WHOLE] * 3,
            2 * patches * skies * span,
            where,
            reflectance,
            direct_coeff,
        )

    sky = sky_matrix
    split = []
    for step in range(len(even)):
        came = lax.ppermute(sky, "col", pairs[step])
        if 0 < step < 3:
            split.append(permute(step - 1, sky))
            came, split[-1] = lax.optimization_barrier((came, split[-1]))
        sky = jnp.concatenate([sky if step else sky_own, came], axis=0)
    sky_other = lax.ppermute(sky, "col", cores)

    flat = jax.ShapeDtypeStruct((patches, hours), jnp.float32)
    flops = 2 * patches * span * hours
    part = call(dot_kernel, "hours_own", flat, [WHOLE] * 2, flops, split[0][1], sky)
    own = call(
        add_dot_kernel, "hours_all", jax.ShapeDtypeStruct(flat.shape, jnp.bfloat16), [WHOLE] * 3, flops, part, split[1][1], sky_other
    )
    held = own
    for step in range(len(even)):
        came = lax.ppermute(held, "col", pairs[step])
        if step == 0:
            _, sky_own, sky_other_own = lax.optimization_barrier((held, sky, sky_other))
            direct, view_factors = call(
                direct_kernel,
                "direct",
                (flat, jax.ShapeDtypeStruct(view_factors.shape, view_factors.dtype)),
                [WHOLE] * 4 + [ANYWHERE],
                2 * flops,
                split[0][0],
                split[1][0],
                sky_own,
                sky_other_own,
                view_factors,
                scratch=[pltpu.SemaphoreType.DMA],
                vmem=24,
            )
            came, direct = lax.optimization_barrier((came, direct))
        held = jnp.concatenate([held, came], axis=0)
    held_other = lax.ppermute(held, "col", cores)
    a, b = arrival(even), arrival(odd)
    flops = 2 * patches * half * patches * hours
    specs = [SCALARS, WHOLE, WHOLE, WHOLE]
    total = call(
        functools.partial(bounce_kernel, list(zip(a, b))), "bounce_own", flat, specs, flops, index, direct, view_factors, held
    )
    return call(
        functools.partial(bounce_kernel, [(y ^ 1, x ^ 1) for x, y in zip(a, b)]),
        "bounce_all",
        jax.ShapeDtypeStruct(flat.shape, jnp.bfloat16),
        specs,
        flops,
        index,
        total,
        view_factors,
        held_other,
    )


def solution(mesh):
    return jax.shard_map(
        functools.partial(shards, mesh.shape["col"]),
        mesh=mesh,
        in_specs=(
            P(("parts", "col"), None),
            P(("parts", "col"), None),
            P(("parts", "col")),
            P("parts"),
            P("col", None),
            P(),
        ),
        out_specs=P(("parts", "col"), None),
        check_vma=False,
    )
```

time: 102 us -> 39.6 us (0.39)
  blocking collectives: 26.5 us -> 0 us
  waiting for transfers between devices: 36.9 us -> 18.6 us
  between operations: 13.5 us -> 0.1 us
  starting transfers between devices: 0.01 us -> 12.5 us
  local copies, waits for them, and re-layouts: 9.05 us -> 0.08 us
  matrix products: 8.78 us -> 0 us
  Pallas kernels: 0 us -> 8.09 us
  other arithmetic: 6.73 us -> 0.06 us
    all_gather x1 -> x0, waiting for transfers between devices: 36.9 us -> none  [shards(): lax.all_gather(own_reflected, 'col', axis=0, tiled=True)]
    all_gather x1 -> x0, blocking collectives: 26.5 us -> none  [shards(): piece = lax.all_gather(sky_matrix, 'col', axis=0, tiled=True)]
    ppermute x0 -> x8, waiting for transfers between devices: none -> 18.6 us  [the longest x3 12.5 us: shards(): came = lax.ppermute(held, 'col', pairs[step])]
    ppermute x0 -> x8, starting transfers between devices: none -> 12.5 us  [the longest x3 7.41 us: shards(): came = lax.ppermute(sky, 'col', pairs[step])]
    dot_general x4 -> x0, matrix products: 8.78 us -> none  [the longest x1 3.05 us: shards(): jnp.dot(reflected, piece, preferred_element_type=jnp.float32)]
    pallas_call x0 -> x8, Pallas kernels: none -> 8.09 us  [call(): pl.pallas_call(kernel, scratch_shapes=scratch, out_shape=outs, in_specs=s...]
    gather x1 -> x0, local copies, waits for them, and re-layouts: 7.43 us -> none  [shards(): direct_sorted = jnp.take(direct_coeff, inverse, axis=1)]
    sort x1 -> x0, other arithmetic: 6.62 us -> none  [shards(): inverse = jnp.argsort(sky_order)]
  transfers between devices with their start and end apart: 1 -> 8, of which waited for: 1 -> 8; matrix products, arithmetic and copies ran while one was open for 2% -> 0% of each run, Pallas kernels for 0% -> 17%
where the time goes in v2:
time: 39.6 us; the launch traced here: 39.4 us
  waiting for transfers between devices  18.6 us (47%)
  starting transfers between devices  12.5 us (32%)
  Pallas kernels  8.09 us (20%)
    ppermute x3, waiting for transfers between devices, shards(): came = lax.ppermute(held, 'col', pairs[step])  12.5 us
    pallas_call x8, Pallas kernels, call(): pl.pallas_call(kernel, scratch_shapes=scratch, out_shape=outs, in_specs=s...  8.09 us
    ppermute x3, starting transfers between devices, shards(): came = lax.ppermute(sky, 'col', pairs[step])  7.41 us
    ppermute x3, starting transfers between devices, shards(): came = lax.ppermute(held, 'col', pairs[step])  4.99 us
    ppermute x3, waiting for transfers between devices, shards(): came = lax.ppermute(sky, 'col', pairs[step])  3.37 us
    ppermute x1, waiting for transfers between devices, shards(): held_other = lax.ppermute(held, 'col', cores)  1.46 us
    ppermute x1, waiting for transfers between devices, shards(): sky_other = lax.ppermute(sky, 'col', cores)  1.26 us
  transfers between devices with their start and end apart: 8, of which 8 were waited for; matrix products, arithmetic and copies ran while one was open for 0% of the time, Pallas kernels for 17%

profile of v2, /device:TPU:0, one launch (start us, length us, event | category | flops | bytes accessed | tf_op | source)
XLA Modules:
  0.0 39.4 jit_solution(11038339566444207405)
XLA Ops:
  0.0 4.0 %collective-permute-start = (bf16[144,128]{1,0:T(8,128)(2,1)}, bf16[144,128]{1,0:T(8,128)(2,1)S(1)}, u32[]{:S(2)}, u32[]{:S(2)}) collective-permute-start(bf16[144,128]{1,0:T(8,128)(2,1)} %sky_in.1), channel_id=1, source_target_pairs={{0,8},{1,9},{2,10},{3,11},{4,12},{5,13},{6,14},{7,15},{8,0},{9,1},... | collective-permute-start | bytes 110600 | tf_op jit(solution)/shard_map/ppermute | solution.py:168
  4.0 1.4 %prepare.1 = (bf16[144,128]{1,0:T(8,128)(2,1)S(1)}, bf16[256,2304]{1,0:T(8,128)(2,1)S(1)}, f32[256,128]{1,0:T(8,128)S(1)}, s32[1,2304]{1,0:T(1,128)S(1)}) custom-call(f32[16]{0:T(128)} %albedo_in.1, s32[256]{0:T(256)} %material_in.1, s32[2304]{0:T(1024)} %order_in.1, bf16[144,128]{1,0:T(8,128)(2,1)} %sky_in.1, bf16[256,2304]{1,0:T(8,128)(2,1)} %direct_in.1, ...), custom_call_target="tpu_custom_call" | custom-call | flops 1000000000 | tf_op jit(solution)/shard_map/prepare/pallas_call | solution.py:32
  5.4 1.1 %collective-permute-done = bf16[144,128]{1,0:T(8,128)(2,1)S(1)} collective-permute-done((bf16[144,128]{1,0:T(8,128)(2,1)}, bf16[144,128]{1,0:T(8,128)(2,1)S(1)}, u32[]{:S(2)}, u32[]{:S(2)}) %collective-permute-start) | collective-permute-done | bytes 36896 | tf_op jit(solution)/shard_map/ppermute | solution.py:168
  6.6 1.8 %collective-permute-start.1 = (bf16[288,128]{1,0:T(8,128)(2,1)S(1)}, bf16[288,128]{1,0:T(8,128)(2,1)S(1)}, u32[]{:S(2)}, u32[]{:S(2)}) collective-permute-start(bf16[288,128]{1,0:T(8,128)(2,1)S(1)} %get-tuple-element.53), channel_id=1, source_target_pairs={{0,2},{1,5},{2,0},{3,7},{4,6},{5,1},{6,4},{7,3},{8,10},{9,13},{10,... | collective-permute-start | bytes 221192 | tf_op jit(solution)/shard_map/ppermute | solution.py:168
  8.4 2.0 %permute0.1 = (bf16[256,1152]{1,0:T(8,128)(2,1)S(1)}, bf16[256,1152]{1,0:T(8,128)(2,1)S(1)}) custom-call(s32[1,2304]{1,0:T(1,128)S(1)} %get-tuple-element.36.place_ref, f32[256,128]{1,0:T(8,128)S(1)} %get-tuple-element.30.reflectance_ref, bf16[256,2304]{1,0:T(8,128)(2,1)S(1)} %get-tuple-element.31.direct_ref), custom_call_target="tpu_custom_call" | custom-call | flops 1358954496 | tf_op jit(solution)/shard_map/permute0/pallas_call | solution.py:32
  10.4 0.6 %collective-permute-done.1 = bf16[288,128]{1,0:T(8,128)(2,1)S(1)} collective-permute-done((bf16[288,128]{1,0:T(8,128)(2,1)S(1)}, bf16[288,128]{1,0:T(8,128)(2,1)S(1)}, u32[]{:S(2)}, u32[]{:S(2)}) %collective-permute-start.1) | collective-permute-done | bytes 73760 | tf_op jit(solution)/shard_map/ppermute | solution.py:168
  11.0 1.6 %collective-permute-start.2 = (bf16[576,128]{1,0:T(8,128)(2,1)S(1)}, bf16[576,128]{1,0:T(8,128)(2,1)S(1)}, u32[]{:S(2)}, u32[]{:S(2)}) collective-permute-start(bf16[576,128]{1,0:T(8,128)(2,1)S(1)} %get-tuple-element.49), channel_id=1, source_target_pairs={{0,4},{1,3},{2,6},{3,1},{4,0},{5,7},{6,2},{7,5},{8,12},{9,11},{10,... | collective-permute-start | bytes 442376 | tf_op jit(solution)/shard_map/ppermute | solution.py:168
  12.6 2.0 %permute1.1 = (bf16[256,1152]{1,0:T(8,128)(2,1)S(1)}, bf16[256,1152]{1,0:T(8,128)(2,1)S(1)}) custom-call(s32[1,2304]{1,0:T(1,128)S(1)} %get-tuple-element.36.place_ref, f32[256,128]{1,0:T(8,128)S(1)} %get-tuple-element.30.reflectance_ref, bf16[256,2304]{1,0:T(8,128)(2,1)S(1)} %get-tuple-element.31.direct_ref), custom_call_target="tpu_custom_call" | custom-call | flops 1358954496 | tf_op jit(solution)/shard_map/permute1/pallas_call | solution.py:32
  14.7 1.6 %collective-permute-done.2 = bf16[576,128]{1,0:T(8,128)(2,1)S(1)} collective-permute-done((bf16[576,128]{1,0:T(8,128)(2,1)S(1)}, bf16[576,128]{1,0:T(8,128)(2,1)S(1)}, u32[]{:S(2)}, u32[]{:S(2)}) %collective-permute-start.2) | collective-permute-done | bytes 147488 | tf_op jit(solution)/shard_map/ppermute | solution.py:168
  16.3 0.1 collective-permute-start.3
  16.4 0.3 hours_own.1.base_ref
  16.7 1.3 %collective-permute-done.3.b_ref.sky_other_ref = bf16[1152,128]{1,0:T(8,128)(2,1)S(1)} collective-permute-done((bf16[1152,128]{1,0:T(8,128)(2,1)S(1)}, bf16[1152,128]{1,0:T(8,128)(2,1)S(1)}, u32[]{:S(2)}, u32[]{:S(2)}) %collective-permute-start.3) | collective-permute-done | bytes 294944 | tf_op jit(solution)/shard_map/ppermute | solution.py:173
  17.9 0.3 hours_all.1
  18.2 2.6 %collective-permute-start.4 = (bf16[256,128]{1,0:T(8,128)(2,1)S(1)}, bf16[256,128]{1,0:T(8,128)(2,1)S(1)}, u32[]{:S(2)}, u32[]{:S(2)}) collective-permute-start(bf16[256,128]{1,0:T(8,128)(2,1)S(1)} %hours_all.1), channel_id=1, source_target_pairs={{0,8},{1,9},{2,10},{3,11},{4,12},{5,13},{6,14},{7,15},{8,0},{9,1},... | collective-permute-start | bytes 196616 | tf_op jit(solution)/shard_map/ppermute | solution.py:183
  20.9 0.6 %direct.1 = (f32[256,128]{1,0:T(8,128)S(1)}, bf16[256,4096]{1,0:T(8,128)(2,1)S(1)}) custom-call(bf16[256,1152]{1,0:T(8,128)(2,1)S(1)} %get-tuple-element.41.own_ref, bf16[256,1152]{1,0:T(8,128)(2,1)S(1)} %get-tuple-element.42.other_ref, bf16[1152,128]{1,0:T(8,128)(2,1)S(1)} %constant_dynamic-update-slice_fusion.5.b_ref.sky_own_ref, ...), custom_call_target="tpu_custom_call" | custom-call | flops 150994944 | tf_op jit(solution)/shard_map/direct/pallas_call | solution.py:32
  21.5 3.4 %collective-permute-done.4 = bf16[256,128]{1,0:T(8,128)(2,1)S(1)} collective-permute-done((bf16[256,128]{1,0:T(8,128)(2,1)S(1)}, bf16[256,128]{1,0:T(8,128)(2,1)S(1)}, u32[]{:S(2)}, u32[]{:S(2)}) %collective-permute-start.4) | collective-permute-done | bytes 65568 | tf_op jit(solution)/shard_map/ppermute | solution.py:183
  24.9 1.8 %collective-permute-start.5 = (bf16[512,128]{1,0:T(8,128)(2,1)S(1)}, bf16[512,128]{1,0:T(8,128)(2,1)S(1)}, u32[]{:S(2)}, u32[]{:S(2)}) collective-permute-start(bf16[512,128]{1,0:T(8,128)(2,1)S(1)} %pad_maximum_fusion.2), channel_id=1, source_target_pairs={{0,2},{1,5},{2,0},{3,7},{4,6},{5,1},{6,4},{7,3},{8,10},{9,13},{10,... | collective-permute-start | bytes 393224 | tf_op jit(solution)/shard_map/ppermute | solution.py:183
  26.7 3.2 %collective-permute-done.5 = bf16[512,128]{1,0:T(8,128)(2,1)S(1)} collective-permute-done((bf16[512,128]{1,0:T(8,128)(2,1)S(1)}, bf16[512,128]{1,0:T(8,128)(2,1)S(1)}, u32[]{:S(2)}, u32[]{:S(2)}) %collective-permute-start.5) | collective-permute-done | bytes 131104 | tf_op jit(solution)/shard_map/ppermute | solution.py:183
  29.9 0.6 %collective-permute-start.6 = (bf16[1024,128]{1,0:T(8,128)(2,1)S(1)}, bf16[1024,128]{1,0:T(8,128)(2,1)S(1)}, u32[]{:S(2)}, u32[]{:S(2)}) collective-permute-start(bf16[1024,128]{1,0:T(8,128)(2,1)S(1)} %pad_maximum_fusion.1), channel_id=1, source_target_pairs={{0,4},{1,3},{2,6},{3,1},{4,0},{5,7},{6,2},{7,5},{8,12},{9,11},{10,... | collective-permute-start | bytes 786440 | tf_op jit(solution)/shard_map/ppermute | solution.py:183
  30.5 5.9 %collective-permute-done.6 = bf16[1024,128]{1,0:T(8,128)(2,1)S(1)} collective-permute-done((bf16[1024,128]{1,0:T(8,128)(2,1)S(1)}, bf16[1024,128]{1,0:T(8,128)(2,1)S(1)}, u32[]{:S(2)}, u32[]{:S(2)}) %collective-permute-start.6) | collective-permute-done | bytes 262176 | tf_op jit(solution)/shard_map/ppermute | solution.py:183
  36.4 0.1 collective-permute-start.7
  36.5 0.4 %bounce_own.1.base_ref = f32[256,128]{1,0:T(8,128)S(1)} custom-call(s32[1]{0:T(128)} %bitcast.me_ref, f32[256,128]{1,0:T(8,128)S(1)} %get-tuple-element.46.base_ref, bf16[256,4096]{1,0:T(8,128)(2,1)S(1)} %get-tuple-element.47.factors_ref, bf16[2048,128]{1,0:T(8,128)(2,1)S(1)} %pad_maximum_fusion.hours_ref), custom_call_target="tpu_custom_call" | custom-call | flops 134217728 | tf_op jit(solution)/shard_map/bounce_own/pallas_call | solution.py:32
  36.9 1.5 %collective-permute-done.7.hours_ref = bf16[2048,128]{1,0:T(8,128)(2,1)S(1)} collective-permute-done((bf16[2048,128]{1,0:T(8,128)(2,1)S(1)}, bf16[2048,128]{1,0:T(8,128)(2,1)S(1)}, u32[]{:S(2)}, u32[]{:S(2)}) %collective-permute-start.7) | collective-permute-done | bytes 524320 | tf_op jit(solution)/shard_map/ppermute | solution.py:202
  38.4 1.1 %bounce_all.1 = bf16[256,128]{1,0:T(8,128)(2,1)} custom-call(s32[1]{0:T(128)} %bitcast.me_ref, f32[256,128]{1,0:T(8,128)S(1)} %bounce_own.1.base_ref, bf16[256,4096]{1,0:T(8,128)(2,1)S(1)} %get-tuple-element.47.factors_ref, bf16[2048,128]{1,0:T(8,128)(2,1)S(1)} %collective-permute-done.7.hours_ref), custom_call_target="tpu_custom_call" | custom-call | flops 134217728 | tf_op jit(solution)/shard_map/bounce_all/pallas_call | solution.py:32
  (9 shorter events, 0.1 us)
Async XLA Ops:
  0.0 6.6 %collective-permute-start = (bf16[144,128]{1,0:T(8,128)(2,1)}, bf16[144,128]{1,0:T(8,128)(2,1)S(1)}, u32[]{:S(2)}, u32[]{:S(2)}) collective-permute-start(bf16[144,128]{1,0:T(8,128)(2,1)} %sky_in.1), channel_id=1, source_target_pairs={{0,8},{1,9},{2,10},{3,11},{4,12},{5,13},{6,14},{7,15},{8,0},{9,1},... | collective-permute-start | bytes 110600 | tf_op jit(solution)/shard_map/ppermute | solution.py:168
  6.6 4.4 %collective-permute-start.1 = (bf16[288,128]{1,0:T(8,128)(2,1)S(1)}, bf16[288,128]{1,0:T(8,128)(2,1)S(1)}, u32[]{:S(2)}, u32[]{:S(2)}) collective-permute-start(bf16[288,128]{1,0:T(8,128)(2,1)S(1)} %get-tuple-element.53), channel_id=1, source_target_pairs={{0,2},{1,5},{2,0},{3,7},{4,6},{5,1},{6,4},{7,3},{8,10},{9,13},{10,... | collective-permute-start | bytes 221192 | tf_op jit(solution)/shard_map/ppermute | solution.py:168
  11.0 5.2 %collective-permute-start.2 = (bf16[576,128]{1,0:T(8,128)(2,1)S(1)}, bf16[576,128]{1,0:T(8,128)(2,1)S(1)}, u32[]{:S(2)}, u32[]{:S(2)}) collective-permute-start(bf16[576,128]{1,0:T(8,128)(2,1)S(1)} %get-tuple-element.49), channel_id=1, source_target_pairs={{0,4},{1,3},{2,6},{3,1},{4,0},{5,7},{6,2},{7,5},{8,12},{9,11},{10,... | collective-permute-start | bytes 442376 | tf_op jit(solution)/shard_map/ppermute | solution.py:168
  14.6 6.2 %copy-start = (bf16[256,4096]{1,0:T(8,128)(2,1)S(1)}, bf16[256,4096]{1,0:T(8,128)(2,1)}, u32[]{:S(2)}) copy-start(bf16[256,4096]{1,0:T(8,128)(2,1)} %factors_ref.1) | copy-start | bytes 6291460
  16.3 1.6 %collective-permute-start.3 = (bf16[1152,128]{1,0:T(8,128)(2,1)S(1)}, bf16[1152,128]{1,0:T(8,128)(2,1)S(1)}, u32[]{:S(2)}, u32[]{:S(2)}) collective-permute-start(bf16[1152,128]{1,0:T(8,128)(2,1)S(1)} %constant_dynamic-update-slice_fusion.5.b_ref.sky_own_ref), channel_id=1, source_target_pairs={{0,1},{1,0},{2,3},{3,2},{4,5},{5,4},{6,7},{7,6},{8,9},{9,8},{10,11... | collective-permute-start | bytes 884744 | tf_op jit(solution)/shard_map/ppermute | solution.py:173
  18.2 6.6 %collective-permute-start.4 = (bf16[256,128]{1,0:T(8,128)(2,1)S(1)}, bf16[256,128]{1,0:T(8,128)(2,1)S(1)}, u32[]{:S(2)}, u32[]{:S(2)}) collective-permute-start(bf16[256,128]{1,0:T(8,128)(2,1)S(1)} %hours_all.1), channel_id=1, source_target_pairs={{0,8},{1,9},{2,10},{3,11},{4,12},{5,13},{6,14},{7,15},{8,0},{9,1},... | collective-permute-start | bytes 196616 | tf_op jit(solution)/shard_map/ppermute | solution.py:183
  24.9 5.0 %collective-permute-start.5 = (bf16[512,128]{1,0:T(8,128)(2,1)S(1)}, bf16[512,128]{1,0:T(8,128)(2,1)S(1)}, u32[]{:S(2)}, u32[]{:S(2)}) collective-permute-start(bf16[512,128]{1,0:T(8,128)(2,1)S(1)} %pad_maximum_fusion.2), channel_id=1, source_target_pairs={{0,2},{1,5},{2,0},{3,7},{4,6},{5,1},{6,4},{7,3},{8,10},{9,13},{10,... | collective-permute-start | bytes 393224 | tf_op jit(solution)/shard_map/ppermute | solution.py:183
  29.9 6.4 %collective-permute-start.6 = (bf16[1024,128]{1,0:T(8,128)(2,1)S(1)}, bf16[1024,128]{1,0:T(8,128)(2,1)S(1)}, u32[]{:S(2)}, u32[]{:S(2)}) collective-permute-start(bf16[1024,128]{1,0:T(8,128)(2,1)S(1)} %pad_maximum_fusion.1), channel_id=1, source_target_pairs={{0,4},{1,3},{2,6},{3,1},{4,0},{5,7},{6,2},{7,5},{8,12},{9,11},{10,... | collective-permute-start | bytes 786440 | tf_op jit(solution)/shard_map/ppermute | solution.py:183
  36.4 2.0 %collective-permute-start.7 = (bf16[2048,128]{1,0:T(8,128)(2,1)S(1)}, bf16[2048,128]{1,0:T(8,128)(2,1)S(1)}, u32[]{:S(2)}, u32[]{:S(2)}) collective-permute-start(bf16[2048,128]{1,0:T(8,128)(2,1)S(1)} %pad_maximum_fusion.hours_ref), channel_id=1, source_target_pairs={{0,1},{1,0},{2,3},{3,2},{4,5},{5,4},{6,7},{7,6},{8,9},{9,8},{10,11... | collective-permute-start | bytes 1572872 | tf_op jit(solution)/shard_map/ppermute | solution.py:202

commit v3 on v2

v3 whole, which is shorter than its diff:
```python
import functools

import jax
import jax.numpy as jnp
from jax import lax
from jax.experimental import pallas as pl
from jax.experimental.pallas import tpu as pltpu
from jax.sharding import PartitionSpec as P

WHOLE = pl.BlockSpec(memory_space=pltpu.VMEM)
ANYWHERE = pl.BlockSpec(memory_space=pltpu.HBM)
SCALARS = pl.BlockSpec(memory_space=pltpu.SMEM)


def parity(i):
    for shift in (8, 4, 2, 1):
        i = i ^ (i >> shift)
    return i & 1


class Piece:
    def __init__(self, value, masks):
        self.value = value
        self.masks = masks


def join(*pieces):
    masks = [sum((p.masks[c] for p in pieces), []) for c in range(2)]
    return Piece(None if pieces[0].value is None else jnp.concatenate([p.value for p in pieces], axis=0), masks)


def swap(size, piece, *bits):
    bits = bits * (2 // len(bits))
    pairs = [(i, i ^ bits[parity(i)]) for i in range(size)]
    masks = [[m ^ bits[c] for m in piece.masks[c ^ parity(bits[c])]] for c in range(2)]
    return Piece(None if piece.value is None else lax.ppermute(piece.value, "col", pairs), masks)


def gather(size, block, copy, early=(), late=lambda _: []):
    exchange = functools.partial(swap, size)
    near, next_, far, *farther = [2 << b | 1 for b in range(size.bit_length() - 2)]
    one, other, both = (near, next_), (next_, near), near ^ next_ ^ 1

    def wait(piece, others):
        if len(others) and piece.value is not None:
            piece.value, others = lax.optimization_barrier((piece.value, others))
        return others

    mine = [Piece(value, [[0], [0]]) for value in (block, copy)]
    for bits in farther[::-1]:
        mine = [join(piece, exchange(piece, bits)) for piece in mine]
    from_far = exchange(mine[0], far)
    came = exchange(mine[1], *one)
    ours = join(mine[1], came)
    beside = exchange(ours, *other)
    early = wait(from_far, [ours.value, *early])[1:]
    beyond = [exchange(from_far, *other), exchange(from_far, *one), exchange(from_far, both)]
    late = wait(beyond[-1], late(from_far.value))
    same = join(from_far, ours, *beyond, beside)
    return same, exchange(same, 1), early, late


def call(kernel, name, outs, specs, flops, *args, scratch=(), vmem=24):
    return pl.pallas_call(
        kernel,
        scratch_shapes=scratch,
        out_shape=outs,
        in_specs=specs,
        out_specs=jax.tree.map(lambda _: WHOLE, outs),
        compiler_params=pltpu.CompilerParams(vmem_limit_bytes=vmem * 2**20),
        cost_estimate=pl.CostEstimate(flops=flops, bytes_accessed=0, transcendentals=0),
        name=name,
    )(*args)


def prepare_kernel(albedo_in, material_in, order_in, sky_in, direct_in, me_ref, *refs):
    sky_out, direct_out, reflectance_out, where_out, albedo_ref, material_ref, order_ref, sems = refs
    moves = ((albedo_in, albedo_ref), (material_in, material_ref), (order_in, order_ref))
    moves += ((sky_in, sky_out), (direct_in, direct_out))
    copies = [pltpu.make_async_copy(source, target, sems.at[i]) for i, (source, target) in enumerate(moves)]
    for copy in copies:
        copy.start()
    for copy in copies[:3]:
        copy.wait()
    material = material_ref[...].reshape(1, -1)
    reflectance = jnp.zeros(material.shape, jnp.float32)
    for m in range(albedo_ref.shape[0]):
        reflectance = jnp.where(material == m, albedo_ref[m], reflectance)
    reflectance_out[...] = jnp.broadcast_to(reflectance, (128, reflectance.shape[1])).T
    rows = sky_in.shape[0]
    order = order_ref[...].reshape(1, -1)
    owner = (order * -(-(1 << 20) // rows)) >> 20
    where_out[:1] = owner ^ me_ref[0]
    where_out[1:] = order - owner * rows
    for copy in copies[3:]:
        copy.wait()


def permute_kernel(masks, rows, me_ref, where_ref, reflectance_ref, direct_ref, sorted_ref, reflected_ref):
    count = sorted_ref.shape[1]
    odd = parity(me_ref[0])
    apart = where_ref[:1]
    first = jnp.full(apart.shape, -count, jnp.int32)
    for slot, (mask_even, mask_odd) in enumerate(zip(*masks)):
        first = jnp.where(apart == jnp.where(odd == 0, mask_even, mask_odd), slot * rows, first)
    place = first + where_ref[1:]
    reflectance = reflectance_ref[:, :1]
    step = 384
    for j in range(0, count, step):
        width = min(step, count - j)
        position = lax.broadcasted_iota(jnp.int32, (width, place.shape[1]), 0) + j
        pick = jnp.where(position == place, 1.0, 0.0).astype(jnp.bfloat16)
        part = lax.dot_general(direct_ref[...], pick, (((1,), (1,)), ((), ())), preferred_element_type=jnp.float32)
        sorted_ref[:, j : j + width] = part.astype(jnp.bfloat16)
        reflected_ref[:, j : j + width] = (reflectance * part).astype(jnp.bfloat16)


def dot_kernel(a_ref, b_ref, out_ref):
    out_ref[...] = jnp.dot(a_ref[...], b_ref[...], preferred_element_type=jnp.float32)


def add_dot_kernel(base_ref, a_ref, b_ref, out_ref):
    part = jnp.dot(a_ref[...], b_ref[...], preferred_element_type=jnp.float32)
    out_ref[...] = (base_ref[...] + part).astype(out_ref.dtype)


def direct_kernel(first_ref, second_ref, sky_first_ref, sky_second_ref, hours_ref, out_ref, hours_out):
    hours_out[...] = hours_ref[...]
    out = jnp.dot(first_ref[...], sky_first_ref[...], preferred_element_type=jnp.float32)
    out_ref[...] = out + jnp.dot(second_ref[...], sky_second_ref[...], preferred_element_type=jnp.float32)


def bounce_kernel(masks, me_ref, base_ref, factors_ref, hours_ref, out_ref):
    me = me_ref[0]
    odd = parity(me)
    total = base_ref[...]
    patches = out_ref.shape[0]
    for slot, (mask_even, mask_odd) in enumerate(zip(*masks)):
        owner = me ^ jnp.where(odd == 0, mask_even, mask_odd)
        total += jnp.dot(
            factors_ref[:, pl.ds(pl.multiple_of(owner * patches, patches), patches)],
            hours_ref[slot * patches : (slot + 1) * patches, :],
            preferred_element_type=jnp.float32,
        )
    out_ref[...] = total.astype(out_ref.dtype)


def shards(size, view_factors, direct_coeff, material, albedo, sky_matrix, sky_order):
    index = lax.axis_index("col").reshape(1)
    rows, hours = sky_matrix.shape
    patches, skies = direct_coeff.shape
    span = size // 2 * rows
    sky, direct_coeff, reflectance, where = call(
        prepare_kernel,
        "prepare",
        (
            pltpu.VMEM(sky_matrix.shape, sky_matrix.dtype),
            pltpu.VMEM(direct_coeff.shape, direct_coeff.dtype),
            pltpu.VMEM((patches, 128), jnp.float32),
            pltpu.VMEM((2, skies), jnp.int32),
        ),
        [ANYWHERE] * 5 + [SCALARS],
        10**9,
        *(pltpu.with_memory_space_constraint(x, pltpu.HBM) for x in (albedo, material, sky_order, sky_matrix, direct_coeff)),
        index,
        scratch=[
            pltpu.SMEM(albedo.shape, albedo.dtype),
            pltpu.VMEM(material.shape, material.dtype),
            pltpu.VMEM(sky_order.shape, sky_order.dtype),
            pltpu.SemaphoreType.DMA((5,)),
        ],
    )
    same, across, _, _ = gather(size, None, None)

    def permute(piece, name, start=None):
        place = where if start is None else lax.optimization_barrier((where, start))[0]
        return call(
            functools.partial(permute_kernel, piece.masks, rows),
            name,
            (jax.ShapeDtypeStruct((patches, span), jnp.bfloat16),) * 2,
            [SCALARS] + [WHOLE] * 3,
            2 * patches * skies * span,
            index,
            place,
            reflectance,
            direct_coeff,
        )

    late = functools.partial(permute, across, "permute_across")
    same, across, first, second = gather(size, sky_matrix, sky, permute(same, "permute_same"), late)

    flat = jax.ShapeDtypeStruct((patches, hours), jnp.float32)
    short = jax.ShapeDtypeStruct((patches, hours), jnp.bfloat16)
    flops = 2 * patches * span * hours
    part = call(dot_kernel, "hours_same", flat, [WHOLE] * 2, flops, first[1], same.value)
    own = call(add_dot_kernel, "hours_all", short, [WHOLE] * 3, flops, part, second[1], across.value)
    total, copy = call(
        direct_kernel,
        "direct",
        (flat, pltpu.VMEM(own.shape, own.dtype)),
        [WHOLE] * 5,
        2 * flops,
        first[0],
        second[0],
        same.value,
        across.value,
        own,
    )
    same, across, (total,), _ = gather(size, own, copy, [total])

    def bounce(name, base, piece, out):
        return call(
            functools.partial(bounce_kernel, piece.masks),
            name,
            out,
            [SCALARS] + [WHOLE] * 3,
            2 * patches * piece.value.size,
            index,
            base,
            view_factors,
            piece.value,
        )

    return bounce("bounce_across", bounce("bounce_same", total, same, flat), across, short)


def solution(mesh):
    return jax.shard_map(
        functools.partial(shards, mesh.shape["col"]),
        mesh=mesh,
        in_specs=(
            P(("parts", "col"), None),
            P(("parts", "col"), None),
            P(("parts", "col")),
            P("parts"),
            P("col", None),
            P(),
        ),
        out_specs=P(("parts", "col"), None),
        check_vma=False,
    )
```

time: 39.6 us -> 35.7 us (0.902)
  waiting for transfers between devices: 18.6 us -> 12.6 us
  starting transfers between devices: 12.5 us -> 14.6 us
    ppermute x8 -> x14, waiting for transfers between devices: 18.6 us -> 12.6 us  [swap(): lax.ppermute(piece.value, 'col', pairs)]
    ppermute x8 -> x14, starting transfers between devices: 12.5 us -> 14.6 us  [swap(): lax.ppermute(piece.value, 'col', pairs)]
  transfers between devices with their start and end apart: 8 -> 14, of which waited for: 8 -> 7; matrix products, arithmetic and copies ran while one was open for 0% -> 0% of each run, Pallas kernels for 17% -> 19%
where the time goes in v3:
time: 35.7 us; the launch traced here: 35.5 us
  starting transfers between devices  14.6 us (41%)
  waiting for transfers between devices  12.6 us (35%)
  Pallas kernels  7.94 us (22%)
    ppermute x14, starting transfers between devices, swap(): lax.ppermute(piece.value, 'col', pairs)  14.6 us
    ppermute x14, waiting for transfers between devices, swap(): lax.ppermute(piece.value, 'col', pairs)  12.6 us
    pallas_call x8, Pallas kernels, call(): pl.pallas_call(kernel, scratch_shapes=scratch, out_shape=outs, in_specs=s...  7.94 us
  transfers between devices with their start and end apart: 14, of which 7 were waited for; matrix products, arithmetic and copies ran while one was open for 0% of the time, Pallas kernels for 19%

profile of v3, /device:TPU:0, one launch (start us, length us, event | category | flops | bytes accessed | tf_op | source)
XLA Modules:
  0.0 35.5 jit_solution(16190881328468549066)
XLA Ops:
  0.0 3.5 %collective-permute-start = (bf16[144,128]{1,0:T(8,128)(2,1)}, bf16[144,128]{1,0:T(8,128)(2,1)S(1)}, u32[]{:S(2)}, u32[]{:S(2)}) collective-permute-start(bf16[144,128]{1,0:T(8,128)(2,1)} %sky_in.1), channel_id=1, source_target_pairs={{0,9},{1,8},{2,11},{3,10},{4,13},{5,12},{6,15},{7,14},{8,1},{9,0},... | collective-permute-start | bytes 110600 | tf_op jit(solution)/shard_map/ppermute | solution.py:36
  3.5 1.4 %prepare.1 = (bf16[144,128]{1,0:T(8,128)(2,1)S(1)}, bf16[256,2304]{1,0:T(8,128)(2,1)S(1)}, f32[256,128]{1,0:T(8,128)S(1)}, s32[2,2304]{1,0:T(2,128)S(1)}) custom-call(f32[16]{0:T(128)} %albedo_in.1, s32[256]{0:T(256)} %material_in.1, s32[2304]{0:T(1024)} %order_in.1, bf16[144,128]{1,0:T(8,128)(2,1)} %sky_in.1, bf16[256,2304]{1,0:T(8,128)(2,1)} %direct_in.1, ...), custom_call_target="tpu_custom_call" | custom-call | flops 1000000000 | tf_op jit(solution)/shard_map/prepare/pallas_call | solution.py:64
  4.9 1.9 %collective-permute-start.1 = (bf16[144,128]{1,0:T(8,128)(2,1)S(1)}, bf16[144,128]{1,0:T(8,128)(2,1)S(1)}, u32[]{:S(2)}, u32[]{:S(2)}) collective-permute-start(bf16[144,128]{1,0:T(8,128)(2,1)S(1)} %get-tuple-element.24), channel_id=1, source_target_pairs={{0,3},{1,4},{2,7},{3,0},{4,1},{5,6},{6,5},{7,2},{8,13},{9,10},{10,... | collective-permute-start | bytes 110600 | tf_op jit(solution)/shard_map/ppermute | solution.py:36
  6.7 2.0 %permute_same.1 = (bf16[256,1152]{1,0:T(8,128)(2,1)S(1)}, bf16[256,1152]{1,0:T(8,128)(2,1)S(1)}) custom-call(s32[1]{0:T(128)} %bitcast.me_ref, s32[2,2304]{1,0:T(2,128)S(1)} %get-tuple-element.32.where_ref, f32[256,128]{1,0:T(8,128)S(1)} %get-tuple-element.26.reflectance_ref, bf16[256,2304]{1,0:T(8,128)(2,1)S(1)} %get-tuple-element.27.direct_ref), custom_call_target="tpu_custom_call" | custom-call | flops 1358954496 | tf_op jit(solution)/shard_map/permute_same/pallas_call | solution.py:64
  8.8 1.5 %collective-permute-start.5 = (bf16[288,128]{1,0:T(8,128)(2,1)S(1)}, bf16[288,128]{1,0:T(8,128)(2,1)S(1)}, u32[]{:S(2)}, u32[]{:S(2)}) collective-permute-start(bf16[288,128]{1,0:T(8,128)(2,1)S(1)} %constant_dynamic-update-slice_fusion), channel_id=1, source_target_pairs={{0,5},{1,2},{2,1},{3,6},{4,7},{5,0},{6,3},{7,4},{8,11},{9,12},{10,... | collective-permute-start | bytes 221192 | tf_op jit(solution)/shard_map/ppermute | solution.py:36
  10.2 1.0 %collective-permute-start.4 = (bf16[144,128]{1,0:T(8,128)(2,1)S(1)}, bf16[144,128]{1,0:T(8,128)(2,1)S(1)}, u32[]{:S(2)}, u32[]{:S(2)}) collective-permute-start(bf16[144,128]{1,0:T(8,128)(2,1)S(1)} %collective-permute-done), channel_id=1, source_target_pairs={{0,7},{1,6},{2,5},{3,4},{4,3},{5,2},{6,1},{7,0},{8,15},{9,14},{10,... | collective-permute-start | bytes 110600 | tf_op jit(solution)/shard_map/ppermute | solution.py:36
  11.3 1.7 %collective-permute-start.3 = (bf16[144,128]{1,0:T(8,128)(2,1)S(1)}, bf16[144,128]{1,0:T(8,128)(2,1)S(1)}, u32[]{:S(2)}, u32[]{:S(2)}) collective-permute-start(bf16[144,128]{1,0:T(8,128)(2,1)S(1)} %collective-permute-done), channel_id=1, source_target_pairs={{0,3},{1,4},{2,7},{3,0},{4,1},{5,6},{6,5},{7,2},{8,13},{9,10},{10,... | collective-permute-start | bytes 110600 | tf_op jit(solution)/shard_map/ppermute | solution.py:36
  12.9 0.4 %collective-permute-start.2 = (bf16[144,128]{1,0:T(8,128)(2,1)S(1)}, bf16[144,128]{1,0:T(8,128)(2,1)S(1)}, u32[]{:S(2)}, u32[]{:S(2)}) collective-permute-start(bf16[144,128]{1,0:T(8,128)(2,1)S(1)} %collective-permute-done), channel_id=1, source_target_pairs={{0,5},{1,2},{2,1},{3,6},{4,7},{5,0},{6,3},{7,4},{8,11},{9,12},{10,... | collective-permute-start | bytes 110600 | tf_op jit(solution)/shard_map/ppermute | solution.py:36
  13.4 2.0 %permute_across.1 = (bf16[256,1152]{1,0:T(8,128)(2,1)S(1)}, bf16[256,1152]{1,0:T(8,128)(2,1)S(1)}) custom-call(s32[1]{0:T(128)} %bitcast.me_ref, s32[2,2304]{1,0:T(2,128)S(1)} %get-tuple-element.32.where_ref, f32[256,128]{1,0:T(8,128)S(1)} %get-tuple-element.26.reflectance_ref, bf16[256,2304]{1,0:T(8,128)(2,1)S(1)} %get-tuple-element.27.direct_ref), custom_call_target="tpu_custom_call" | custom-call | flops 1358954496 | tf_op jit(solution)/shard_map/permute_across/pallas_call | solution.py:64
  15.4 0.9 %collective-permute-done.2 = bf16[144,128]{1,0:T(8,128)(2,1)S(1)} collective-permute-done((bf16[144,128]{1,0:T(8,128)(2,1)S(1)}, bf16[144,128]{1,0:T(8,128)(2,1)S(1)}, u32[]{:S(2)}, u32[]{:S(2)}) %collective-permute-start.2) | collective-permute-done | bytes 36896 | tf_op jit(solution)/shard_map/ppermute | solution.py:36
  16.9 1.2 %collective-permute-done.6.b_ref.sky_second_ref = bf16[1152,128]{1,0:T(8,128)(2,1)S(1)} collective-permute-done((bf16[1152,128]{1,0:T(8,128)(2,1)S(1)}, bf16[1152,128]{1,0:T(8,128)(2,1)S(1)}, u32[]{:S(2)}, u32[]{:S(2)}) %collective-permute-start.6) | collective-permute-done | bytes 294944 | tf_op jit(solution)/shard_map/ppermute | solution.py:36
  18.4 0.4 %collective-permute-start.7 = (bf16[256,128]{1,0:T(8,128)(2,1)S(1)}, bf16[256,128]{1,0:T(8,128)(2,1)S(1)}, u32[]{:S(2)}, u32[]{:S(2)}) collective-permute-start(bf16[256,128]{1,0:T(8,128)(2,1)S(1)} %hours_all.1.hours_ref), channel_id=1, source_target_pairs={{0,9},{1,8},{2,11},{3,10},{4,13},{5,12},{6,15},{7,14},{8,1},{9,0},... | collective-permute-start | bytes 196616 | tf_op jit(solution)/shard_map/ppermute | solution.py:36
  18.8 0.5 %direct.1 = (f32[256,128]{1,0:T(8,128)S(1)}, bf16[256,128]{1,0:T(8,128)(2,1)S(1)}) custom-call(bf16[256,1152]{1,0:T(8,128)(2,1)S(1)} %get-tuple-element.37.first_ref, bf16[256,1152]{1,0:T(8,128)(2,1)S(1)} %get-tuple-element.38.second_ref, bf16[1152,128]{1,0:T(8,128)(2,1)S(1)} %constant_dynamic-update-slice_fusion.2.b_ref.sky_first_ref, ...), custom_call_target="tpu_custom_call" | custom-call | flops 150994944 | tf_op jit(solution)/shard_map/direct/pallas_call | solution.py:64
  19.3 0.8 %collective-permute-start.8 = (bf16[256,128]{1,0:T(8,128)(2,1)S(1)}, bf16[256,128]{1,0:T(8,128)(2,1)S(1)}, u32[]{:S(2)}, u32[]{:S(2)}) collective-permute-start(bf16[256,128]{1,0:T(8,128)(2,1)S(1)} %get-tuple-element.39), channel_id=1, source_target_pairs={{0,3},{1,4},{2,7},{3,0},{4,1},{5,6},{6,5},{7,2},{8,13},{9,10},{10,... | collective-permute-start | bytes 196616 | tf_op jit(solution)/shard_map/ppermute | solution.py:36
  20.1 3.0 %collective-permute-done.8 = bf16[256,128]{1,0:T(8,128)(2,1)S(1)} collective-permute-done((bf16[256,128]{1,0:T(8,128)(2,1)S(1)}, bf16[256,128]{1,0:T(8,128)(2,1)S(1)}, u32[]{:S(2)}, u32[]{:S(2)}) %collective-permute-start.8) | collective-permute-done | bytes 65568 | tf_op jit(solution)/shard_map/ppermute | solution.py:36
  23.1 2.0 %collective-permute-done.7 = bf16[256,128]{1,0:T(8,128)(2,1)S(1)} collective-permute-done((bf16[256,128]{1,0:T(8,128)(2,1)S(1)}, bf16[256,128]{1,0:T(8,128)(2,1)S(1)}, u32[]{:S(2)}, u32[]{:S(2)}) %collective-permute-start.7) | collective-permute-done | bytes 65568 | tf_op jit(solution)/shard_map/ppermute | solution.py:36
  25.0 0.5 %collective-permute-start.10 = (bf16[256,128]{1,0:T(8,128)(2,1)S(1)}, bf16[256,128]{1,0:T(8,128)(2,1)S(1)}, u32[]{:S(2)}, u32[]{:S(2)}) collective-permute-start(bf16[256,128]{1,0:T(8,128)(2,1)S(1)} %collective-permute-done.7), channel_id=1, source_target_pairs={{0,3},{1,4},{2,7},{3,0},{4,1},{5,6},{6,5},{7,2},{8,13},{9,10},{10,... | collective-permute-start | bytes 196616 | tf_op jit(solution)/shard_map/ppermute | solution.py:36
  25.5 2.5 %collective-permute-start.9 = (bf16[256,128]{1,0:T(8,128)(2,1)S(1)}, bf16[256,128]{1,0:T(8,128)(2,1)S(1)}, u32[]{:S(2)}, u32[]{:S(2)}) collective-permute-start(bf16[256,128]{1,0:T(8,128)(2,1)S(1)} %collective-permute-done.7), channel_id=1, source_target_pairs={{0,5},{1,2},{2,1},{3,6},{4,7},{5,0},{6,3},{7,4},{8,11},{9,12},{10,... | collective-permute-start | bytes 196616 | tf_op jit(solution)/shard_map/ppermute | solution.py:36
  28.0 2.7 %collective-permute-done.9 = bf16[256,128]{1,0:T(8,128)(2,1)S(1)} collective-permute-done((bf16[256,128]{1,0:T(8,128)(2,1)S(1)}, bf16[256,128]{1,0:T(8,128)(2,1)S(1)}, u32[]{:S(2)}, u32[]{:S(2)}) %collective-permute-start.9) | collective-permute-done | bytes 65568 | tf_op jit(solution)/shard_map/ppermute | solution.py:36
  30.8 1.6 %collective-permute-done.12 = bf16[512,128]{1,0:T(8,128)(2,1)S(1)} collective-permute-done((bf16[512,128]{1,0:T(8,128)(2,1)S(1)}, bf16[512,128]{1,0:T(8,128)(2,1)S(1)}, u32[]{:S(2)}, u32[]{:S(2)}) %collective-permute-start.12) | collective-permute-done | bytes 131104 | tf_op jit(solution)/shard_map/ppermute | solution.py:36
  32.5 0.3 collective-permute-start.13
  32.8 0.4 %bounce_same.1.base_ref = f32[256,128]{1,0:T(8,128)S(1)} custom-call(s32[1]{0:T(128)} %bitcast.me_ref, f32[256,128]{1,0:T(8,128)S(1)} %get-tuple-element.41.base_ref, bf16[256,4096]{1,0:T(8,128)(2,1)S(1)} %copy-done, bf16[2048,128]{1,0:T(8,128)(2,1)S(1)} %constant_dynamic-update-slice_fusion.11.hours_ref), custom_call_target="tpu_custom_call" | custom-call | flops 134217728 | tf_op jit(solution)/shard_map/bounce_same/pallas_call | solution.py:64
  33.3 1.2 %collective-permute-done.13.hours_ref = bf16[2048,128]{1,0:T(8,128)(2,1)S(1)} collective-permute-done((bf16[2048,128]{1,0:T(8,128)(2,1)S(1)}, bf16[2048,128]{1,0:T(8,128)(2,1)S(1)}, u32[]{:S(2)}, u32[]{:S(2)}) %collective-permute-start.13) | collective-permute-done | bytes 524320 | tf_op jit(solution)/shard_map/ppermute | solution.py:36
  34.5 1.1 %bounce_across.1 = bf16[256,128]{1,0:T(8,128)(2,1)} custom-call(s32[1]{0:T(128)} %bitcast.me_ref, f32[256,128]{1,0:T(8,128)S(1)} %bounce_same.1.base_ref, bf16[256,4096]{1,0:T(8,128)(2,1)S(1)} %copy-done, bf16[2048,128]{1,0:T(8,128)(2,1)S(1)} %collective-permute-done.13.hours_ref), custom_call_target="tpu_custom_call" | custom-call | flops 134217728 | tf_op jit(solution)/shard_map/bounce_across/pallas_call | solution.py:64
  (32 shorter events, 1.0 us)
Async XLA Ops:
  0.0 10.2 %collective-permute-start = (bf16[144,128]{1,0:T(8,128)(2,1)}, bf16[144,128]{1,0:T(8,128)(2,1)S(1)}, u32[]{:S(2)}, u32[]{:S(2)}) collective-permute-start(bf16[144,128]{1,0:T(8,128)(2,1)} %sky_in.1), channel_id=1, source_target_pairs={{0,9},{1,8},{2,11},{3,10},{4,13},{5,12},{6,15},{7,14},{8,1},{9,0},... | collective-permute-start | bytes 110600 | tf_op jit(solution)/shard_map/ppermute | solution.py:36
  4.9 3.9 %collective-permute-start.1 = (bf16[144,128]{1,0:T(8,128)(2,1)S(1)}, bf16[144,128]{1,0:T(8,128)(2,1)S(1)}, u32[]{:S(2)}, u32[]{:S(2)}) collective-permute-start(bf16[144,128]{1,0:T(8,128)(2,1)S(1)} %get-tuple-element.24), channel_id=1, source_target_pairs={{0,3},{1,4},{2,7},{3,0},{4,1},{5,6},{6,5},{7,2},{8,13},{9,10},{10,... | collective-permute-start | bytes 110600 | tf_op jit(solution)/shard_map/ppermute | solution.py:36
  8.8 7.6 %collective-permute-start.5 = (bf16[288,128]{1,0:T(8,128)(2,1)S(1)}, bf16[288,128]{1,0:T(8,128)(2,1)S(1)}, u32[]{:S(2)}, u32[]{:S(2)}) collective-permute-start(bf16[288,128]{1,0:T(8,128)(2,1)S(1)} %constant_dynamic-update-slice_fusion), channel_id=1, source_target_pairs={{0,5},{1,2},{2,1},{3,6},{4,7},{5,0},{6,3},{7,4},{8,11},{9,12},{10,... | collective-permute-start | bytes 221192 | tf_op jit(solution)/shard_map/ppermute | solution.py:36
  10.2 6.1 %collective-permute-start.4 = (bf16[144,128]{1,0:T(8,128)(2,1)S(1)}, bf16[144,128]{1,0:T(8,128)(2,1)S(1)}, u32[]{:S(2)}, u32[]{:S(2)}) collective-permute-start(bf16[144,128]{1,0:T(8,128)(2,1)S(1)} %collective-permute-done), channel_id=1, source_target_pairs={{0,7},{1,6},{2,5},{3,4},{4,3},{5,2},{6,1},{7,0},{8,15},{9,14},{10,... | collective-permute-start | bytes 110600 | tf_op jit(solution)/shard_map/ppermute | solution.py:36
  11.3 5.1 %collective-permute-start.3 = (bf16[144,128]{1,0:T(8,128)(2,1)S(1)}, bf16[144,128]{1,0:T(8,128)(2,1)S(1)}, u32[]{:S(2)}, u32[]{:S(2)}) collective-permute-start(bf16[144,128]{1,0:T(8,128)(2,1)S(1)} %collective-permute-done), channel_id=1, source_target_pairs={{0,3},{1,4},{2,7},{3,0},{4,1},{5,6},{6,5},{7,2},{8,13},{9,10},{10,... | collective-permute-start | bytes 110600 | tf_op jit(solution)/shard_map/ppermute | solution.py:36
  12.9 3.4 %collective-permute-start.2 = (bf16[144,128]{1,0:T(8,128)(2,1)S(1)}, bf16[144,128]{1,0:T(8,128)(2,1)S(1)}, u32[]{:S(2)}, u32[]{:S(2)}) collective-permute-start(bf16[144,128]{1,0:T(8,128)(2,1)S(1)} %collective-permute-done), channel_id=1, source_target_pairs={{0,5},{1,2},{2,1},{3,6},{4,7},{5,0},{6,3},{7,4},{8,11},{9,12},{10,... | collective-permute-start | bytes 110600 | tf_op jit(solution)/shard_map/ppermute | solution.py:36
  16.4 1.6 %collective-permute-start.6 = (bf16[1152,128]{1,0:T(8,128)(2,1)S(1)}, bf16[1152,128]{1,0:T(8,128)(2,1)S(1)}, u32[]{:S(2)}, u32[]{:S(2)}) collective-permute-start(bf16[1152,128]{1,0:T(8,128)(2,1)S(1)} %constant_dynamic-update-slice_fusion.2.b_ref.sky_first_ref), channel_id=1, source_target_pairs={{0,1},{1,0},{2,3},{3,2},{4,5},{5,4},{6,7},{7,6},{8,9},{9,8},{10,11... | collective-permute-start | bytes 884744 | tf_op jit(solution)/shard_map/ppermute | solution.py:36
  18.4 14.5 %copy-start = (bf16[256,4096]{1,0:T(8,128)(2,1)S(1)}, bf16[256,4096]{1,0:T(8,128)(2,1)}, u32[]{:S(2)}) copy-start(bf16[256,4096]{1,0:T(8,128)(2,1)} %factors_ref.3) | copy-start | bytes 6291460
  18.4 6.6 %collective-permute-start.7 = (bf16[256,128]{1,0:T(8,128)(2,1)S(1)}, bf16[256,128]{1,0:T(8,128)(2,1)S(1)}, u32[]{:S(2)}, u32[]{:S(2)}) collective-permute-start(bf16[256,128]{1,0:T(8,128)(2,1)S(1)} %hours_all.1.hours_ref), channel_id=1, source_target_pairs={{0,9},{1,8},{2,11},{3,10},{4,13},{5,12},{6,15},{7,14},{8,1},{9,0},... | collective-permute-start | bytes 196616 | tf_op jit(solution)/shard_map/ppermute | solution.py:36
  19.3 3.8 %collective-permute-start.8 = (bf16[256,128]{1,0:T(8,128)(2,1)S(1)}, bf16[256,128]{1,0:T(8,128)(2,1)S(1)}, u32[]{:S(2)}, u32[]{:S(2)}) collective-permute-start(bf16[256,128]{1,0:T(8,128)(2,1)S(1)} %get-tuple-element.39), channel_id=1, source_target_pairs={{0,3},{1,4},{2,7},{3,0},{4,1},{5,6},{6,5},{7,2},{8,13},{9,10},{10,... | collective-permute-start | bytes 196616 | tf_op jit(solution)/shard_map/ppermute | solution.py:36
  25.0 5.8 %collective-permute-start.11 = (bf16[256,128]{1,0:T(8,128)(2,1)S(1)}, bf16[256,128]{1,0:T(8,128)(2,1)S(1)}, u32[]{:S(2)}, u32[]{:S(2)}) collective-permute-start(bf16[256,128]{1,0:T(8,128)(2,1)S(1)} %collective-permute-done.7), channel_id=1, source_target_pairs={{0,7},{1,6},{2,5},{3,4},{4,3},{5,2},{6,1},{7,0},{8,15},{9,14},{10,... | collective-permute-start | bytes 196616 | tf_op jit(solution)/shard_map/ppermute | solution.py:36
  25.0 5.7 %collective-permute-start.10 = (bf16[256,128]{1,0:T(8,128)(2,1)S(1)}, bf16[256,128]{1,0:T(8,128)(2,1)S(1)}, u32[]{:S(2)}, u32[]{:S(2)}) collective-permute-start(bf16[256,128]{1,0:T(8,128)(2,1)S(1)} %collective-permute-done.7), channel_id=1, source_target_pairs={{0,3},{1,4},{2,7},{3,0},{4,1},{5,6},{6,5},{7,2},{8,13},{9,10},{10,... | collective-permute-start | bytes 196616 | tf_op jit(solution)/shard_map/ppermute | solution.py:36
  25.5 5.3 %collective-permute-start.9 = (bf16[256,128]{1,0:T(8,128)(2,1)S(1)}, bf16[256,128]{1,0:T(8,128)(2,1)S(1)}, u32[]{:S(2)}, u32[]{:S(2)}) collective-permute-start(bf16[256,128]{1,0:T(8,128)(2,1)S(1)} %collective-permute-done.7), channel_id=1, source_target_pairs={{0,5},{1,2},{2,1},{3,6},{4,7},{5,0},{6,3},{7,4},{8,11},{9,12},{10,... | collective-permute-start | bytes 196616 | tf_op jit(solution)/shard_map/ppermute | solution.py:36
  28.0 4.5 %collective-permute-start.12 = (bf16[512,128]{1,0:T(8,128)(2,1)S(1)}, bf16[512,128]{1,0:T(8,128)(2,1)S(1)}, u32[]{:S(2)}, u32[]{:S(2)}) collective-permute-start(bf16[512,128]{1,0:T(8,128)(2,1)S(1)} %constant_dynamic-update-slice_fusion.9), channel_id=1, source_target_pairs={{0,5},{1,2},{2,1},{3,6},{4,7},{5,0},{6,3},{7,4},{8,11},{9,12},{10,... | collective-permute-start | bytes 393224 | tf_op jit(solution)/shard_map/ppermute | solution.py:36
  32.5 2.0 %collective-permute-start.13 = (bf16[2048,128]{1,0:T(8,128)(2,1)S(1)}, bf16[2048,128]{1,0:T(8,128)(2,1)S(1)}, u32[]{:S(2)}, u32[]{:S(2)}) collective-permute-start(bf16[2048,128]{1,0:T(8,128)(2,1)S(1)} %constant_dynamic-update-slice_fusion.11.hours_ref), channel_id=1, source_target_pairs={{0,1},{1,0},{2,3},{3,2},{4,5},{5,4},{6,7},{7,6},{8,9},{9,8},{10,11... | collective-permute-start | bytes 1572872 | tf_op jit(solution)/shard_map/ppermute | solution.py:36

commit v4 on v3

--- a/solution.py
+++ b/solution.py
@@ -36,28 +36,30 @@
     return Piece(None if piece.value is None else lax.ppermute(piece.value, "col", pairs), masks)
 
 
-def gather(size, block, copy, early=(), late=lambda _: []):
+def gather(size, block, copy, sent, order, early, late=None, patient=False):
     exchange = functools.partial(swap, size)
     near, next_, far, *farther = [2 << b | 1 for b in range(size.bit_length() - 2)]
     one, other, both = (near, next_), (next_, near), near ^ next_ ^ 1
 
-    def wait(piece, others):
-        if len(others) and piece.value is not None:
-            piece.value, others = lax.optimization_barrier((piece.value, others))
-        return others
-
-    mine = [Piece(value, [[0], [0]]) for value in (block, copy)]
+    def wait(piece, values):
+        if piece.value is not None:
+            piece.value, values = lax.optimization_barrier((piece.value, values))
+        return values
+
+    block, copy, sent = (Piece(value, [[0], [0]]) for value in (block, copy, sent))
     for bits in farther[::-1]:
-        mine = [join(piece, exchange(piece, bits)) for piece in mine]
-    from_far = exchange(mine[0], far)
-    came = exchange(mine[1], *one)
-    ours = join(mine[1], came)
+        block, copy, sent = (join(piece, exchange(piece, bits)) for piece in (block, copy, sent))
+    from_far = exchange(block, far)
+    ours = join(copy, exchange(sent, *one))
     beside = exchange(ours, *other)
-    early = wait(from_far, [ours.value, *early])[1:]
-    beyond = [exchange(from_far, *other), exchange(from_far, *one), exchange(from_far, both)]
-    late = wait(beyond[-1], late(from_far.value))
-    same = join(from_far, ours, *beyond, beside)
-    return same, exchange(same, 1), early, late
+    early, *_ = wait(from_far, [early, ours.value] if patient else [early])
+    third, second, first = exchange(from_far, *other), exchange(from_far, *one), exchange(from_far, both)
+    if late is not None:
+        late = wait(first, late(from_far.value))
+    parts = dict(ours=ours, beside=beside, far=from_far, first=first, second=second, third=third)
+    gathered = join(*(parts[name] for name in order))
+    gathered.head = join(*(parts[name] for name in order[:3]))
+    return gathered, early, late
 
 
 def call(kernel, name, outs, specs, flops, *args, scratch=(), vmem=24):
@@ -105,7 +107,7 @@
         first = jnp.where(apart == jnp.where(odd == 0, mask_even, mask_odd), slot * rows, first)
     place = first + where_ref[1:]
     reflectance = reflectance_ref[:, :1]
-    step = 384
+    step = 256
     for j in range(0, count, step):
         width = min(step, count - j)
         position = lax.broadcasted_iota(jnp.int32, (width, place.shape[1]), 0) + j
@@ -124,25 +126,51 @@
     out_ref[...] = (base_ref[...] + part).astype(out_ref.dtype)
 
 
-def direct_kernel(first_ref, second_ref, sky_first_ref, sky_second_ref, hours_ref, out_ref, hours_out):
-    hours_out[...] = hours_ref[...]
+def copy_kernel(in_ref, out_ref):
+    out_ref[...] = in_ref[...]
+
+
+def direct_kernel(first_ref, second_ref, sky_first_ref, sky_second_ref, out_ref):
     out = jnp.dot(first_ref[...], sky_first_ref[...], preferred_element_type=jnp.float32)
     out_ref[...] = out + jnp.dot(second_ref[...], sky_second_ref[...], preferred_element_type=jnp.float32)
 
 
+def owners(masks, me):
+    odd = parity(me)
+    return [me ^ jnp.where(odd == 0, mask_even, mask_odd) for mask_even, mask_odd in zip(*masks)]
+
+
+def select_kernel(masks, me_ref, factors_ref, out_ref):
+    patches = out_ref.shape[0]
+    for slot, owner in enumerate(owners(masks, me_ref[0])):
+        columns = factors_ref[:, pl.ds(pl.multiple_of(owner * patches, patches), patches)]
+        out_ref[:, slot * patches : (slot + 1) * patches] = columns
+
+
 def bounce_kernel(masks, me_ref, base_ref, factors_ref, hours_ref, out_ref):
-    me = me_ref[0]
-    odd = parity(me)
     total = base_ref[...]
     patches = out_ref.shape[0]
-    for slot, (mask_even, mask_odd) in enumerate(zip(*masks)):
-        owner = me ^ jnp.where(odd == 0, mask_even, mask_odd)
+    for slot, owner in enumerate(owners(masks, me_ref[0])):
         total += jnp.dot(
             factors_ref[:, pl.ds(pl.multiple_of(owner * patches, patches), patches)],
             hours_ref[slot * patches : (slot + 1) * patches, :],
             preferred_element_type=jnp.float32,
         )
-    out_ref[...] = total.astype(out_ref.dtype)
+    out_ref[...] = total
+
+
+def head_kernel(factors_ref, hours_ref, out_ref):
+    count = hours_ref.shape[0]
+    out_ref[...] = jnp.dot(factors_ref[:, :count], hours_ref[...], preferred_element_type=jnp.float32)
+
+
+def tail_kernel(start, base_ref, factors_ref, hours_ref, out_ref):
+    part = jnp.dot(factors_ref[:, start:], hours_ref[start:, :], preferred_element_type=jnp.float32)
+    out_ref[...] = base_ref[...] + part
+
+
+def sum_kernel(a_ref, b_ref, out_ref):
+    out_ref[...] = (a_ref[...] + b_ref[...]).astype(out_ref.dtype)
 
 
 def shards(size, view_factors, direct_coeff, material, albedo, sky_matrix, sky_order):
@@ -170,12 +198,10 @@
             pltpu.SemaphoreType.DMA((5,)),
         ],
     )
-    same, across, _, _ = gather(size, None, None)
-
-    def permute(piece, name, start=None):
+    def permute(masks, name, start=None):
         place = where if start is None else lax.optimization_barrier((where, start))[0]
         return call(
-            functools.partial(permute_kernel, piece.masks, rows),
+            functools.partial(permute_kernel, masks, rows),
             name,
             (jax.ShapeDtypeStruct((patches, span), jnp.bfloat16),) * 2,
             [SCALARS] + [WHOLE] * 3,
@@ -186,42 +212,56 @@
             direct_coeff,
         )
 
-    late = functools.partial(permute, across, "permute_across")
-    same, across, first, second = gather(size, sky_matrix, sky, permute(same, "permute_same"), late)
+    order = ("far", "ours", "third", "second", "first", "beside")
+    plan, _, _ = gather(size, None, None, None, order, [])
+    first = permute(plan.masks, "permute_same")
+    late = functools.partial(permute, swap(size, plan, 1).masks, "permute_across")
+    same, first, second = gather(size, sky_matrix, sky, sky_matrix, order, first, late, patient=True)
+    across = swap(size, same, 1)
 
     flat = jax.ShapeDtypeStruct((patches, hours), jnp.float32)
     short = jax.ShapeDtypeStruct((patches, hours), jnp.bfloat16)
     flops = 2 * patches * span * hours
     part = call(dot_kernel, "hours_same", flat, [WHOLE] * 2, flops, first[1], same.value)
     own = call(add_dot_kernel, "hours_all", short, [WHOLE] * 3, flops, part, second[1], across.value)
-    total, copy = call(
-        direct_kernel,
-        "direct",
-        (flat, pltpu.VMEM(own.shape, own.dtype)),
-        [WHOLE] * 5,
-        2 * flops,
-        first[0],
-        second[0],
+    copy = call(copy_kernel, "copy", pltpu.VMEM(own.shape, own.dtype), [WHOLE], 10**8, own)
+    total = call(
+        direct_kernel, "direct", flat, [WHOLE] * 4, 2 * 10**9, first[0], second[0], same.value, across.value
+    )
+
+    order = ("ours", "beside", "far", "third", "second", "first")
+    plan, _, _ = gather(size, None, None, None, order, [])
+    factors, _ = lax.optimization_barrier((view_factors, copy))
+    chosen = call(
+        functools.partial(select_kernel, swap(size, plan, 1).masks),
+        "select",
+        pltpu.VMEM((patches, size // 2 * patches), view_factors.dtype),
+        [SCALARS, WHOLE],
+        0,
+        index,
+        factors,
+    )
+    theirs = swap(size, Piece(chosen, [[0], [0]]), 1).value
+    same, total, _ = gather(size, own, copy, copy, order, total)
+    head = same.head.value
+    flops = 2 * patches * size // 2 * patches * hours
+    partial = call(head_kernel, "partner_head", flat, [WHOLE] * 2, flops, theirs, head)
+    partial = call(
+        functools.partial(tail_kernel, head.shape[0]), "partner", flat, [WHOLE] * 3, flops, partial, theirs, same.value
+    )
+    partial = swap(size, Piece(partial, [[0], [0]]), 1).value
+    total = call(
+        functools.partial(bounce_kernel, same.masks),
+        "bounce_same",
+        flat,
+        [SCALARS] + [WHOLE] * 3,
+        flops,
+        index,
+        total,
+        view_factors,
         same.value,
-        across.value,
-        own,
-    )
-    same, across, (total,), _ = gather(size, own, copy, [total])
-
-    def bounce(name, base, piece, out):
-        return call(
-            functools.partial(bounce_kernel, piece.masks),
-            name,
-            out,
-            [SCALARS] + [WHOLE] * 3,
-            2 * patches * piece.value.size,
-            index,
-            base,
-            view_factors,
-            piece.value,
-        )
-
-    return bounce("bounce_across", bounce("bounce_same", total, same, flat), across, short)
+    )
+    return call(sum_kernel, "sum", short, [WHOLE] * 2, 0, total, partial)
 
 
 def solution(mesh):

time: 35.7 us -> 32.9 us (0.922)
  waiting for transfers between devices: 12.6 us -> 7.75 us
  starting transfers between devices: 14.6 us -> 16.9 us
    ppermute x14 -> x15, waiting for transfers between devices: 12.6 us -> 7.75 us  [swap(): lax.ppermute(piece.value, 'col', pairs)]
    ppermute x14 -> x15, starting transfers between devices: 14.6 us -> 16.9 us  [swap(): lax.ppermute(piece.value, 'col', pairs)]
    pallas_call x8 -> x12, Pallas kernels: 7.94 us -> 7.75 us  [call(): pl.pallas_call(kernel, scratch_shapes=scratch, out_shape=outs, in_specs=s...]
  transfers between devices with their start and end apart: 14 -> 15, of which waited for: 7 -> 7; matrix products, arithmetic and copies ran while one was open for 0% -> 1% of each run, Pallas kernels for 19% -> 19%
where the time goes in v4:
time: 32.9 us; the launch traced here: 32.8 us
  starting transfers between devices  16.9 us (51%)
  Pallas kernels  7.75 us (24%)
  waiting for transfers between devices  7.75 us (24%)
    ppermute x15, starting transfers between devices, swap(): lax.ppermute(piece.value, 'col', pairs)  16.9 us
    ppermute x15, waiting for transfers between devices, swap(): lax.ppermute(piece.value, 'col', pairs)  7.75 us
    pallas_call x12, Pallas kernels, call(): pl.pallas_call(kernel, scratch_shapes=scratch, out_shape=outs, in_specs=s...  7.75 us
  transfers between devices with their start and end apart: 15, of which 7 were waited for; matrix products, arithmetic and copies ran while one was open for 1% of the time, Pallas kernels for 19%

profile of v4, /device:TPU:0, one launch (start us, length us, event | category | flops | bytes accessed | tf_op | source)
XLA Modules:
  0.0 32.8 jit_solution(12135492393632399321)
XLA Ops:
  0.0 3.5 %collective-permute-start = (bf16[144,128]{1,0:T(8,128)(2,1)}, bf16[144,128]{1,0:T(8,128)(2,1)S(1)}, u32[]{:S(2)}, u32[]{:S(2)}) collective-permute-start(bf16[144,128]{1,0:T(8,128)(2,1)} %sky_in.1), channel_id=1, source_target_pairs={{0,9},{1,8},{2,11},{3,10},{4,13},{5,12},{6,15},{7,14},{8,1},{9,0},... | collective-permute-start | bytes 110600 | tf_op jit(solution)/shard_map/ppermute | solution.py:36
  3.5 1.8 %collective-permute-start.1 = (bf16[144,128]{1,0:T(8,128)(2,1)}, bf16[144,128]{1,0:T(8,128)(2,1)S(1)}, u32[]{:S(2)}, u32[]{:S(2)}) collective-permute-start(bf16[144,128]{1,0:T(8,128)(2,1)} %sky_in.1), channel_id=1, source_target_pairs={{0,3},{1,4},{2,7},{3,0},{4,1},{5,6},{6,5},{7,2},{8,13},{9,10},{10,... | collective-permute-start | bytes 110600 | tf_op jit(solution)/shard_map/ppermute | solution.py:36
  5.3 1.4 %prepare.1 = (bf16[144,128]{1,0:T(8,128)(2,1)S(1)}, bf16[256,2304]{1,0:T(8,128)(2,1)S(1)}, f32[256,128]{1,0:T(8,128)S(1)}, s32[2,2304]{1,0:T(2,128)S(1)}) custom-call(f32[16]{0:T(128)} %albedo_in.1, s32[256]{0:T(256)} %material_in.1, s32[2304]{0:T(1024)} %order_in.1, bf16[144,128]{1,0:T(8,128)(2,1)} %sky_in.1, bf16[256,2304]{1,0:T(8,128)(2,1)} %direct_in.1, ...), custom_call_target="tpu_custom_call" | custom-call | flops 1000000000 | tf_op jit(solution)/shard_map/prepare/pallas_call | solution.py:66
  6.7 1.7 %permute_same.1 = (bf16[256,1152]{1,0:T(8,128)(2,1)S(1)}, bf16[256,1152]{1,0:T(8,128)(2,1)S(1)}) custom-call(s32[1]{0:T(128)} %bitcast.me_ref, s32[2,2304]{1,0:T(2,128)S(1)} %get-tuple-element.31.where_ref, f32[256,128]{1,0:T(8,128)S(1)} %get-tuple-element.24.reflectance_ref, bf16[256,2304]{1,0:T(8,128)(2,1)S(1)} %get-tuple-element.25.direct_ref), custom_call_target="tpu_custom_call" | custom-call | flops 1358954496 | tf_op jit(solution)/shard_map/permute_same/pallas_call | solution.py:66
  8.4 1.1 %collective-permute-start.5 = (bf16[288,128]{1,0:T(8,128)(2,1)S(1)}, bf16[288,128]{1,0:T(8,128)(2,1)S(1)}, u32[]{:S(2)}, u32[]{:S(2)}) collective-permute-start(bf16[288,128]{1,0:T(8,128)(2,1)S(1)} %constant_dynamic-update-slice_fusion), channel_id=1, source_target_pairs={{0,5},{1,2},{2,1},{3,6},{4,7},{5,0},{6,3},{7,4},{8,11},{9,12},{10,... | collective-permute-start | bytes 221192 | tf_op jit(solution)/shard_map/ppermute | solution.py:36
  9.5 0.7 %collective-permute-start.4 = (bf16[144,128]{1,0:T(8,128)(2,1)S(1)}, bf16[144,128]{1,0:T(8,128)(2,1)S(1)}, u32[]{:S(2)}, u32[]{:S(2)}) collective-permute-start(bf16[144,128]{1,0:T(8,128)(2,1)S(1)} %collective-permute-done), channel_id=1, source_target_pairs={{0,7},{1,6},{2,5},{3,4},{4,3},{5,2},{6,1},{7,0},{8,15},{9,14},{10,... | collective-permute-start | bytes 110600 | tf_op jit(solution)/shard_map/ppermute | solution.py:36
  10.2 1.5 %collective-permute-start.3 = (bf16[144,128]{1,0:T(8,128)(2,1)S(1)}, bf16[144,128]{1,0:T(8,128)(2,1)S(1)}, u32[]{:S(2)}, u32[]{:S(2)}) collective-permute-start(bf16[144,128]{1,0:T(8,128)(2,1)S(1)} %collective-permute-done), channel_id=1, source_target_pairs={{0,3},{1,4},{2,7},{3,0},{4,1},{5,6},{6,5},{7,2},{8,13},{9,10},{10,... | collective-permute-start | bytes 110600 | tf_op jit(solution)/shard_map/ppermute | solution.py:36
  11.7 1.3 %collective-permute-start.2 = (bf16[144,128]{1,0:T(8,128)(2,1)S(1)}, bf16[144,128]{1,0:T(8,128)(2,1)S(1)}, u32[]{:S(2)}, u32[]{:S(2)}) collective-permute-start(bf16[144,128]{1,0:T(8,128)(2,1)S(1)} %collective-permute-done), channel_id=1, source_target_pairs={{0,5},{1,2},{2,1},{3,6},{4,7},{5,0},{6,3},{7,4},{8,11},{9,12},{10,... | collective-permute-start | bytes 110600 | tf_op jit(solution)/shard_map/ppermute | solution.py:36
  13.0 1.7 %permute_across.1 = (bf16[256,1152]{1,0:T(8,128)(2,1)S(1)}, bf16[256,1152]{1,0:T(8,128)(2,1)S(1)}) custom-call(s32[1]{0:T(128)} %bitcast.me_ref, s32[2,2304]{1,0:T(2,128)S(1)} %get-tuple-element.31.where_ref, f32[256,128]{1,0:T(8,128)S(1)} %get-tuple-element.24.reflectance_ref, bf16[256,2304]{1,0:T(8,128)(2,1)S(1)} %get-tuple-element.25.direct_ref), custom_call_target="tpu_custom_call" | custom-call | flops 1358954496 | tf_op jit(solution)/shard_map/permute_across/pallas_call | solution.py:66
  15.8 1.1 %collective-permute-done.6.b_ref.sky_second_ref = bf16[1152,128]{1,0:T(8,128)(2,1)S(1)} collective-permute-done((bf16[1152,128]{1,0:T(8,128)(2,1)S(1)}, bf16[1152,128]{1,0:T(8,128)(2,1)S(1)}, u32[]{:S(2)}, u32[]{:S(2)}) %collective-permute-start.6) | collective-permute-done | bytes 294944 | tf_op jit(solution)/shard_map/ppermute | solution.py:36
  17.2 0.7 %collective-permute-start.7 = (bf16[256,128]{1,0:T(8,128)(2,1)S(1)}, bf16[256,128]{1,0:T(8,128)(2,1)S(1)}, u32[]{:S(2)}, u32[]{:S(2)}) collective-permute-start(bf16[256,128]{1,0:T(8,128)(2,1)S(1)} %hours_all.1.in_ref), channel_id=1, source_target_pairs={{0,9},{1,8},{2,11},{3,10},{4,13},{5,12},{6,15},{7,14},{8,1},{9,0},... | collective-permute-start | bytes 196616 | tf_op jit(solution)/shard_map/ppermute | solution.py:36
  17.9 1.2 %collective-permute-start.8 = (bf16[256,128]{1,0:T(8,128)(2,1)S(1)}, bf16[256,128]{1,0:T(8,128)(2,1)S(1)}, u32[]{:S(2)}, u32[]{:S(2)}) collective-permute-start(bf16[256,128]{1,0:T(8,128)(2,1)S(1)} %copy.21), channel_id=1, source_target_pairs={{0,3},{1,4},{2,7},{3,0},{4,1},{5,6},{6,5},{7,2},{8,13},{9,10},{10,... | collective-permute-start | bytes 196616 | tf_op jit(solution)/shard_map/ppermute | solution.py:36
  19.5 0.5 %direct.1.base_ref = f32[256,128]{1,0:T(8,128)S(1)} custom-call(bf16[256,1152]{1,0:T(8,128)(2,1)S(1)} %get-tuple-element.36.first_ref, bf16[256,1152]{1,0:T(8,128)(2,1)S(1)} %get-tuple-element.37.second_ref, bf16[1152,128]{1,0:T(8,128)(2,1)S(1)} %constant_dynamic-update-slice_fusion.2.b_ref.sky_first_ref, ...), custom_call_target="tpu_custom_call" | custom-call | flops 2000000000 | tf_op jit(solution)/shard_map/direct/pallas_call | solution.py:66
  19.9 1.7 %collective-permute-done.8 = bf16[256,128]{1,0:T(8,128)(2,1)S(1)} collective-permute-done((bf16[256,128]{1,0:T(8,128)(2,1)S(1)}, bf16[256,128]{1,0:T(8,128)(2,1)S(1)}, u32[]{:S(2)}, u32[]{:S(2)}) %collective-permute-start.8) | collective-permute-done | bytes 65568 | tf_op jit(solution)/shard_map/ppermute | solution.py:36
  21.6 1.3 %collective-permute-start.9 = (bf16[512,128]{1,0:T(8,128)(2,1)S(1)}, bf16[512,128]{1,0:T(8,128)(2,1)S(1)}, u32[]{:S(2)}, u32[]{:S(2)}) collective-permute-start(bf16[512,128]{1,0:T(8,128)(2,1)S(1)} %pad_maximum_fusion.1), channel_id=1, source_target_pairs={{0,5},{1,2},{2,1},{3,6},{4,7},{5,0},{6,3},{7,4},{8,11},{9,12},{10,... | collective-permute-start | bytes 393224 | tf_op jit(solution)/shard_map/ppermute | solution.py:36
  23.0 0.6 %collective-permute-done.7 = bf16[256,128]{1,0:T(8,128)(2,1)S(1)} collective-permute-done((bf16[256,128]{1,0:T(8,128)(2,1)S(1)}, bf16[256,128]{1,0:T(8,128)(2,1)S(1)}, u32[]{:S(2)}, u32[]{:S(2)}) %collective-permute-start.7) | collective-permute-done | bytes 65568 | tf_op jit(solution)/shard_map/ppermute | solution.py:36
  23.5 1.1 %collective-permute-start.12 = (bf16[256,128]{1,0:T(8,128)(2,1)S(1)}, bf16[256,128]{1,0:T(8,128)(2,1)S(1)}, u32[]{:S(2)}, u32[]{:S(2)}) collective-permute-start(bf16[256,128]{1,0:T(8,128)(2,1)S(1)} %collective-permute-done.7), channel_id=1, source_target_pairs={{0,7},{1,6},{2,5},{3,4},{4,3},{5,2},{6,1},{7,0},{8,15},{9,14},{10,... | collective-permute-start | bytes 196616 | tf_op jit(solution)/shard_map/ppermute | solution.py:36
  24.6 0.7 %collective-permute-start.11 = (bf16[256,128]{1,0:T(8,128)(2,1)S(1)}, bf16[256,128]{1,0:T(8,128)(2,1)S(1)}, u32[]{:S(2)}, u32[]{:S(2)}) collective-permute-start(bf16[256,128]{1,0:T(8,128)(2,1)S(1)} %collective-permute-done.7), channel_id=1, source_target_pairs={{0,3},{1,4},{2,7},{3,0},{4,1},{5,6},{6,5},{7,2},{8,13},{9,10},{10,... | collective-permute-start | bytes 196616 | tf_op jit(solution)/shard_map/ppermute | solution.py:36
  25.3 1.3 %collective-permute-start.10 = (bf16[256,128]{1,0:T(8,128)(2,1)S(1)}, bf16[256,128]{1,0:T(8,128)(2,1)S(1)}, u32[]{:S(2)}, u32[]{:S(2)}) collective-permute-start(bf16[256,128]{1,0:T(8,128)(2,1)S(1)} %collective-permute-done.7), channel_id=1, source_target_pairs={{0,5},{1,2},{2,1},{3,6},{4,7},{5,0},{6,3},{7,4},{8,11},{9,12},{10,... | collective-permute-start | bytes 196616 | tf_op jit(solution)/shard_map/ppermute | solution.py:36
  26.6 3.1 %collective-permute-done.10 = bf16[256,128]{1,0:T(8,128)(2,1)S(1)} collective-permute-done((bf16[256,128]{1,0:T(8,128)(2,1)S(1)}, bf16[256,128]{1,0:T(8,128)(2,1)S(1)}, u32[]{:S(2)}, u32[]{:S(2)}) %collective-permute-start.10) | collective-permute-done | bytes 65568 | tf_op jit(solution)/shard_map/ppermute | solution.py:36
  29.7 0.4 %collective-permute-done.11 = bf16[256,128]{1,0:T(8,128)(2,1)S(1)} collective-permute-done((bf16[256,128]{1,0:T(8,128)(2,1)S(1)}, bf16[256,128]{1,0:T(8,128)(2,1)S(1)}, u32[]{:S(2)}, u32[]{:S(2)}) %collective-permute-start.11) | collective-permute-done | bytes 65568 | tf_op jit(solution)/shard_map/ppermute | solution.py:36
  30.9 0.4 %bounce_same.1.a_ref = f32[256,128]{1,0:T(8,128)S(1)} custom-call(s32[1]{0:T(128)} %bitcast.me_ref, f32[256,128]{1,0:T(8,128)S(1)} %direct.1.base_ref, bf16[256,4096]{1,0:T(8,128)(2,1)S(1)} %copy-done, bf16[2048,128]{1,0:T(8,128)(2,1)S(1)} %constant_dynamic-update-slice_fusion.9.hours_ref), custom_call_target="tpu_custom_call" | custom-call | flops 134217728 | tf_op jit(solution)/shard_map/bounce_same/pallas_call | solution.py:66
  31.4 0.8 %collective-permute-done.14.b_ref = f32[256,128]{1,0:T(8,128)S(1)} collective-permute-done((f32[256,128]{1,0:T(8,128)S(1)}, f32[256,128]{1,0:T(8,128)S(1)}, u32[]{:S(2)}, u32[]{:S(2)}) %collective-permute-start.14) | collective-permute-done | bytes 131104 | tf_op jit(solution)/shard_map/ppermute | solution.py:36
  32.1 0.6 %sum.1 = bf16[256,128]{1,0:T(8,128)(2,1)} custom-call(f32[256,128]{1,0:T(8,128)S(1)} %bounce_same.1.a_ref, f32[256,128]{1,0:T(8,128)S(1)} %collective-permute-done.14.b_ref), custom_call_target="tpu_custom_call" | custom-call | tf_op jit(solution)/shard_map/sum/pallas_call | solution.py:66
  (38 shorter events, 2.5 us)
Async XLA Ops:
  0.0 9.5 %collective-permute-start = (bf16[144,128]{1,0:T(8,128)(2,1)}, bf16[144,128]{1,0:T(8,128)(2,1)S(1)}, u32[]{:S(2)}, u32[]{:S(2)}) collective-permute-start(bf16[144,128]{1,0:T(8,128)(2,1)} %sky_in.1), channel_id=1, source_target_pairs={{0,9},{1,8},{2,11},{3,10},{4,13},{5,12},{6,15},{7,14},{8,1},{9,0},... | collective-permute-start | bytes 110600 | tf_op jit(solution)/shard_map/ppermute | solution.py:36
  3.5 4.9 %collective-permute-start.1 = (bf16[144,128]{1,0:T(8,128)(2,1)}, bf16[144,128]{1,0:T(8,128)(2,1)S(1)}, u32[]{:S(2)}, u32[]{:S(2)}) collective-permute-start(bf16[144,128]{1,0:T(8,128)(2,1)} %sky_in.1), channel_id=1, source_target_pairs={{0,3},{1,4},{2,7},{3,0},{4,1},{5,6},{6,5},{7,2},{8,13},{9,10},{10,... | collective-permute-start | bytes 110600 | tf_op jit(solution)/shard_map/ppermute | solution.py:36
  8.4 6.7 %collective-permute-start.5 = (bf16[288,128]{1,0:T(8,128)(2,1)S(1)}, bf16[288,128]{1,0:T(8,128)(2,1)S(1)}, u32[]{:S(2)}, u32[]{:S(2)}) collective-permute-start(bf16[288,128]{1,0:T(8,128)(2,1)S(1)} %constant_dynamic-update-slice_fusion), channel_id=1, source_target_pairs={{0,5},{1,2},{2,1},{3,6},{4,7},{5,0},{6,3},{7,4},{8,11},{9,12},{10,... | collective-permute-start | bytes 221192 | tf_op jit(solution)/shard_map/ppermute | solution.py:36
  9.5 5.6 %collective-permute-start.4 = (bf16[144,128]{1,0:T(8,128)(2,1)S(1)}, bf16[144,128]{1,0:T(8,128)(2,1)S(1)}, u32[]{:S(2)}, u32[]{:S(2)}) collective-permute-start(bf16[144,128]{1,0:T(8,128)(2,1)S(1)} %collective-permute-done), channel_id=1, source_target_pairs={{0,7},{1,6},{2,5},{3,4},{4,3},{5,2},{6,1},{7,0},{8,15},{9,14},{10,... | collective-permute-start | bytes 110600 | tf_op jit(solution)/shard_map/ppermute | solution.py:36
  10.2 4.9 %collective-permute-start.3 = (bf16[144,128]{1,0:T(8,128)(2,1)S(1)}, bf16[144,128]{1,0:T(8,128)(2,1)S(1)}, u32[]{:S(2)}, u32[]{:S(2)}) collective-permute-start(bf16[144,128]{1,0:T(8,128)(2,1)S(1)} %collective-permute-done), channel_id=1, source_target_pairs={{0,3},{1,4},{2,7},{3,0},{4,1},{5,6},{6,5},{7,2},{8,13},{9,10},{10,... | collective-permute-start | bytes 110600 | tf_op jit(solution)/shard_map/ppermute | solution.py:36
  11.7 3.4 %collective-permute-start.2 = (bf16[144,128]{1,0:T(8,128)(2,1)S(1)}, bf16[144,128]{1,0:T(8,128)(2,1)S(1)}, u32[]{:S(2)}, u32[]{:S(2)}) collective-permute-start(bf16[144,128]{1,0:T(8,128)(2,1)S(1)} %collective-permute-done), channel_id=1, source_target_pairs={{0,5},{1,2},{2,1},{3,6},{4,7},{5,0},{6,3},{7,4},{8,11},{9,12},{10,... | collective-permute-start | bytes 110600 | tf_op jit(solution)/shard_map/ppermute | solution.py:36
  15.2 4.0 %copy-start = (bf16[256,4096]{1,0:T(8,128)(2,1)S(1)}, bf16[256,4096]{1,0:T(8,128)(2,1)}, u32[]{:S(2)}) copy-start(bf16[256,4096]{1,0:T(8,128)(2,1)} %factors_ref.2) | copy-start | bytes 6291460
  15.2 1.6 %collective-permute-start.6 = (bf16[1152,128]{1,0:T(8,128)(2,1)S(1)}, bf16[1152,128]{1,0:T(8,128)(2,1)S(1)}, u32[]{:S(2)}, u32[]{:S(2)}) collective-permute-start(bf16[1152,128]{1,0:T(8,128)(2,1)S(1)} %constant_dynamic-update-slice_fusion.2.b_ref.sky_first_ref), channel_id=1, source_target_pairs={{0,1},{1,0},{2,3},{3,2},{4,5},{5,4},{6,7},{7,6},{8,9},{9,8},{10,11... | collective-permute-start | bytes 884744 | tf_op jit(solution)/shard_map/ppermute | solution.py:36
  17.2 6.3 %collective-permute-start.7 = (bf16[256,128]{1,0:T(8,128)(2,1)S(1)}, bf16[256,128]{1,0:T(8,128)(2,1)S(1)}, u32[]{:S(2)}, u32[]{:S(2)}) collective-permute-start(bf16[256,128]{1,0:T(8,128)(2,1)S(1)} %hours_all.1.in_ref), channel_id=1, source_target_pairs={{0,9},{1,8},{2,11},{3,10},{4,13},{5,12},{6,15},{7,14},{8,1},{9,0},... | collective-permute-start | bytes 196616 | tf_op jit(solution)/shard_map/ppermute | solution.py:36
  17.9 3.7 %collective-permute-start.8 = (bf16[256,128]{1,0:T(8,128)(2,1)S(1)}, bf16[256,128]{1,0:T(8,128)(2,1)S(1)}, u32[]{:S(2)}, u32[]{:S(2)}) collective-permute-start(bf16[256,128]{1,0:T(8,128)(2,1)S(1)} %copy.21), channel_id=1, source_target_pairs={{0,3},{1,4},{2,7},{3,0},{4,1},{5,6},{6,5},{7,2},{8,13},{9,10},{10,... | collective-permute-start | bytes 196616 | tf_op jit(solution)/shard_map/ppermute | solution.py:36
  19.3 10.9 %collective-permute-start.13 = (bf16[256,2048]{1,0:T(8,128)(2,1)S(1)}, bf16[256,2048]{1,0:T(8,128)(2,1)S(1)}, u32[]{:S(2)}, u32[]{:S(2)}) collective-permute-start(bf16[256,2048]{1,0:T(8,128)(2,1)S(1)} %select.1), channel_id=1, source_target_pairs={{0,1},{1,0},{2,3},{3,2},{4,5},{5,4},{6,7},{7,6},{8,9},{9,8},{10,11... | collective-permute-start | bytes 3145736 | tf_op jit(solution)/shard_map/ppermute | solution.py:36
  21.6 5.0 %collective-permute-start.9 = (bf16[512,128]{1,0:T(8,128)(2,1)S(1)}, bf16[512,128]{1,0:T(8,128)(2,1)S(1)}, u32[]{:S(2)}, u32[]{:S(2)}) collective-permute-start(bf16[512,128]{1,0:T(8,128)(2,1)S(1)} %pad_maximum_fusion.1), channel_id=1, source_target_pairs={{0,5},{1,2},{2,1},{3,6},{4,7},{5,0},{6,3},{7,4},{8,11},{9,12},{10,... | collective-permute-start | bytes 393224 | tf_op jit(solution)/shard_map/ppermute | solution.py:36
  23.5 6.6 %collective-permute-start.12 = (bf16[256,128]{1,0:T(8,128)(2,1)S(1)}, bf16[256,128]{1,0:T(8,128)(2,1)S(1)}, u32[]{:S(2)}, u32[]{:S(2)}) collective-permute-start(bf16[256,128]{1,0:T(8,128)(2,1)S(1)} %collective-permute-done.7), channel_id=1, source_target_pairs={{0,7},{1,6},{2,5},{3,4},{4,3},{5,2},{6,1},{7,0},{8,15},{9,14},{10,... | collective-permute-start | bytes 196616 | tf_op jit(solution)/shard_map/ppermute | solution.py:36
  24.6 5.4 %collective-permute-start.11 = (bf16[256,128]{1,0:T(8,128)(2,1)S(1)}, bf16[256,128]{1,0:T(8,128)(2,1)S(1)}, u32[]{:S(2)}, u32[]{:S(2)}) collective-permute-start(bf16[256,128]{1,0:T(8,128)(2,1)S(1)} %collective-permute-done.7), channel_id=1, source_target_pairs={{0,3},{1,4},{2,7},{3,0},{4,1},{5,6},{6,5},{7,2},{8,13},{9,10},{10,... | collective-permute-start | bytes 196616 | tf_op jit(solution)/shard_map/ppermute | solution.py:36
  25.3 4.4 %collective-permute-start.10 = (bf16[256,128]{1,0:T(8,128)(2,1)S(1)}, bf16[256,128]{1,0:T(8,128)(2,1)S(1)}, u32[]{:S(2)}, u32[]{:S(2)}) collective-permute-start(bf16[256,128]{1,0:T(8,128)(2,1)S(1)} %collective-permute-done.7), channel_id=1, source_target_pairs={{0,5},{1,2},{2,1},{3,6},{4,7},{5,0},{6,3},{7,4},{8,11},{9,12},{10,... | collective-permute-start | bytes 196616 | tf_op jit(solution)/shard_map/ppermute | solution.py:36
  30.7 1.4 %collective-permute-start.14 = (f32[256,128]{1,0:T(8,128)S(1)}, f32[256,128]{1,0:T(8,128)S(1)}, u32[]{:S(2)}, u32[]{:S(2)}) collective-permute-start(f32[256,128]{1,0:T(8,128)S(1)} %partner.1), channel_id=1, source_target_pairs={{0,1},{1,0},{2,3},{3,2},{4,5},{5,4},{6,7},{7,6},{8,9},{9,8},{10,11... | collective-permute-start | bytes 393224 | tf_op jit(solution)/shard_map/ppermute | solution.py:36

commit v5 on v4

--- a/solution.py
+++ b/solution.py
@@ -54,12 +54,11 @@
     beside = exchange(ours, *other)
     early, *_ = wait(from_far, [early, ours.value] if patient else [early])
     third, second, first = exchange(from_far, *other), exchange(from_far, *one), exchange(from_far, both)
+    parts = dict(ours=ours, beside=beside, far=from_far, first=first, second=second, third=third)
     if late is not None:
-        late = wait(first, late(from_far.value))
-    parts = dict(ours=ours, beside=beside, far=from_far, first=first, second=second, third=third)
-    gathered = join(*(parts[name] for name in order))
-    gathered.head = join(*(parts[name] for name in order[:3]))
-    return gathered, early, late
+        name, work = late
+        late = wait(parts[name], work(parts))
+    return join(*(parts[name] for name in order)), early, late
 
 
 def call(kernel, name, outs, specs, flops, *args, scratch=(), vmem=24):
@@ -215,7 +214,8 @@
     order = ("far", "ours", "third", "second", "first", "beside")
     plan, _, _ = gather(size, None, None, None, order, [])
     first = permute(plan.masks, "permute_same")
-    late = functools.partial(permute, swap(size, plan, 1).masks, "permute_across")
+    masks = swap(size, plan, 1).masks
+    late = ("first", lambda parts: permute(masks, "permute_across", parts["far"].value))
     same, first, second = gather(size, sky_matrix, sky, sky_matrix, order, first, late, patient=True)
     across = swap(size, same, 1)
 
@@ -242,12 +242,17 @@
         factors,
     )
     theirs = swap(size, Piece(chosen, [[0], [0]]), 1).value
-    same, total, _ = gather(size, own, copy, copy, order, total)
-    head = same.head.value
     flops = 2 * patches * size // 2 * patches * hours
-    partial = call(head_kernel, "partner_head", flat, [WHOLE] * 2, flops, theirs, head)
+    head = []
+
+    def partner_head(parts):
+        head.append(join(*(parts[name] for name in order[:3])))
+        return call(head_kernel, "partner_head", flat, [WHOLE] * 2, 2 * 10**9, theirs, head[0].value)
+
+    same, total, partial = gather(size, own, copy, copy, order, total, ("second", partner_head))
+    start = head[0].value.shape[0]
     partial = call(
-        functools.partial(tail_kernel, head.shape[0]), "partner", flat, [WHOLE] * 3, flops, partial, theirs, same.value
+        functools.partial(tail_kernel, start), "partner", flat, [WHOLE] * 3, flops, partial, theirs, same.value
     )
     partial = swap(size, Piece(partial, [[0], [0]]), 1).value
     total = call(

time: 32.9 us -> 32.7 us (level)
  waiting for transfers between devices: 7.75 us -> 7.19 us
    ppermute x15, waiting for transfers between devices: 7.75 us -> 7.19 us  [swap(): lax.ppermute(piece.value, 'col', pairs)]
    ppermute x15, starting transfers between devices: 16.9 us -> 17.2 us  [swap(): lax.ppermute(piece.value, 'col', pairs)]
  transfers between devices with their start and end apart: 15 -> 15, of which waited for: 7 -> 6; matrix products, arithmetic and copies ran while one was open for 1% -> 1% of each run, Pallas kernels for 19% -> 20%
where the time goes in v5:
time: 32.7 us; the launch traced here: 32.6 us
  starting transfers between devices  17.2 us (53%)
  Pallas kernels  7.76 us (24%)
  waiting for transfers between devices  7.19 us (22%)
    ppermute x15, starting transfers between devices, swap(): lax.ppermute(piece.value, 'col', pairs)  17.2 us
    pallas_call x12, Pallas kernels, call(): pl.pallas_call(kernel, scratch_shapes=scratch, out_shape=outs, in_specs=s...  7.76 us
    ppermute x15, waiting for transfers between devices, swap(): lax.ppermute(piece.value, 'col', pairs)  7.19 us
  transfers between devices with their start and end apart: 15, of which 6 were waited for; matrix products, arithmetic and copies ran while one was open for 1% of the time, Pallas kernels for 20%

profile of v5, /device:TPU:0, one launch (start us, length us, event | category | flops | bytes accessed | tf_op | source)
XLA Modules:
  0.0 32.6 jit_solution(8145187323281417653)
XLA Ops:
  0.0 3.5 %collective-permute-start = (bf16[144,128]{1,0:T(8,128)(2,1)}, bf16[144,128]{1,0:T(8,128)(2,1)S(1)}, u32[]{:S(2)}, u32[]{:S(2)}) collective-permute-start(bf16[144,128]{1,0:T(8,128)(2,1)} %sky_in.1), channel_id=1, source_target_pairs={{0,9},{1,8},{2,11},{3,10},{4,13},{5,12},{6,15},{7,14},{8,1},{9,0},... | collective-permute-start | bytes 110600 | tf_op jit(solution)/shard_map/ppermute | solution.py:36
  3.5 1.8 %collective-permute-start.1 = (bf16[144,128]{1,0:T(8,128)(2,1)}, bf16[144,128]{1,0:T(8,128)(2,1)S(1)}, u32[]{:S(2)}, u32[]{:S(2)}) collective-permute-start(bf16[144,128]{1,0:T(8,128)(2,1)} %sky_in.1), channel_id=1, source_target_pairs={{0,3},{1,4},{2,7},{3,0},{4,1},{5,6},{6,5},{7,2},{8,13},{9,10},{10,... | collective-permute-start | bytes 110600 | tf_op jit(solution)/shard_map/ppermute | solution.py:36
  5.3 1.4 %prepare.1 = (bf16[144,128]{1,0:T(8,128)(2,1)S(1)}, bf16[256,2304]{1,0:T(8,128)(2,1)S(1)}, f32[256,128]{1,0:T(8,128)S(1)}, s32[2,2304]{1,0:T(2,128)S(1)}) custom-call(f32[16]{0:T(128)} %albedo_in.1, s32[256]{0:T(256)} %material_in.1, s32[2304]{0:T(1024)} %order_in.1, bf16[144,128]{1,0:T(8,128)(2,1)} %sky_in.1, bf16[256,2304]{1,0:T(8,128)(2,1)} %direct_in.1, ...), custom_call_target="tpu_custom_call" | custom-call | flops 1000000000 | tf_op jit(solution)/shard_map/prepare/pallas_call | solution.py:65
  6.7 1.7 %permute_same.1 = (bf16[256,1152]{1,0:T(8,128)(2,1)S(1)}, bf16[256,1152]{1,0:T(8,128)(2,1)S(1)}) custom-call(s32[1]{0:T(128)} %bitcast.me_ref, s32[2,2304]{1,0:T(2,128)S(1)} %get-tuple-element.33.where_ref, f32[256,128]{1,0:T(8,128)S(1)} %get-tuple-element.26.reflectance_ref, bf16[256,2304]{1,0:T(8,128)(2,1)S(1)} %get-tuple-element.27.direct_ref), custom_call_target="tpu_custom_call" | custom-call | flops 1358954496 | tf_op jit(solution)/shard_map/permute_same/pallas_call | solution.py:65
  8.4 1.1 %collective-permute-start.5 = (bf16[288,128]{1,0:T(8,128)(2,1)S(1)}, bf16[288,128]{1,0:T(8,128)(2,1)S(1)}, u32[]{:S(2)}, u32[]{:S(2)}) collective-permute-start(bf16[288,128]{1,0:T(8,128)(2,1)S(1)} %constant_dynamic-update-slice_fusion), channel_id=1, source_target_pairs={{0,5},{1,2},{2,1},{3,6},{4,7},{5,0},{6,3},{7,4},{8,11},{9,12},{10,... | collective-permute-start | bytes 221192 | tf_op jit(solution)/shard_map/ppermute | solution.py:36
  9.5 0.7 %collective-permute-start.4 = (bf16[144,128]{1,0:T(8,128)(2,1)S(1)}, bf16[144,128]{1,0:T(8,128)(2,1)S(1)}, u32[]{:S(2)}, u32[]{:S(2)}) collective-permute-start(bf16[144,128]{1,0:T(8,128)(2,1)S(1)} %collective-permute-done), channel_id=1, source_target_pairs={{0,7},{1,6},{2,5},{3,4},{4,3},{5,2},{6,1},{7,0},{8,15},{9,14},{10,... | collective-permute-start | bytes 110600 | tf_op jit(solution)/shard_map/ppermute | solution.py:36
  10.2 1.5 %collective-permute-start.3 = (bf16[144,128]{1,0:T(8,128)(2,1)S(1)}, bf16[144,128]{1,0:T(8,128)(2,1)S(1)}, u32[]{:S(2)}, u32[]{:S(2)}) collective-permute-start(bf16[144,128]{1,0:T(8,128)(2,1)S(1)} %collective-permute-done), channel_id=1, source_target_pairs={{0,3},{1,4},{2,7},{3,0},{4,1},{5,6},{6,5},{7,2},{8,13},{9,10},{10,... | collective-permute-start | bytes 110600 | tf_op jit(solution)/shard_map/ppermute | solution.py:36
  11.7 1.3 %collective-permute-start.2 = (bf16[144,128]{1,0:T(8,128)(2,1)S(1)}, bf16[144,128]{1,0:T(8,128)(2,1)S(1)}, u32[]{:S(2)}, u32[]{:S(2)}) collective-permute-start(bf16[144,128]{1,0:T(8,128)(2,1)S(1)} %collective-permute-done), channel_id=1, source_target_pairs={{0,5},{1,2},{2,1},{3,6},{4,7},{5,0},{6,3},{7,4},{8,11},{9,12},{10,... | collective-permute-start | bytes 110600 | tf_op jit(solution)/shard_map/ppermute | solution.py:36
  13.0 1.7 %permute_across.1 = (bf16[256,1152]{1,0:T(8,128)(2,1)S(1)}, bf16[256,1152]{1,0:T(8,128)(2,1)S(1)}) custom-call(s32[1]{0:T(128)} %bitcast.me_ref, s32[2,2304]{1,0:T(2,128)S(1)} %get-tuple-element.33.where_ref, f32[256,128]{1,0:T(8,128)S(1)} %get-tuple-element.26.reflectance_ref, bf16[256,2304]{1,0:T(8,128)(2,1)S(1)} %get-tuple-element.27.direct_ref), custom_call_target="tpu_custom_call" | custom-call | flops 1358954496 | tf_op jit(solution)/shard_map/permute_across/pallas_call | solution.py:65
  15.8 1.1 %collective-permute-done.6.b_ref.sky_second_ref = bf16[1152,128]{1,0:T(8,128)(2,1)S(1)} collective-permute-done((bf16[1152,128]{1,0:T(8,128)(2,1)S(1)}, bf16[1152,128]{1,0:T(8,128)(2,1)S(1)}, u32[]{:S(2)}, u32[]{:S(2)}) %collective-permute-start.6) | collective-permute-done | bytes 294944 | tf_op jit(solution)/shard_map/ppermute | solution.py:36
  17.2 0.7 %collective-permute-start.7 = (bf16[256,128]{1,0:T(8,128)(2,1)S(1)}, bf16[256,128]{1,0:T(8,128)(2,1)S(1)}, u32[]{:S(2)}, u32[]{:S(2)}) collective-permute-start(bf16[256,128]{1,0:T(8,128)(2,1)S(1)} %hours_all.1.in_ref), channel_id=1, source_target_pairs={{0,9},{1,8},{2,11},{3,10},{4,13},{5,12},{6,15},{7,14},{8,1},{9,0},... | collective-permute-start | bytes 196616 | tf_op jit(solution)/shard_map/ppermute | solution.py:36
  17.9 1.2 %collective-permute-start.8 = (bf16[256,128]{1,0:T(8,128)(2,1)S(1)}, bf16[256,128]{1,0:T(8,128)(2,1)S(1)}, u32[]{:S(2)}, u32[]{:S(2)}) collective-permute-start(bf16[256,128]{1,0:T(8,128)(2,1)S(1)} %copy.21), channel_id=1, source_target_pairs={{0,3},{1,4},{2,7},{3,0},{4,1},{5,6},{6,5},{7,2},{8,13},{9,10},{10,... | collective-permute-start | bytes 196616 | tf_op jit(solution)/shard_map/ppermute | solution.py:36
  19.5 0.5 %direct.1.base_ref = f32[256,128]{1,0:T(8,128)S(1)} custom-call(bf16[256,1152]{1,0:T(8,128)(2,1)S(1)} %get-tuple-element.38.first_ref, bf16[256,1152]{1,0:T(8,128)(2,1)S(1)} %get-tuple-element.39.second_ref, bf16[1152,128]{1,0:T(8,128)(2,1)S(1)} %constant_dynamic-update-slice_fusion.2.b_ref.sky_first_ref, ...), custom_call_target="tpu_custom_call" | custom-call | flops 2000000000 | tf_op jit(solution)/shard_map/direct/pallas_call | solution.py:65
  19.9 1.7 %collective-permute-done.8 = bf16[256,128]{1,0:T(8,128)(2,1)S(1)} collective-permute-done((bf16[256,128]{1,0:T(8,128)(2,1)S(1)}, bf16[256,128]{1,0:T(8,128)(2,1)S(1)}, u32[]{:S(2)}, u32[]{:S(2)}) %collective-permute-start.8) | collective-permute-done | bytes 65568 | tf_op jit(solution)/shard_map/ppermute | solution.py:36
  21.6 1.3 %collective-permute-start.9 = (bf16[512,128]{1,0:T(8,128)(2,1)S(1)}, bf16[512,128]{1,0:T(8,128)(2,1)S(1)}, u32[]{:S(2)}, u32[]{:S(2)}) collective-permute-start(bf16[512,128]{1,0:T(8,128)(2,1)S(1)} %pad_maximum_fusion.1), channel_id=1, source_target_pairs={{0,5},{1,2},{2,1},{3,6},{4,7},{5,0},{6,3},{7,4},{8,11},{9,12},{10,... | collective-permute-start | bytes 393224 | tf_op jit(solution)/shard_map/ppermute | solution.py:36
  23.0 0.6 %collective-permute-done.7 = bf16[256,128]{1,0:T(8,128)(2,1)S(1)} collective-permute-done((bf16[256,128]{1,0:T(8,128)(2,1)S(1)}, bf16[256,128]{1,0:T(8,128)(2,1)S(1)}, u32[]{:S(2)}, u32[]{:S(2)}) %collective-permute-start.7) | collective-permute-done | bytes 65568 | tf_op jit(solution)/shard_map/ppermute | solution.py:36
  23.5 1.1 %collective-permute-start.13 = (bf16[256,128]{1,0:T(8,128)(2,1)S(1)}, bf16[256,128]{1,0:T(8,128)(2,1)S(1)}, u32[]{:S(2)}, u32[]{:S(2)}) collective-permute-start(bf16[256,128]{1,0:T(8,128)(2,1)S(1)} %collective-permute-done.7), channel_id=1, source_target_pairs={{0,7},{1,6},{2,5},{3,4},{4,3},{5,2},{6,1},{7,0},{8,15},{9,14},{10,... | collective-permute-start | bytes 196616 | tf_op jit(solution)/shard_map/ppermute | solution.py:36
  24.6 0.7 %collective-permute-start.11 = (bf16[256,128]{1,0:T(8,128)(2,1)S(1)}, bf16[256,128]{1,0:T(8,128)(2,1)S(1)}, u32[]{:S(2)}, u32[]{:S(2)}) collective-permute-start(bf16[256,128]{1,0:T(8,128)(2,1)S(1)} %collective-permute-done.7), channel_id=1, source_target_pairs={{0,3},{1,4},{2,7},{3,0},{4,1},{5,6},{6,5},{7,2},{8,13},{9,10},{10,... | collective-permute-start | bytes 196616 | tf_op jit(solution)/shard_map/ppermute | solution.py:36
  25.3 1.3 %collective-permute-start.10 = (bf16[256,128]{1,0:T(8,128)(2,1)S(1)}, bf16[256,128]{1,0:T(8,128)(2,1)S(1)}, u32[]{:S(2)}, u32[]{:S(2)}) collective-permute-start(bf16[256,128]{1,0:T(8,128)(2,1)S(1)} %collective-permute-done.7), channel_id=1, source_target_pairs={{0,5},{1,2},{2,1},{3,6},{4,7},{5,0},{6,3},{7,4},{8,11},{9,12},{10,... | collective-permute-start | bytes 196616 | tf_op jit(solution)/shard_map/ppermute | solution.py:36
  26.6 3.1 %collective-permute-done.10 = bf16[256,128]{1,0:T(8,128)(2,1)S(1)} collective-permute-done((bf16[256,128]{1,0:T(8,128)(2,1)S(1)}, bf16[256,128]{1,0:T(8,128)(2,1)S(1)}, u32[]{:S(2)}, u32[]{:S(2)}) %collective-permute-start.10) | collective-permute-done | bytes 65568 | tf_op jit(solution)/shard_map/ppermute | solution.py:36
  30.4 0.6 %collective-permute-start.14 = (f32[256,128]{1,0:T(8,128)S(1)}, f32[256,128]{1,0:T(8,128)S(1)}, u32[]{:S(2)}, u32[]{:S(2)}) collective-permute-start(f32[256,128]{1,0:T(8,128)S(1)} %partner.1), channel_id=1, source_target_pairs={{0,1},{1,0},{2,3},{3,2},{4,5},{5,4},{6,7},{7,6},{8,9},{9,8},{10,11... | collective-permute-start | bytes 393224 | tf_op jit(solution)/shard_map/ppermute | solution.py:36
  30.9 0.4 %bounce_same.1.a_ref = f32[256,128]{1,0:T(8,128)S(1)} custom-call(s32[1]{0:T(128)} %bitcast.me_ref, f32[256,128]{1,0:T(8,128)S(1)} %direct.1.base_ref, bf16[256,4096]{1,0:T(8,128)(2,1)S(1)} %copy-done, bf16[2048,128]{1,0:T(8,128)(2,1)S(1)} %constant_dynamic-update-slice_fusion.9.hours_ref), custom_call_target="tpu_custom_call" | custom-call | flops 134217728 | tf_op jit(solution)/shard_map/bounce_same/pallas_call | solution.py:65
  31.4 0.6 %collective-permute-done.14.b_ref = f32[256,128]{1,0:T(8,128)S(1)} collective-permute-done((f32[256,128]{1,0:T(8,128)S(1)}, f32[256,128]{1,0:T(8,128)S(1)}, u32[]{:S(2)}, u32[]{:S(2)}) %collective-permute-start.14) | collective-permute-done | bytes 131104 | tf_op jit(solution)/shard_map/ppermute | solution.py:36
  31.9 0.7 %sum.1 = bf16[256,128]{1,0:T(8,128)(2,1)} custom-call(f32[256,128]{1,0:T(8,128)S(1)} %bounce_same.1.a_ref, f32[256,128]{1,0:T(8,128)S(1)} %collective-permute-done.14.b_ref), custom_call_target="tpu_custom_call" | custom-call | tf_op jit(solution)/shard_map/sum/pallas_call | solution.py:65
  (38 shorter events, 2.3 us)
Async XLA Ops:
  0.0 9.5 %collective-permute-start = (bf16[144,128]{1,0:T(8,128)(2,1)}, bf16[144,128]{1,0:T(8,128)(2,1)S(1)}, u32[]{:S(2)}, u32[]{:S(2)}) collective-permute-start(bf16[144,128]{1,0:T(8,128)(2,1)} %sky_in.1), channel_id=1, source_target_pairs={{0,9},{1,8},{2,11},{3,10},{4,13},{5,12},{6,15},{7,14},{8,1},{9,0},... | collective-permute-start | bytes 110600 | tf_op jit(solution)/shard_map/ppermute | solution.py:36
  3.5 4.9 %collective-permute-start.1 = (bf16[144,128]{1,0:T(8,128)(2,1)}, bf16[144,128]{1,0:T(8,128)(2,1)S(1)}, u32[]{:S(2)}, u32[]{:S(2)}) collective-permute-start(bf16[144,128]{1,0:T(8,128)(2,1)} %sky_in.1), channel_id=1, source_target_pairs={{0,3},{1,4},{2,7},{3,0},{4,1},{5,6},{6,5},{7,2},{8,13},{9,10},{10,... | collective-permute-start | bytes 110600 | tf_op jit(solution)/shard_map/ppermute | solution.py:36
  8.4 6.7 %collective-permute-start.5 = (bf16[288,128]{1,0:T(8,128)(2,1)S(1)}, bf16[288,128]{1,0:T(8,128)(2,1)S(1)}, u32[]{:S(2)}, u32[]{:S(2)}) collective-permute-start(bf16[288,128]{1,0:T(8,128)(2,1)S(1)} %constant_dynamic-update-slice_fusion), channel_id=1, source_target_pairs={{0,5},{1,2},{2,1},{3,6},{4,7},{5,0},{6,3},{7,4},{8,11},{9,12},{10,... | collective-permute-start | bytes 221192 | tf_op jit(solution)/shard_map/ppermute | solution.py:36
  9.5 5.6 %collective-permute-start.4 = (bf16[144,128]{1,0:T(8,128)(2,1)S(1)}, bf16[144,128]{1,0:T(8,128)(2,1)S(1)}, u32[]{:S(2)}, u32[]{:S(2)}) collective-permute-start(bf16[144,128]{1,0:T(8,128)(2,1)S(1)} %collective-permute-done), channel_id=1, source_target_pairs={{0,7},{1,6},{2,5},{3,4},{4,3},{5,2},{6,1},{7,0},{8,15},{9,14},{10,... | collective-permute-start | bytes 110600 | tf_op jit(solution)/shard_map/ppermute | solution.py:36
  10.2 4.9 %collective-permute-start.3 = (bf16[144,128]{1,0:T(8,128)(2,1)S(1)}, bf16[144,128]{1,0:T(8,128)(2,1)S(1)}, u32[]{:S(2)}, u32[]{:S(2)}) collective-permute-start(bf16[144,128]{1,0:T(8,128)(2,1)S(1)} %collective-permute-done), channel_id=1, source_target_pairs={{0,3},{1,4},{2,7},{3,0},{4,1},{5,6},{6,5},{7,2},{8,13},{9,10},{10,... | collective-permute-start | bytes 110600 | tf_op jit(solution)/shard_map/ppermute | solution.py:36
  11.7 3.4 %collective-permute-start.2 = (bf16[144,128]{1,0:T(8,128)(2,1)S(1)}, bf16[144,128]{1,0:T(8,128)(2,1)S(1)}, u32[]{:S(2)}, u32[]{:S(2)}) collective-permute-start(bf16[144,128]{1,0:T(8,128)(2,1)S(1)} %collective-permute-done), channel_id=1, source_target_pairs={{0,5},{1,2},{2,1},{3,6},{4,7},{5,0},{6,3},{7,4},{8,11},{9,12},{10,... | collective-permute-start | bytes 110600 | tf_op jit(solution)/shard_map/ppermute | solution.py:36
  15.2 4.0 %copy-start = (bf16[256,4096]{1,0:T(8,128)(2,1)S(1)}, bf16[256,4096]{1,0:T(8,128)(2,1)}, u32[]{:S(2)}) copy-start(bf16[256,4096]{1,0:T(8,128)(2,1)} %factors_ref.2) | copy-start | bytes 6291460
  15.2 1.6 %collective-permute-start.6 = (bf16[1152,128]{1,0:T(8,128)(2,1)S(1)}, bf16[1152,128]{1,0:T(8,128)(2,1)S(1)}, u32[]{:S(2)}, u32[]{:S(2)}) collective-permute-start(bf16[1152,128]{1,0:T(8,128)(2,1)S(1)} %constant_dynamic-update-slice_fusion.2.b_ref.sky_first_ref), channel_id=1, source_target_pairs={{0,1},{1,0},{2,3},{3,2},{4,5},{5,4},{6,7},{7,6},{8,9},{9,8},{10,11... | collective-permute-start | bytes 884744 | tf_op jit(solution)/shard_map/ppermute | solution.py:36
  17.2 6.3 %collective-permute-start.7 = (bf16[256,128]{1,0:T(8,128)(2,1)S(1)}, bf16[256,128]{1,0:T(8,128)(2,1)S(1)}, u32[]{:S(2)}, u32[]{:S(2)}) collective-permute-start(bf16[256,128]{1,0:T(8,128)(2,1)S(1)} %hours_all.1.in_ref), channel_id=1, source_target_pairs={{0,9},{1,8},{2,11},{3,10},{4,13},{5,12},{6,15},{7,14},{8,1},{9,0},... | collective-permute-start | bytes 196616 | tf_op jit(solution)/shard_map/ppermute | solution.py:36
  17.9 3.7 %collective-permute-start.8 = (bf16[256,128]{1,0:T(8,128)(2,1)S(1)}, bf16[256,128]{1,0:T(8,128)(2,1)S(1)}, u32[]{:S(2)}, u32[]{:S(2)}) collective-permute-start(bf16[256,128]{1,0:T(8,128)(2,1)S(1)} %copy.21), channel_id=1, source_target_pairs={{0,3},{1,4},{2,7},{3,0},{4,1},{5,6},{6,5},{7,2},{8,13},{9,10},{10,... | collective-permute-start | bytes 196616 | tf_op jit(solution)/shard_map/ppermute | solution.py:36
  19.3 10.5 %collective-permute-start.12 = (bf16[256,2048]{1,0:T(8,128)(2,1)S(1)}, bf16[256,2048]{1,0:T(8,128)(2,1)S(1)}, u32[]{:S(2)}, u32[]{:S(2)}) collective-permute-start(bf16[256,2048]{1,0:T(8,128)(2,1)S(1)} %select.1), channel_id=1, source_target_pairs={{0,1},{1,0},{2,3},{3,2},{4,5},{5,4},{6,7},{7,6},{8,9},{9,8},{10,11... | collective-permute-start | bytes 3145736 | tf_op jit(solution)/shard_map/ppermute | solution.py:36
  21.6 5.0 %collective-permute-start.9 = (bf16[512,128]{1,0:T(8,128)(2,1)S(1)}, bf16[512,128]{1,0:T(8,128)(2,1)S(1)}, u32[]{:S(2)}, u32[]{:S(2)}) collective-permute-start(bf16[512,128]{1,0:T(8,128)(2,1)S(1)} %pad_maximum_fusion.1), channel_id=1, source_target_pairs={{0,5},{1,2},{2,1},{3,6},{4,7},{5,0},{6,3},{7,4},{8,11},{9,12},{10,... | collective-permute-start | bytes 393224 | tf_op jit(solution)/shard_map/ppermute | solution.py:36
  23.5 6.6 %collective-permute-start.13 = (bf16[256,128]{1,0:T(8,128)(2,1)S(1)}, bf16[256,128]{1,0:T(8,128)(2,1)S(1)}, u32[]{:S(2)}, u32[]{:S(2)}) collective-permute-start(bf16[256,128]{1,0:T(8,128)(2,1)S(1)} %collective-permute-done.7), channel_id=1, source_target_pairs={{0,7},{1,6},{2,5},{3,4},{4,3},{5,2},{6,1},{7,0},{8,15},{9,14},{10,... | collective-permute-start | bytes 196616 | tf_op jit(solution)/shard_map/ppermute | solution.py:36
  24.6 5.4 %collective-permute-start.11 = (bf16[256,128]{1,0:T(8,128)(2,1)S(1)}, bf16[256,128]{1,0:T(8,128)(2,1)S(1)}, u32[]{:S(2)}, u32[]{:S(2)}) collective-permute-start(bf16[256,128]{1,0:T(8,128)(2,1)S(1)} %collective-permute-done.7), channel_id=1, source_target_pairs={{0,3},{1,4},{2,7},{3,0},{4,1},{5,6},{6,5},{7,2},{8,13},{9,10},{10,... | collective-permute-start | bytes 196616 | tf_op jit(solution)/shard_map/ppermute | solution.py:36
  25.3 4.4 %collective-permute-start.10 = (bf16[256,128]{1,0:T(8,128)(2,1)S(1)}, bf16[256,128]{1,0:T(8,128)(2,1)S(1)}, u32[]{:S(2)}, u32[]{:S(2)}) collective-permute-start(bf16[256,128]{1,0:T(8,128)(2,1)S(1)} %collective-permute-done.7), channel_id=1, source_target_pairs={{0,5},{1,2},{2,1},{3,6},{4,7},{5,0},{6,3},{7,4},{8,11},{9,12},{10,... | collective-permute-start | bytes 196616 | tf_op jit(solution)/shard_map/ppermute | solution.py:36
  30.4 1.5 %collective-permute-start.14 = (f32[256,128]{1,0:T(8,128)S(1)}, f32[256,128]{1,0:T(8,128)S(1)}, u32[]{:S(2)}, u32[]{:S(2)}) collective-permute-start(f32[256,128]{1,0:T(8,128)S(1)} %partner.1), channel_id=1, source_target_pairs={{0,1},{1,0},{2,3},{3,2},{4,5},{5,4},{6,7},{7,6},{8,9},{9,8},{10,11... | collective-permute-start | bytes 393224 | tf_op jit(solution)/shard_map/ppermute | solution.py:36

commit v6 on v5

--- a/solution.py
+++ b/solution.py
@@ -165,7 +165,7 @@
 
 def tail_kernel(start, base_ref, factors_ref, hours_ref, out_ref):
     part = jnp.dot(factors_ref[:, start:], hours_ref[start:, :], preferred_element_type=jnp.float32)
-    out_ref[...] = base_ref[...] + part
+    out_ref[...] = (base_ref[...] + part).astype(out_ref.dtype)
 
 
 def sum_kernel(a_ref, b_ref, out_ref):
@@ -252,7 +252,7 @@
     same, total, partial = gather(size, own, copy, copy, order, total, ("second", partner_head))
     start = head[0].value.shape[0]
     partial = call(
-        functools.partial(tail_kernel, start), "partner", flat, [WHOLE] * 3, flops, partial, theirs, same.value
+        functools.partial(tail_kernel, start), "partner", short, [WHOLE] * 3, flops, partial, theirs, same.value
     )
     partial = swap(size, Piece(partial, [[0], [0]]), 1).value
     total = call(

time: 32.7 us -> 32.6 us (level)
  no operation moved by 1% of the time
where the time goes in v6:
time: 32.6 us; the launch traced here: 32.5 us
  starting transfers between devices  17.2 us (53%)
  Pallas kernels  7.76 us (24%)
  waiting for transfers between devices  7.11 us (22%)
    ppermute x15, starting transfers between devices, swap(): lax.ppermute(piece.value, 'col', pairs)  17.2 us
    pallas_call x12, Pallas kernels, call(): pl.pallas_call(kernel, scratch_shapes=scratch, out_shape=outs, in_specs=s...  7.76 us
    ppermute x15, waiting for transfers between devices, swap(): lax.ppermute(piece.value, 'col', pairs)  7.11 us
  transfers between devices with their start and end apart: 15, of which 6 were waited for; matrix products, arithmetic and copies ran while one was open for 1% of the time, Pallas kernels for 20%

profile of v6, /device:TPU:0, one launch (start us, length us, event | category | flops | bytes accessed | tf_op | source)
XLA Modules:
  0.0 32.5 jit_solution(5099808888734358770)
XLA Ops:
  0.0 3.5 %collective-permute-start = (bf16[144,128]{1,0:T(8,128)(2,1)}, bf16[144,128]{1,0:T(8,128)(2,1)S(1)}, u32[]{:S(2)}, u32[]{:S(2)}) collective-permute-start(bf16[144,128]{1,0:T(8,128)(2,1)} %sky_in.1), channel_id=1, source_target_pairs={{0,9},{1,8},{2,11},{3,10},{4,13},{5,12},{6,15},{7,14},{8,1},{9,0},... | collective-permute-start | bytes 110600 | tf_op jit(solution)/shard_map/ppermute | solution.py:36
  3.5 1.8 %collective-permute-start.1 = (bf16[144,128]{1,0:T(8,128)(2,1)}, bf16[144,128]{1,0:T(8,128)(2,1)S(1)}, u32[]{:S(2)}, u32[]{:S(2)}) collective-permute-start(bf16[144,128]{1,0:T(8,128)(2,1)} %sky_in.1), channel_id=1, source_target_pairs={{0,3},{1,4},{2,7},{3,0},{4,1},{5,6},{6,5},{7,2},{8,13},{9,10},{10,... | collective-permute-start | bytes 110600 | tf_op jit(solution)/shard_map/ppermute | solution.py:36
  5.3 1.4 %prepare.1 = (bf16[144,128]{1,0:T(8,128)(2,1)S(1)}, bf16[256,2304]{1,0:T(8,128)(2,1)S(1)}, f32[256,128]{1,0:T(8,128)S(1)}, s32[2,2304]{1,0:T(2,128)S(1)}) custom-call(f32[16]{0:T(128)} %albedo_in.1, s32[256]{0:T(256)} %material_in.1, s32[2304]{0:T(1024)} %order_in.1, bf16[144,128]{1,0:T(8,128)(2,1)} %sky_in.1, bf16[256,2304]{1,0:T(8,128)(2,1)} %direct_in.1, ...), custom_call_target="tpu_custom_call" | custom-call | flops 1000000000 | tf_op jit(solution)/shard_map/prepare/pallas_call | solution.py:65
  6.7 1.7 %permute_same.1 = (bf16[256,1152]{1,0:T(8,128)(2,1)S(1)}, bf16[256,1152]{1,0:T(8,128)(2,1)S(1)}) custom-call(s32[1]{0:T(128)} %bitcast.me_ref, s32[2,2304]{1,0:T(2,128)S(1)} %get-tuple-element.33.where_ref, f32[256,128]{1,0:T(8,128)S(1)} %get-tuple-element.26.reflectance_ref, bf16[256,2304]{1,0:T(8,128)(2,1)S(1)} %get-tuple-element.27.direct_ref), custom_call_target="tpu_custom_call" | custom-call | flops 1358954496 | tf_op jit(solution)/shard_map/permute_same/pallas_call | solution.py:65
  8.4 1.1 %collective-permute-start.5 = (bf16[288,128]{1,0:T(8,128)(2,1)S(1)}, bf16[288,128]{1,0:T(8,128)(2,1)S(1)}, u32[]{:S(2)}, u32[]{:S(2)}) collective-permute-start(bf16[288,128]{1,0:T(8,128)(2,1)S(1)} %constant_dynamic-update-slice_fusion), channel_id=1, source_target_pairs={{0,5},{1,2},{2,1},{3,6},{4,7},{5,0},{6,3},{7,4},{8,11},{9,12},{10,... | collective-permute-start | bytes 221192 | tf_op jit(solution)/shard_map/ppermute | solution.py:36
  9.5 0.7 %collective-permute-start.4 = (bf16[144,128]{1,0:T(8,128)(2,1)S(1)}, bf16[144,128]{1,0:T(8,128)(2,1)S(1)}, u32[]{:S(2)}, u32[]{:S(2)}) collective-permute-start(bf16[144,128]{1,0:T(8,128)(2,1)S(1)} %collective-permute-done), channel_id=1, source_target_pairs={{0,7},{1,6},{2,5},{3,4},{4,3},{5,2},{6,1},{7,0},{8,15},{9,14},{10,... | collective-permute-start | bytes 110600 | tf_op jit(solution)/shard_map/ppermute | solution.py:36
  10.2 1.5 %collective-permute-start.3 = (bf16[144,128]{1,0:T(8,128)(2,1)S(1)}, bf16[144,128]{1,0:T(8,128)(2,1)S(1)}, u32[]{:S(2)}, u32[]{:S(2)}) collective-permute-start(bf16[144,128]{1,0:T(8,128)(2,1)S(1)} %collective-permute-done), channel_id=1, source_target_pairs={{0,3},{1,4},{2,7},{3,0},{4,1},{5,6},{6,5},{7,2},{8,13},{9,10},{10,... | collective-permute-start | bytes 110600 | tf_op jit(solution)/shard_map/ppermute | solution.py:36
  11.7 1.3 %collective-permute-start.2 = (bf16[144,128]{1,0:T(8,128)(2,1)S(1)}, bf16[144,128]{1,0:T(8,128)(2,1)S(1)}, u32[]{:S(2)}, u32[]{:S(2)}) collective-permute-start(bf16[144,128]{1,0:T(8,128)(2,1)S(1)} %collective-permute-done), channel_id=1, source_target_pairs={{0,5},{1,2},{2,1},{3,6},{4,7},{5,0},{6,3},{7,4},{8,11},{9,12},{10,... | collective-permute-start | bytes 110600 | tf_op jit(solution)/shard_map/ppermute | solution.py:36
  13.0 1.7 %permute_across.1 = (bf16[256,1152]{1,0:T(8,128)(2,1)S(1)}, bf16[256,1152]{1,0:T(8,128)(2,1)S(1)}) custom-call(s32[1]{0:T(128)} %bitcast.me_ref, s32[2,2304]{1,0:T(2,128)S(1)} %get-tuple-element.33.where_ref, f32[256,128]{1,0:T(8,128)S(1)} %get-tuple-element.26.reflectance_ref, bf16[256,2304]{1,0:T(8,128)(2,1)S(1)} %get-tuple-element.27.direct_ref), custom_call_target="tpu_custom_call" | custom-call | flops 1358954496 | tf_op jit(solution)/shard_map/permute_across/pallas_call | solution.py:65
  15.8 1.1 %collective-permute-done.6.b_ref.sky_second_ref = bf16[1152,128]{1,0:T(8,128)(2,1)S(1)} collective-permute-done((bf16[1152,128]{1,0:T(8,128)(2,1)S(1)}, bf16[1152,128]{1,0:T(8,128)(2,1)S(1)}, u32[]{:S(2)}, u32[]{:S(2)}) %collective-permute-start.6) | collective-permute-done | bytes 294944 | tf_op jit(solution)/shard_map/ppermute | solution.py:36
  17.2 0.7 %collective-permute-start.7 = (bf16[256,128]{1,0:T(8,128)(2,1)S(1)}, bf16[256,128]{1,0:T(8,128)(2,1)S(1)}, u32[]{:S(2)}, u32[]{:S(2)}) collective-permute-start(bf16[256,128]{1,0:T(8,128)(2,1)S(1)} %hours_all.1.in_ref), channel_id=1, source_target_pairs={{0,9},{1,8},{2,11},{3,10},{4,13},{5,12},{6,15},{7,14},{8,1},{9,0},... | collective-permute-start | bytes 196616 | tf_op jit(solution)/shard_map/ppermute | solution.py:36
  17.9 1.2 %collective-permute-start.8 = (bf16[256,128]{1,0:T(8,128)(2,1)S(1)}, bf16[256,128]{1,0:T(8,128)(2,1)S(1)}, u32[]{:S(2)}, u32[]{:S(2)}) collective-permute-start(bf16[256,128]{1,0:T(8,128)(2,1)S(1)} %copy.21), channel_id=1, source_target_pairs={{0,3},{1,4},{2,7},{3,0},{4,1},{5,6},{6,5},{7,2},{8,13},{9,10},{10,... | collective-permute-start | bytes 196616 | tf_op jit(solution)/shard_map/ppermute | solution.py:36
  19.5 0.5 %direct.1.base_ref = f32[256,128]{1,0:T(8,128)S(1)} custom-call(bf16[256,1152]{1,0:T(8,128)(2,1)S(1)} %get-tuple-element.38.first_ref, bf16[256,1152]{1,0:T(8,128)(2,1)S(1)} %get-tuple-element.39.second_ref, bf16[1152,128]{1,0:T(8,128)(2,1)S(1)} %constant_dynamic-update-slice_fusion.2.b_ref.sky_first_ref, ...), custom_call_target="tpu_custom_call" | custom-call | flops 2000000000 | tf_op jit(solution)/shard_map/direct/pallas_call | solution.py:65
  19.9 1.7 %collective-permute-done.8 = bf16[256,128]{1,0:T(8,128)(2,1)S(1)} collective-permute-done((bf16[256,128]{1,0:T(8,128)(2,1)S(1)}, bf16[256,128]{1,0:T(8,128)(2,1)S(1)}, u32[]{:S(2)}, u32[]{:S(2)}) %collective-permute-start.8) | collective-permute-done | bytes 65568 | tf_op jit(solution)/shard_map/ppermute | solution.py:36
  21.6 1.3 %collective-permute-start.9 = (bf16[512,128]{1,0:T(8,128)(2,1)S(1)}, bf16[512,128]{1,0:T(8,128)(2,1)S(1)}, u32[]{:S(2)}, u32[]{:S(2)}) collective-permute-start(bf16[512,128]{1,0:T(8,128)(2,1)S(1)} %pad_maximum_fusion.1), channel_id=1, source_target_pairs={{0,5},{1,2},{2,1},{3,6},{4,7},{5,0},{6,3},{7,4},{8,11},{9,12},{10,... | collective-permute-start | bytes 393224 | tf_op jit(solution)/shard_map/ppermute | solution.py:36
  23.0 0.6 %collective-permute-done.7 = bf16[256,128]{1,0:T(8,128)(2,1)S(1)} collective-permute-done((bf16[256,128]{1,0:T(8,128)(2,1)S(1)}, bf16[256,128]{1,0:T(8,128)(2,1)S(1)}, u32[]{:S(2)}, u32[]{:S(2)}) %collective-permute-start.7) | collective-permute-done | bytes 65568 | tf_op jit(solution)/shard_map/ppermute | solution.py:36
  23.5 1.1 %collective-permute-start.13 = (bf16[256,128]{1,0:T(8,128)(2,1)S(1)}, bf16[256,128]{1,0:T(8,128)(2,1)S(1)}, u32[]{:S(2)}, u32[]{:S(2)}) collective-permute-start(bf16[256,128]{1,0:T(8,128)(2,1)S(1)} %collective-permute-done.7), channel_id=1, source_target_pairs={{0,7},{1,6},{2,5},{3,4},{4,3},{5,2},{6,1},{7,0},{8,15},{9,14},{10,... | collective-permute-start | bytes 196616 | tf_op jit(solution)/shard_map/ppermute | solution.py:36
  24.6 0.7 %collective-permute-start.11 = (bf16[256,128]{1,0:T(8,128)(2,1)S(1)}, bf16[256,128]{1,0:T(8,128)(2,1)S(1)}, u32[]{:S(2)}, u32[]{:S(2)}) collective-permute-start(bf16[256,128]{1,0:T(8,128)(2,1)S(1)} %collective-permute-done.7), channel_id=1, source_target_pairs={{0,3},{1,4},{2,7},{3,0},{4,1},{5,6},{6,5},{7,2},{8,13},{9,10},{10,... | collective-permute-start | bytes 196616 | tf_op jit(solution)/shard_map/ppermute | solution.py:36
  25.3 1.3 %collective-permute-start.10 = (bf16[256,128]{1,0:T(8,128)(2,1)S(1)}, bf16[256,128]{1,0:T(8,128)(2,1)S(1)}, u32[]{:S(2)}, u32[]{:S(2)}) collective-permute-start(bf16[256,128]{1,0:T(8,128)(2,1)S(1)} %collective-permute-done.7), channel_id=1, source_target_pairs={{0,5},{1,2},{2,1},{3,6},{4,7},{5,0},{6,3},{7,4},{8,11},{9,12},{10,... | collective-permute-start | bytes 196616 | tf_op jit(solution)/shard_map/ppermute | solution.py:36
  26.6 3.1 %collective-permute-done.10 = bf16[256,128]{1,0:T(8,128)(2,1)S(1)} collective-permute-done((bf16[256,128]{1,0:T(8,128)(2,1)S(1)}, bf16[256,128]{1,0:T(8,128)(2,1)S(1)}, u32[]{:S(2)}, u32[]{:S(2)}) %collective-permute-start.10) | collective-permute-done | bytes 65568 | tf_op jit(solution)/shard_map/ppermute | solution.py:36
  30.4 0.6 %collective-permute-start.14 = (bf16[256,128]{1,0:T(8,128)(2,1)S(1)}, bf16[256,128]{1,0:T(8,128)(2,1)S(1)}, u32[]{:S(2)}, u32[]{:S(2)}) collective-permute-start(bf16[256,128]{1,0:T(8,128)(2,1)S(1)} %partner.1), channel_id=1, source_target_pairs={{0,1},{1,0},{2,3},{3,2},{4,5},{5,4},{6,7},{7,6},{8,9},{9,8},{10,11... | collective-permute-start | bytes 196616 | tf_op jit(solution)/shard_map/ppermute | solution.py:36
  30.9 0.4 %bounce_same.1.a_ref = f32[256,128]{1,0:T(8,128)S(1)} custom-call(s32[1]{0:T(128)} %bitcast.me_ref, f32[256,128]{1,0:T(8,128)S(1)} %direct.1.base_ref, bf16[256,4096]{1,0:T(8,128)(2,1)S(1)} %copy-done, bf16[2048,128]{1,0:T(8,128)(2,1)S(1)} %constant_dynamic-update-slice_fusion.9.hours_ref), custom_call_target="tpu_custom_call" | custom-call | flops 134217728 | tf_op jit(solution)/shard_map/bounce_same/pallas_call | solution.py:65
  31.4 0.5 %collective-permute-done.14.b_ref = bf16[256,128]{1,0:T(8,128)(2,1)S(1)} collective-permute-done((bf16[256,128]{1,0:T(8,128)(2,1)S(1)}, bf16[256,128]{1,0:T(8,128)(2,1)S(1)}, u32[]{:S(2)}, u32[]{:S(2)}) %collective-permute-start.14) | collective-permute-done | bytes 65568 | tf_op jit(solution)/shard_map/ppermute | solution.py:36
  31.8 0.6 %sum.1 = bf16[256,128]{1,0:T(8,128)(2,1)} custom-call(f32[256,128]{1,0:T(8,128)S(1)} %bounce_same.1.a_ref, bf16[256,128]{1,0:T(8,128)(2,1)S(1)} %collective-permute-done.14.b_ref), custom_call_target="tpu_custom_call" | custom-call | tf_op jit(solution)/shard_map/sum/pallas_call | solution.py:65
  (38 shorter events, 2.3 us)
Async XLA Ops:
  0.0 9.5 %collective-permute-start = (bf16[144,128]{1,0:T(8,128)(2,1)}, bf16[144,128]{1,0:T(8,128)(2,1)S(1)}, u32[]{:S(2)}, u32[]{:S(2)}) collective-permute-start(bf16[144,128]{1,0:T(8,128)(2,1)} %sky_in.1), channel_id=1, source_target_pairs={{0,9},{1,8},{2,11},{3,10},{4,13},{5,12},{6,15},{7,14},{8,1},{9,0},... | collective-permute-start | bytes 110600 | tf_op jit(solution)/shard_map/ppermute | solution.py:36
  3.5 4.9 %collective-permute-start.1 = (bf16[144,128]{1,0:T(8,128)(2,1)}, bf16[144,128]{1,0:T(8,128)(2,1)S(1)}, u32[]{:S(2)}, u32[]{:S(2)}) collective-permute-start(bf16[144,128]{1,0:T(8,128)(2,1)} %sky_in.1), channel_id=1, source_target_pairs={{0,3},{1,4},{2,7},{3,0},{4,1},{5,6},{6,5},{7,2},{8,13},{9,10},{10,... | collective-permute-start | bytes 110600 | tf_op jit(solution)/shard_map/ppermute | solution.py:36
  8.4 6.7 %collective-permute-start.5 = (bf16[288,128]{1,0:T(8,128)(2,1)S(1)}, bf16[288,128]{1,0:T(8,128)(2,1)S(1)}, u32[]{:S(2)}, u32[]{:S(2)}) collective-permute-start(bf16[288,128]{1,0:T(8,128)(2,1)S(1)} %constant_dynamic-update-slice_fusion), channel_id=1, source_target_pairs={{0,5},{1,2},{2,1},{3,6},{4,7},{5,0},{6,3},{7,4},{8,11},{9,12},{10,... | collective-permute-start | bytes 221192 | tf_op jit(solution)/shard_map/ppermute | solution.py:36
  9.5 5.6 %collective-permute-start.4 = (bf16[144,128]{1,0:T(8,128)(2,1)S(1)}, bf16[144,128]{1,0:T(8,128)(2,1)S(1)}, u32[]{:S(2)}, u32[]{:S(2)}) collective-permute-start(bf16[144,128]{1,0:T(8,128)(2,1)S(1)} %collective-permute-done), channel_id=1, source_target_pairs={{0,7},{1,6},{2,5},{3,4},{4,3},{5,2},{6,1},{7,0},{8,15},{9,14},{10,... | collective-permute-start | bytes 110600 | tf_op jit(solution)/shard_map/ppermute | solution.py:36
  10.2 4.9 %collective-permute-start.3 = (bf16[144,128]{1,0:T(8,128)(2,1)S(1)}, bf16[144,128]{1,0:T(8,128)(2,1)S(1)}, u32[]{:S(2)}, u32[]{:S(2)}) collective-permute-start(bf16[144,128]{1,0:T(8,128)(2,1)S(1)} %collective-permute-done), channel_id=1, source_target_pairs={{0,3},{1,4},{2,7},{3,0},{4,1},{5,6},{6,5},{7,2},{8,13},{9,10},{10,... | collective-permute-start | bytes 110600 | tf_op jit(solution)/shard_map/ppermute | solution.py:36
  11.7 3.4 %collective-permute-start.2 = (bf16[144,128]{1,0:T(8,128)(2,1)S(1)}, bf16[144,128]{1,0:T(8,128)(2,1)S(1)}, u32[]{:S(2)}, u32[]{:S(2)}) collective-permute-start(bf16[144,128]{1,0:T(8,128)(2,1)S(1)} %collective-permute-done), channel_id=1, source_target_pairs={{0,5},{1,2},{2,1},{3,6},{4,7},{5,0},{6,3},{7,4},{8,11},{9,12},{10,... | collective-permute-start | bytes 110600 | tf_op jit(solution)/shard_map/ppermute | solution.py:36
  15.2 4.0 %copy-start = (bf16[256,4096]{1,0:T(8,128)(2,1)S(1)}, bf16[256,4096]{1,0:T(8,128)(2,1)}, u32[]{:S(2)}) copy-start(bf16[256,4096]{1,0:T(8,128)(2,1)} %factors_ref.2) | copy-start | bytes 6291460
  15.2 1.6 %collective-permute-start.6 = (bf16[1152,128]{1,0:T(8,128)(2,1)S(1)}, bf16[1152,128]{1,0:T(8,128)(2,1)S(1)}, u32[]{:S(2)}, u32[]{:S(2)}) collective-permute-start(bf16[1152,128]{1,0:T(8,128)(2,1)S(1)} %constant_dynamic-update-slice_fusion.2.b_ref.sky_first_ref), channel_id=1, source_target_pairs={{0,1},{1,0},{2,3},{3,2},{4,5},{5,4},{6,7},{7,6},{8,9},{9,8},{10,11... | collective-permute-start | bytes 884744 | tf_op jit(solution)/shard_map/ppermute | solution.py:36
  17.2 6.3 %collective-permute-start.7 = (bf16[256,128]{1,0:T(8,128)(2,1)S(1)}, bf16[256,128]{1,0:T(8,128)(2,1)S(1)}, u32[]{:S(2)}, u32[]{:S(2)}) collective-permute-start(bf16[256,128]{1,0:T(8,128)(2,1)S(1)} %hours_all.1.in_ref), channel_id=1, source_target_pairs={{0,9},{1,8},{2,11},{3,10},{4,13},{5,12},{6,15},{7,14},{8,1},{9,0},... | collective-permute-start | bytes 196616 | tf_op jit(solution)/shard_map/ppermute | solution.py:36
  17.9 3.7 %collective-permute-start.8 = (bf16[256,128]{1,0:T(8,128)(2,1)S(1)}, bf16[256,128]{1,0:T(8,128)(2,1)S(1)}, u32[]{:S(2)}, u32[]{:S(2)}) collective-permute-start(bf16[256,128]{1,0:T(8,128)(2,1)S(1)} %copy.21), channel_id=1, source_target_pairs={{0,3},{1,4},{2,7},{3,0},{4,1},{5,6},{6,5},{7,2},{8,13},{9,10},{10,... | collective-permute-start | bytes 196616 | tf_op jit(solution)/shard_map/ppermute | solution.py:36
  19.3 10.5 %collective-permute-start.12 = (bf16[256,2048]{1,0:T(8,128)(2,1)S(1)}, bf16[256,2048]{1,0:T(8,128)(2,1)S(1)}, u32[]{:S(2)}, u32[]{:S(2)}) collective-permute-start(bf16[256,2048]{1,0:T(8,128)(2,1)S(1)} %select.1), channel_id=1, source_target_pairs={{0,1},{1,0},{2,3},{3,2},{4,5},{5,4},{6,7},{7,6},{8,9},{9,8},{10,11... | collective-permute-start | bytes 3145736 | tf_op jit(solution)/shard_map/ppermute | solution.py:36
  21.6 5.0 %collective-permute-start.9 = (bf16[512,128]{1,0:T(8,128)(2,1)S(1)}, bf16[512,128]{1,0:T(8,128)(2,1)S(1)}, u32[]{:S(2)}, u32[]{:S(2)}) collective-permute-start(bf16[512,128]{1,0:T(8,128)(2,1)S(1)} %pad_maximum_fusion.1), channel_id=1, source_target_pairs={{0,5},{1,2},{2,1},{3,6},{4,7},{5,0},{6,3},{7,4},{8,11},{9,12},{10,... | collective-permute-start | bytes 393224 | tf_op jit(solution)/shard_map/ppermute | solution.py:36
  23.5 6.6 %collective-permute-start.13 = (bf16[256,128]{1,0:T(8,128)(2,1)S(1)}, bf16[256,128]{1,0:T(8,128)(2,1)S(1)}, u32[]{:S(2)}, u32[]{:S(2)}) collective-permute-start(bf16[256,128]{1,0:T(8,128)(2,1)S(1)} %collective-permute-done.7), channel_id=1, source_target_pairs={{0,7},{1,6},{2,5},{3,4},{4,3},{5,2},{6,1},{7,0},{8,15},{9,14},{10,... | collective-permute-start | bytes 196616 | tf_op jit(solution)/shard_map/ppermute | solution.py:36
  24.6 5.4 %collective-permute-start.11 = (bf16[256,128]{1,0:T(8,128)(2,1)S(1)}, bf16[256,128]{1,0:T(8,128)(2,1)S(1)}, u32[]{:S(2)}, u32[]{:S(2)}) collective-permute-start(bf16[256,128]{1,0:T(8,128)(2,1)S(1)} %collective-permute-done.7), channel_id=1, source_target_pairs={{0,3},{1,4},{2,7},{3,0},{4,1},{5,6},{6,5},{7,2},{8,13},{9,10},{10,... | collective-permute-start | bytes 196616 | tf_op jit(solution)/shard_map/ppermute | solution.py:36
  25.3 4.4 %collective-permute-start.10 = (bf16[256,128]{1,0:T(8,128)(2,1)S(1)}, bf16[256,128]{1,0:T(8,128)(2,1)S(1)}, u32[]{:S(2)}, u32[]{:S(2)}) collective-permute-start(bf16[256,128]{1,0:T(8,128)(2,1)S(1)} %collective-permute-done.7), channel_id=1, source_target_pairs={{0,5},{1,2},{2,1},{3,6},{4,7},{5,0},{6,3},{7,4},{8,11},{9,12},{10,... | collective-permute-start | bytes 196616 | tf_op jit(solution)/shard_map/ppermute | solution.py:36
  30.4 1.5 %collective-permute-start.14 = (bf16[256,128]{1,0:T(8,128)(2,1)S(1)}, bf16[256,128]{1,0:T(8,128)(2,1)S(1)}, u32[]{:S(2)}, u32[]{:S(2)}) collective-permute-start(bf16[256,128]{1,0:T(8,128)(2,1)S(1)} %partner.1), channel_id=1, source_target_pairs={{0,1},{1,0},{2,3},{3,2},{4,5},{5,4},{6,7},{7,6},{8,9},{9,8},{10,11... | collective-permute-start | bytes 196616 | tf_op jit(solution)/shard_map/ppermute | solution.py:36

commit v7 on v6

--- a/solution.py
+++ b/solution.py
@@ -117,7 +117,7 @@
 
 
 def dot_kernel(a_ref, b_ref, out_ref):
-    out_ref[...] = jnp.dot(a_ref[...], b_ref[...], preferred_element_type=jnp.float32)
+    out_ref[...] = jnp.dot(a_ref[...], b_ref[...], preferred_element_type=jnp.float32).astype(out_ref.dtype)
 
 
 def add_dot_kernel(base_ref, a_ref, b_ref, out_ref):
@@ -149,23 +149,14 @@
 def bounce_kernel(masks, me_ref, base_ref, factors_ref, hours_ref, out_ref):
     total = base_ref[...]
     patches = out_ref.shape[0]
-    for slot, owner in enumerate(owners(masks, me_ref[0])):
+    start = hours_ref.shape[0] // patches - len(masks[0])
+    for slot, owner in enumerate(owners(masks, me_ref[0]), start):
         total += jnp.dot(
             factors_ref[:, pl.ds(pl.multiple_of(owner * patches, patches), patches)],
             hours_ref[slot * patches : (slot + 1) * patches, :],
             preferred_element_type=jnp.float32,
         )
     out_ref[...] = total
-
-
-def head_kernel(factors_ref, hours_ref, out_ref):
-    count = hours_ref.shape[0]
-    out_ref[...] = jnp.dot(factors_ref[:, :count], hours_ref[...], preferred_element_type=jnp.float32)
-
-
-def tail_kernel(start, base_ref, factors_ref, hours_ref, out_ref):
-    part = jnp.dot(factors_ref[:, start:], hours_ref[start:, :], preferred_element_type=jnp.float32)
-    out_ref[...] = (base_ref[...] + part).astype(out_ref.dtype)
 
 
 def sum_kernel(a_ref, b_ref, out_ref):
@@ -243,29 +234,19 @@
     )
     theirs = swap(size, Piece(chosen, [[0], [0]]), 1).value
     flops = 2 * patches * size // 2 * patches * hours
-    head = []
-
-    def partner_head(parts):
-        head.append(join(*(parts[name] for name in order[:3])))
-        return call(head_kernel, "partner_head", flat, [WHOLE] * 2, 2 * 10**9, theirs, head[0].value)
-
-    same, total, partial = gather(size, own, copy, copy, order, total, ("second", partner_head))
-    start = head[0].value.shape[0]
-    partial = call(
-        functools.partial(tail_kernel, start), "partner", short, [WHOLE] * 3, flops, partial, theirs, same.value
-    )
+    done = []
+
+    def bounce(name, base, piece):
+        masks = [m[len(done) :] for m in piece.masks]
+        done.extend(masks[0])
+        args = (index, base, view_factors, piece.value)
+        return call(functools.partial(bounce_kernel, masks), name, flat, [SCALARS] + [WHOLE] * 3, 2 * 10**9, *args)
+
+    late = ("first", lambda parts: bounce("bounce_head", total, join(*(parts[name] for name in order[:2]))))
+    same, _, total = gather(size, own, copy, copy, order, total, late)
+    partial = call(dot_kernel, "partner", short, [WHOLE] * 2, flops, theirs, same.value)
     partial = swap(size, Piece(partial, [[0], [0]]), 1).value
-    total = call(
-        functools.partial(bounce_kernel, same.masks),
-        "bounce_same",
-        flat,
-        [SCALARS] + [WHOLE] * 3,
-        flops,
-        index,
-        total,
-        view_factors,
-        same.value,
-    )
+    total = bounce("bounce_same", total, same)
     return call(sum_kernel, "sum", short, [WHOLE] * 2, 0, total, partial)
 
 

time: 32.6 us -> 32.8 us (level)
  waiting for transfers between devices: 7.11 us -> 7.6 us
  starting transfers between devices: 17.2 us -> 16.8 us
    ppermute x15, waiting for transfers between devices: 7.11 us -> 7.6 us  [swap(): lax.ppermute(piece.value, 'col', pairs)]
    ppermute x15, starting transfers between devices: 17.2 us -> 16.8 us  [swap(): lax.ppermute(piece.value, 'col', pairs)]
where the time goes in v7:
time: 32.8 us; the launch traced here: 32.6 us
  starting transfers between devices  16.8 us (51%)
  Pallas kernels  7.77 us (24%)
  waiting for transfers between devices  7.6 us (23%)
    ppermute x15, starting transfers between devices, swap(): lax.ppermute(piece.value, 'col', pairs)  16.8 us
    pallas_call x12, Pallas kernels, call(): pl.pallas_call(kernel, scratch_shapes=scratch, out_shape=outs, in_specs=s...  7.77 us
    ppermute x15, waiting for transfers between devices, swap(): lax.ppermute(piece.value, 'col', pairs)  7.6 us
  transfers between devices with their start and end apart: 15, of which 6 were waited for; matrix products, arithmetic and copies ran while one was open for 1% of the time, Pallas kernels for 20%

profile of v7, /device:TPU:0, one launch (start us, length us, event | category | flops | bytes accessed | tf_op | source)
XLA Modules:
  0.0 32.6 jit_solution(3578446463030269401)
XLA Ops:
  0.0 3.5 %collective-permute-start = (bf16[144,128]{1,0:T(8,128)(2,1)}, bf16[144,128]{1,0:T(8,128)(2,1)S(1)}, u32[]{:S(2)}, u32[]{:S(2)}) collective-permute-start(bf16[144,128]{1,0:T(8,128)(2,1)} %sky_in.1), channel_id=1, source_target_pairs={{0,9},{1,8},{2,11},{3,10},{4,13},{5,12},{6,15},{7,14},{8,1},{9,0},... | collective-permute-start | bytes 110600 | tf_op jit(solution)/shard_map/ppermute | solution.py:36
  3.5 1.8 %collective-permute-start.1 = (bf16[144,128]{1,0:T(8,128)(2,1)}, bf16[144,128]{1,0:T(8,128)(2,1)S(1)}, u32[]{:S(2)}, u32[]{:S(2)}) collective-permute-start(bf16[144,128]{1,0:T(8,128)(2,1)} %sky_in.1), channel_id=1, source_target_pairs={{0,3},{1,4},{2,7},{3,0},{4,1},{5,6},{6,5},{7,2},{8,13},{9,10},{10,... | collective-permute-start | bytes 110600 | tf_op jit(solution)/shard_map/ppermute | solution.py:36
  5.3 1.4 %prepare.1 = (bf16[144,128]{1,0:T(8,128)(2,1)S(1)}, bf16[256,2304]{1,0:T(8,128)(2,1)S(1)}, f32[256,128]{1,0:T(8,128)S(1)}, s32[2,2304]{1,0:T(2,128)S(1)}) custom-call(f32[16]{0:T(128)} %albedo_in.1, s32[256]{0:T(256)} %material_in.1, s32[2304]{0:T(1024)} %order_in.1, bf16[144,128]{1,0:T(8,128)(2,1)} %sky_in.1, bf16[256,2304]{1,0:T(8,128)(2,1)} %direct_in.1, ...), custom_call_target="tpu_custom_call" | custom-call | flops 1000000000 | tf_op jit(solution)/shard_map/prepare/pallas_call | solution.py:65
  6.7 1.7 %permute_same.1 = (bf16[256,1152]{1,0:T(8,128)(2,1)S(1)}, bf16[256,1152]{1,0:T(8,128)(2,1)S(1)}) custom-call(s32[1]{0:T(128)} %bitcast.me_ref, s32[2,2304]{1,0:T(2,128)S(1)} %get-tuple-element.32.where_ref, f32[256,128]{1,0:T(8,128)S(1)} %get-tuple-element.25.reflectance_ref, bf16[256,2304]{1,0:T(8,128)(2,1)S(1)} %get-tuple-element.26.direct_ref), custom_call_target="tpu_custom_call" | custom-call | flops 1358954496 | tf_op jit(solution)/shard_map/permute_same/pallas_call | solution.py:65
  8.4 1.1 %collective-permute-start.5 = (bf16[288,128]{1,0:T(8,128)(2,1)S(1)}, bf16[288,128]{1,0:T(8,128)(2,1)S(1)}, u32[]{:S(2)}, u32[]{:S(2)}) collective-permute-start(bf16[288,128]{1,0:T(8,128)(2,1)S(1)} %constant_dynamic-update-slice_fusion), channel_id=1, source_target_pairs={{0,5},{1,2},{2,1},{3,6},{4,7},{5,0},{6,3},{7,4},{8,11},{9,12},{10,... | collective-permute-start | bytes 221192 | tf_op jit(solution)/shard_map/ppermute | solution.py:36
  9.5 0.7 %collective-permute-start.4 = (bf16[144,128]{1,0:T(8,128)(2,1)S(1)}, bf16[144,128]{1,0:T(8,128)(2,1)S(1)}, u32[]{:S(2)}, u32[]{:S(2)}) collective-permute-start(bf16[144,128]{1,0:T(8,128)(2,1)S(1)} %collective-permute-done), channel_id=1, source_target_pairs={{0,7},{1,6},{2,5},{3,4},{4,3},{5,2},{6,1},{7,0},{8,15},{9,14},{10,... | collective-permute-start | bytes 110600 | tf_op jit(solution)/shard_map/ppermute | solution.py:36
  10.2 1.5 %collective-permute-start.3 = (bf16[144,128]{1,0:T(8,128)(2,1)S(1)}, bf16[144,128]{1,0:T(8,128)(2,1)S(1)}, u32[]{:S(2)}, u32[]{:S(2)}) collective-permute-start(bf16[144,128]{1,0:T(8,128)(2,1)S(1)} %collective-permute-done), channel_id=1, source_target_pairs={{0,3},{1,4},{2,7},{3,0},{4,1},{5,6},{6,5},{7,2},{8,13},{9,10},{10,... | collective-permute-start | bytes 110600 | tf_op jit(solution)/shard_map/ppermute | solution.py:36
  11.7 1.3 %collective-permute-start.2 = (bf16[144,128]{1,0:T(8,128)(2,1)S(1)}, bf16[144,128]{1,0:T(8,128)(2,1)S(1)}, u32[]{:S(2)}, u32[]{:S(2)}) collective-permute-start(bf16[144,128]{1,0:T(8,128)(2,1)S(1)} %collective-permute-done), channel_id=1, source_target_pairs={{0,5},{1,2},{2,1},{3,6},{4,7},{5,0},{6,3},{7,4},{8,11},{9,12},{10,... | collective-permute-start | bytes 110600 | tf_op jit(solution)/shard_map/ppermute | solution.py:36
  13.0 1.7 %permute_across.1 = (bf16[256,1152]{1,0:T(8,128)(2,1)S(1)}, bf16[256,1152]{1,0:T(8,128)(2,1)S(1)}) custom-call(s32[1]{0:T(128)} %bitcast.me_ref, s32[2,2304]{1,0:T(2,128)S(1)} %get-tuple-element.32.where_ref, f32[256,128]{1,0:T(8,128)S(1)} %get-tuple-element.25.reflectance_ref, bf16[256,2304]{1,0:T(8,128)(2,1)S(1)} %get-tuple-element.26.direct_ref), custom_call_target="tpu_custom_call" | custom-call | flops 1358954496 | tf_op jit(solution)/shard_map/permute_across/pallas_call | solution.py:65
  15.8 1.1 %collective-permute-done.6.b_ref.sky_second_ref = bf16[1152,128]{1,0:T(8,128)(2,1)S(1)} collective-permute-done((bf16[1152,128]{1,0:T(8,128)(2,1)S(1)}, bf16[1152,128]{1,0:T(8,128)(2,1)S(1)}, u32[]{:S(2)}, u32[]{:S(2)}) %collective-permute-start.6) | collective-permute-done | bytes 294944 | tf_op jit(solution)/shard_map/ppermute | solution.py:36
  16.8 0.3 hours_all.1.in_ref
  17.2 0.7 %collective-permute-start.7 = (bf16[256,128]{1,0:T(8,128)(2,1)S(1)}, bf16[256,128]{1,0:T(8,128)(2,1)S(1)}, u32[]{:S(2)}, u32[]{:S(2)}) collective-permute-start(bf16[256,128]{1,0:T(8,128)(2,1)S(1)} %hours_all.1.in_ref), channel_id=1, source_target_pairs={{0,9},{1,8},{2,11},{3,10},{4,13},{5,12},{6,15},{7,14},{8,1},{9,0},... | collective-permute-start | bytes 196616 | tf_op jit(solution)/shard_map/ppermute | solution.py:36
  17.9 1.2 %collective-permute-start.9 = (bf16[256,128]{1,0:T(8,128)(2,1)S(1)}, bf16[256,128]{1,0:T(8,128)(2,1)S(1)}, u32[]{:S(2)}, u32[]{:S(2)}) collective-permute-start(bf16[256,128]{1,0:T(8,128)(2,1)S(1)} %copy.21), channel_id=1, source_target_pairs={{0,3},{1,4},{2,7},{3,0},{4,1},{5,6},{6,5},{7,2},{8,13},{9,10},{10,... | collective-permute-start | bytes 196616 | tf_op jit(solution)/shard_map/ppermute | solution.py:36
  19.5 0.5 %direct.1.base_ref = f32[256,128]{1,0:T(8,128)S(1)} custom-call(bf16[256,1152]{1,0:T(8,128)(2,1)S(1)} %get-tuple-element.37.first_ref, bf16[256,1152]{1,0:T(8,128)(2,1)S(1)} %get-tuple-element.38.second_ref, bf16[1152,128]{1,0:T(8,128)(2,1)S(1)} %constant_dynamic-update-slice_fusion.2.b_ref.sky_first_ref, ...), custom_call_target="tpu_custom_call" | custom-call | flops 2000000000 | tf_op jit(solution)/shard_map/direct/pallas_call | solution.py:65
  19.9 1.7 %collective-permute-done.9 = bf16[256,128]{1,0:T(8,128)(2,1)S(1)} collective-permute-done((bf16[256,128]{1,0:T(8,128)(2,1)S(1)}, bf16[256,128]{1,0:T(8,128)(2,1)S(1)}, u32[]{:S(2)}, u32[]{:S(2)}) %collective-permute-start.9) | collective-permute-done | bytes 65568 | tf_op jit(solution)/shard_map/ppermute | solution.py:36
  21.6 1.3 %collective-permute-start.10 = (bf16[512,128]{1,0:T(8,128)(2,1)S(1)}, bf16[512,128]{1,0:T(8,128)(2,1)S(1)}, u32[]{:S(2)}, u32[]{:S(2)}) collective-permute-start(bf16[512,128]{1,0:T(8,128)(2,1)S(1)} %pad_maximum_fusion.1), channel_id=1, source_target_pairs={{0,5},{1,2},{2,1},{3,6},{4,7},{5,0},{6,3},{7,4},{8,11},{9,12},{10,... | collective-permute-start | bytes 393224 | tf_op jit(solution)/shard_map/ppermute | solution.py:36
  23.0 0.6 %collective-permute-done.7 = bf16[256,128]{1,0:T(8,128)(2,1)S(1)} collective-permute-done((bf16[256,128]{1,0:T(8,128)(2,1)S(1)}, bf16[256,128]{1,0:T(8,128)(2,1)S(1)}, u32[]{:S(2)}, u32[]{:S(2)}) %collective-permute-start.7) | collective-permute-done | bytes 65568 | tf_op jit(solution)/shard_map/ppermute | solution.py:36
  23.5 0.9 %collective-permute-start.12 = (bf16[256,128]{1,0:T(8,128)(2,1)S(1)}, bf16[256,128]{1,0:T(8,128)(2,1)S(1)}, u32[]{:S(2)}, u32[]{:S(2)}) collective-permute-start(bf16[256,128]{1,0:T(8,128)(2,1)S(1)} %collective-permute-done.7), channel_id=1, source_target_pairs={{0,3},{1,4},{2,7},{3,0},{4,1},{5,6},{6,5},{7,2},{8,13},{9,10},{10,... | collective-permute-start | bytes 196616 | tf_op jit(solution)/shard_map/ppermute | solution.py:36
  24.4 0.6 %collective-permute-start.11 = (bf16[256,128]{1,0:T(8,128)(2,1)S(1)}, bf16[256,128]{1,0:T(8,128)(2,1)S(1)}, u32[]{:S(2)}, u32[]{:S(2)}) collective-permute-start(bf16[256,128]{1,0:T(8,128)(2,1)S(1)} %collective-permute-done.7), channel_id=1, source_target_pairs={{0,5},{1,2},{2,1},{3,6},{4,7},{5,0},{6,3},{7,4},{8,11},{9,12},{10,... | collective-permute-start | bytes 196616 | tf_op jit(solution)/shard_map/ppermute | solution.py:36
  25.0 1.6 %collective-permute-start.8 = (bf16[256,128]{1,0:T(8,128)(2,1)S(1)}, bf16[256,128]{1,0:T(8,128)(2,1)S(1)}, u32[]{:S(2)}, u32[]{:S(2)}) collective-permute-start(bf16[256,128]{1,0:T(8,128)(2,1)S(1)} %collective-permute-done.7), channel_id=1, source_target_pairs={{0,7},{1,6},{2,5},{3,4},{4,3},{5,2},{6,1},{7,0},{8,15},{9,14},{10,... | collective-permute-start | bytes 196616 | tf_op jit(solution)/shard_map/ppermute | solution.py:36
  26.9 3.2 %collective-permute-done.8 = bf16[256,128]{1,0:T(8,128)(2,1)S(1)} collective-permute-done((bf16[256,128]{1,0:T(8,128)(2,1)S(1)}, bf16[256,128]{1,0:T(8,128)(2,1)S(1)}, u32[]{:S(2)}, u32[]{:S(2)}) %collective-permute-start.8) | collective-permute-done | bytes 65568 | tf_op jit(solution)/shard_map/ppermute | solution.py:36
  30.2 0.4 %partner.1 = bf16[256,128]{1,0:T(8,128)(2,1)S(1)} custom-call(bf16[256,2048]{1,0:T(8,128)(2,1)S(1)} %collective-permute-done.13.a_ref, bf16[2048,128]{1,0:T(8,128)(2,1)S(1)} %constant_dynamic-update-slice_fusion.9.hours_ref.b_ref), custom_call_target="tpu_custom_call" | custom-call | flops 134217728 | tf_op jit(solution)/shard_map/partner/pallas_call | solution.py:65
  31.2 0.8 %collective-permute-done.14.b_ref = bf16[256,128]{1,0:T(8,128)(2,1)S(1)} collective-permute-done((bf16[256,128]{1,0:T(8,128)(2,1)S(1)}, bf16[256,128]{1,0:T(8,128)(2,1)S(1)}, u32[]{:S(2)}, u32[]{:S(2)}) %collective-permute-start.14) | collective-permute-done | bytes 65568 | tf_op jit(solution)/shard_map/ppermute | solution.py:36
  32.0 0.6 %sum.1 = bf16[256,128]{1,0:T(8,128)(2,1)} custom-call(f32[256,128]{1,0:T(8,128)S(1)} %bounce_same.1.a_ref, bf16[256,128]{1,0:T(8,128)(2,1)S(1)} %collective-permute-done.14.b_ref), custom_call_target="tpu_custom_call" | custom-call | tf_op jit(solution)/shard_map/sum/pallas_call | solution.py:65
  (38 shorter events, 2.2 us)
Async XLA Ops:
  0.0 9.5 %collective-permute-start = (bf16[144,128]{1,0:T(8,128)(2,1)}, bf16[144,128]{1,0:T(8,128)(2,1)S(1)}, u32[]{:S(2)}, u32[]{:S(2)}) collective-permute-start(bf16[144,128]{1,0:T(8,128)(2,1)} %sky_in.1), channel_id=1, source_target_pairs={{0,9},{1,8},{2,11},{3,10},{4,13},{5,12},{6,15},{7,14},{8,1},{9,0},... | collective-permute-start | bytes 110600 | tf_op jit(solution)/shard_map/ppermute | solution.py:36
  3.5 4.9 %collective-permute-start.1 = (bf16[144,128]{1,0:T(8,128)(2,1)}, bf16[144,128]{1,0:T(8,128)(2,1)S(1)}, u32[]{:S(2)}, u32[]{:S(2)}) collective-permute-start(bf16[144,128]{1,0:T(8,128)(2,1)} %sky_in.1), channel_id=1, source_target_pairs={{0,3},{1,4},{2,7},{3,0},{4,1},{5,6},{6,5},{7,2},{8,13},{9,10},{10,... | collective-permute-start | bytes 110600 | tf_op jit(solution)/shard_map/ppermute | solution.py:36
  8.4 6.7 %collective-permute-start.5 = (bf16[288,128]{1,0:T(8,128)(2,1)S(1)}, bf16[288,128]{1,0:T(8,128)(2,1)S(1)}, u32[]{:S(2)}, u32[]{:S(2)}) collective-permute-start(bf16[288,128]{1,0:T(8,128)(2,1)S(1)} %constant_dynamic-update-slice_fusion), channel_id=1, source_target_pairs={{0,5},{1,2},{2,1},{3,6},{4,7},{5,0},{6,3},{7,4},{8,11},{9,12},{10,... | collective-permute-start | bytes 221192 | tf_op jit(solution)/shard_map/ppermute | solution.py:36
  9.5 5.6 %collective-permute-start.4 = (bf16[144,128]{1,0:T(8,128)(2,1)S(1)}, bf16[144,128]{1,0:T(8,128)(2,1)S(1)}, u32[]{:S(2)}, u32[]{:S(2)}) collective-permute-start(bf16[144,128]{1,0:T(8,128)(2,1)S(1)} %collective-permute-done), channel_id=1, source_target_pairs={{0,7},{1,6},{2,5},{3,4},{4,3},{5,2},{6,1},{7,0},{8,15},{9,14},{10,... | collective-permute-start | bytes 110600 | tf_op jit(solution)/shard_map/ppermute | solution.py:36
  10.2 4.9 %collective-permute-start.3 = (bf16[144,128]{1,0:T(8,128)(2,1)S(1)}, bf16[144,128]{1,0:T(8,128)(2,1)S(1)}, u32[]{:S(2)}, u32[]{:S(2)}) collective-permute-start(bf16[144,128]{1,0:T(8,128)(2,1)S(1)} %collective-permute-done), channel_id=1, source_target_pairs={{0,3},{1,4},{2,7},{3,0},{4,1},{5,6},{6,5},{7,2},{8,13},{9,10},{10,... | collective-permute-start | bytes 110600 | tf_op jit(solution)/shard_map/ppermute | solution.py:36
  11.7 3.4 %collective-permute-start.2 = (bf16[144,128]{1,0:T(8,128)(2,1)S(1)}, bf16[144,128]{1,0:T(8,128)(2,1)S(1)}, u32[]{:S(2)}, u32[]{:S(2)}) collective-permute-start(bf16[144,128]{1,0:T(8,128)(2,1)S(1)} %collective-permute-done), channel_id=1, source_target_pairs={{0,5},{1,2},{2,1},{3,6},{4,7},{5,0},{6,3},{7,4},{8,11},{9,12},{10,... | collective-permute-start | bytes 110600 | tf_op jit(solution)/shard_map/ppermute | solution.py:36
  15.2 4.0 %copy-start = (bf16[256,4096]{1,0:T(8,128)(2,1)S(1)}, bf16[256,4096]{1,0:T(8,128)(2,1)}, u32[]{:S(2)}) copy-start(bf16[256,4096]{1,0:T(8,128)(2,1)} %factors_ref.4) | copy-start | bytes 6291460
  15.2 1.6 %collective-permute-start.6 = (bf16[1152,128]{1,0:T(8,128)(2,1)S(1)}, bf16[1152,128]{1,0:T(8,128)(2,1)S(1)}, u32[]{:S(2)}, u32[]{:S(2)}) collective-permute-start(bf16[1152,128]{1,0:T(8,128)(2,1)S(1)} %constant_dynamic-update-slice_fusion.2.b_ref.sky_first_ref), channel_id=1, source_target_pairs={{0,1},{1,0},{2,3},{3,2},{4,5},{5,4},{6,7},{7,6},{8,9},{9,8},{10,11... | collective-permute-start | bytes 884744 | tf_op jit(solution)/shard_map/ppermute | solution.py:36
  17.2 6.3 %collective-permute-start.7 = (bf16[256,128]{1,0:T(8,128)(2,1)S(1)}, bf16[256,128]{1,0:T(8,128)(2,1)S(1)}, u32[]{:S(2)}, u32[]{:S(2)}) collective-permute-start(bf16[256,128]{1,0:T(8,128)(2,1)S(1)} %hours_all.1.in_ref), channel_id=1, source_target_pairs={{0,9},{1,8},{2,11},{3,10},{4,13},{5,12},{6,15},{7,14},{8,1},{9,0},... | collective-permute-start | bytes 196616 | tf_op jit(solution)/shard_map/ppermute | solution.py:36
  17.9 3.7 %collective-permute-start.9 = (bf16[256,128]{1,0:T(8,128)(2,1)S(1)}, bf16[256,128]{1,0:T(8,128)(2,1)S(1)}, u32[]{:S(2)}, u32[]{:S(2)}) collective-permute-start(bf16[256,128]{1,0:T(8,128)(2,1)S(1)} %copy.21), channel_id=1, source_target_pairs={{0,3},{1,4},{2,7},{3,0},{4,1},{5,6},{6,5},{7,2},{8,13},{9,10},{10,... | collective-permute-start | bytes 196616 | tf_op jit(solution)/shard_map/ppermute | solution.py:36
  19.3 10.9 %collective-permute-start.13 = (bf16[256,2048]{1,0:T(8,128)(2,1)S(1)}, bf16[256,2048]{1,0:T(8,128)(2,1)S(1)}, u32[]{:S(2)}, u32[]{:S(2)}) collective-permute-start(bf16[256,2048]{1,0:T(8,128)(2,1)S(1)} %select.1), channel_id=1, source_target_pairs={{0,1},{1,0},{2,3},{3,2},{4,5},{5,4},{6,7},{7,6},{8,9},{9,8},{10,11... | collective-permute-start | bytes 3145736 | tf_op jit(solution)/shard_map/ppermute | solution.py:36
  21.6 5.0 %collective-permute-start.10 = (bf16[512,128]{1,0:T(8,128)(2,1)S(1)}, bf16[512,128]{1,0:T(8,128)(2,1)S(1)}, u32[]{:S(2)}, u32[]{:S(2)}) collective-permute-start(bf16[512,128]{1,0:T(8,128)(2,1)S(1)} %pad_maximum_fusion.1), channel_id=1, source_target_pairs={{0,5},{1,2},{2,1},{3,6},{4,7},{5,0},{6,3},{7,4},{8,11},{9,12},{10,... | collective-permute-start | bytes 393224 | tf_op jit(solution)/shard_map/ppermute | solution.py:36
  23.5 6.7 %collective-permute-start.12 = (bf16[256,128]{1,0:T(8,128)(2,1)S(1)}, bf16[256,128]{1,0:T(8,128)(2,1)S(1)}, u32[]{:S(2)}, u32[]{:S(2)}) collective-permute-start(bf16[256,128]{1,0:T(8,128)(2,1)S(1)} %collective-permute-done.7), channel_id=1, source_target_pairs={{0,3},{1,4},{2,7},{3,0},{4,1},{5,6},{6,5},{7,2},{8,13},{9,10},{10,... | collective-permute-start | bytes 196616 | tf_op jit(solution)/shard_map/ppermute | solution.py:36
  24.4 5.7 %collective-permute-start.11 = (bf16[256,128]{1,0:T(8,128)(2,1)S(1)}, bf16[256,128]{1,0:T(8,128)(2,1)S(1)}, u32[]{:S(2)}, u32[]{:S(2)}) collective-permute-start(bf16[256,128]{1,0:T(8,128)(2,1)S(1)} %collective-permute-done.7), channel_id=1, source_target_pairs={{0,5},{1,2},{2,1},{3,6},{4,7},{5,0},{6,3},{7,4},{8,11},{9,12},{10,... | collective-permute-start | bytes 196616 | tf_op jit(solution)/shard_map/ppermute | solution.py:36
  25.0 5.1 %collective-permute-start.8 = (bf16[256,128]{1,0:T(8,128)(2,1)S(1)}, bf16[256,128]{1,0:T(8,128)(2,1)S(1)}, u32[]{:S(2)}, u32[]{:S(2)}) collective-permute-start(bf16[256,128]{1,0:T(8,128)(2,1)S(1)} %collective-permute-done.7), channel_id=1, source_target_pairs={{0,7},{1,6},{2,5},{3,4},{4,3},{5,2},{6,1},{7,0},{8,15},{9,14},{10,... | collective-permute-start | bytes 196616 | tf_op jit(solution)/shard_map/ppermute | solution.py:36
  30.7 1.3 %collective-permute-start.14 = (bf16[256,128]{1,0:T(8,128)(2,1)S(1)}, bf16[256,128]{1,0:T(8,128)(2,1)S(1)}, u32[]{:S(2)}, u32[]{:S(2)}) collective-permute-start(bf16[256,128]{1,0:T(8,128)(2,1)S(1)} %partner.1), channel_id=1, source_target_pairs={{0,1},{1,0},{2,3},{3,2},{4,5},{5,4},{6,7},{7,6},{8,9},{9,8},{10,11... | collective-permute-start | bytes 196616 | tf_op jit(solution)/shard_map/ppermute | solution.py:36
